TPU v7x, 32 devices: a whole 2x2x4 slice. The times are simulated.
32 devices in a mesh: gz: 4 (over z), xy: 8 (over y, x, core).
Axes of the slice: x: 2, y: 2, z: 4, core: 2. Of those that a mesh axis runs over, the one named last changes fastest.
Arguments:
- positions: float32 [3, 4096], P(None, ('gz', 'xy')), may hold values from 0 to 16, as said below
- velocities: float32 [3, 4096], P(None, ('gz', 'xy')), may hold values from -6 to 6
- forces: float32 [3, 4096], P(None, ('gz', 'xy')), may hold values from -6 to 6
- species: int32 [4096], P(('gz', 'xy')), may hold values from 0 to 3
- counts: int32 [32], P(('gz', 'xy')), may hold values from 16 to 128, as said below
- neighbours: int32 [24, 4096], P(None, ('gz', 'xy')), may hold values from 0 to 320, as said below
- send_inplane: int32 [2, 1024], P(None, ('gz', 'xy')), may hold values from 0 to 127
- send_normal: int32 [2, 2048], P(None, ('gz', 'xy')), may hold values from 0 to 191
- embedding: float32 [4, 128], replicated, may hold values from -6 to 6
- inverse_mass: float32 [4], replicated, may hold values from 0.25 to 1
- radial_weight: float32 [16, 128], replicated, may hold values from -1.5 to 1.5
- mix_weight: float32 [128, 128], replicated, may hold values from -0.5 to 0.5
- self_weight: float32 [128, 128], replicated, may hold values from -0.5 to 0.5
- charge_weight: float32 [128, 128], replicated, may hold values from -0.5 to 0.5
- readout_weight: float32 [128, 128], replicated, may hold values from -0.5 to 0.5
- readout_vector: float32 [128], replicated, may hold values from -0.5 to 0.5
- kernel_filter: float32 [512, 128], replicated, may hold values from 0.2 to 2
Outputs:
- positions_new: float32 [3, 4096], P(None, ('gz', 'xy'))
- velocities_new: float32 [3, 4096], P(None, ('gz', 'xy'))
- forces_new: float32 [3, 4096], P(None, ('gz', 'xy'))
- energy: float32 [], replicated
Inputs may be any that keep to these rules, and one draw needn't show every extreme that they name: `positions`: coordinates of domain (g, p) lie in [2 p, 2 p + 2) x [0, 4) x [2 g, 2 g + 2). `counts`: the first domain is full; filling falls along the slab-normal axis. `neighbours`: slots of the extended list: own 128, then 32 from the lower and 32 from the upper in-plane neighbour, 64 from the lower and 64 from the upper slab-normal neighbour, then the padding slot 320.
All inputs are finite; a program needn't handle non-finite values.
Results may differ from a plain program's by a relative error of at most 0.0003.
Values sent between devices are 32-bit elements; how exact they have to be, the bound alone decides.
No kernel may reach another device: no remote copies, remote signals or barrier semaphores. Data moves between devices by JAX's collectives and lax.ppermute only.
A program may use at most 64 MiB of HBM per device.

v0:
```python
import jax
import jax.numpy as jnp
from jax import lax
from jax.sharding import PartitionSpec as P

KGRID = 8


time_step = 0.5
width_x = 2.0
width_y = 4.0
width_z = 2.0
far_away = 1000.0
softening = 0.25
basis_reach = 6.0
envelope_reach = 4.0
highest = lax.Precision.HIGHEST


def padded(cells, sides, width, closed):
    for axis, dim in sides:
        count = lax.axis_size(axis)
        ends = count if closed else count - 1
        head = lax.slice_in_dim(cells, 0, width, axis=dim)
        tail = lax.slice_in_dim(cells, cells.shape[dim] - width, cells.shape[dim], axis=dim)
        cells = jnp.concatenate(
            [
                lax.ppermute(tail, axis, [(i, (i + 1) % count) for i in range(ends)]),
                cells,
                lax.ppermute(head, axis, [((i + 1) % count, i) for i in range(ends)]),
            ],
            axis=dim,
        )
    return cells


def wave_vectors(grid_side, layers, strips):
    wave_index = jnp.arange(grid_side**3)
    along_x = (wave_index // (grid_side * grid_side)).astype(jnp.float32) / (strips * width_x)
    along_y = (wave_index // grid_side % grid_side - grid_side // 2).astype(jnp.float32) / width_y
    along_z = (wave_index % grid_side - grid_side // 2).astype(jnp.float32) / (layers * width_z)
    wave_rows = 2.0 * jnp.pi * jnp.stack([along_x, along_y, along_z], axis=1)
    keeper = (wave_index != grid_side // 2 * grid_side + grid_side // 2).astype(jnp.float32)
    return (wave_rows, keeper)


def local_terms(
    ext_pos,
    ext_kind,
    ext_live,
    neighbour_rows,
    embedding,
    radial_weight,
    mix_weight,
    self_weight,
    readout_weight,
    readout_vector,
    charge_weight,
):
    own_atoms = neighbour_rows.shape[1]
    kind_values = jnp.arange(embedding.shape[0]).astype(jnp.float32)
    one_hot = (ext_kind[:, None] == kind_values[None, :]).astype(jnp.float32)
    embedded = jnp.dot(one_hot, embedding, precision=highest)
    outgoing = jnp.dot(embedded, mix_weight, precision=highest) * ext_live[:, None]
    centre = ext_pos[:, :own_atoms]
    partner = jnp.take(ext_pos, neighbour_rows, axis=1)
    offsets = partner - centre[:, None, :]
    distance = jnp.sqrt(jnp.sum(offsets * offsets, axis=0) + softening)
    basis_count = radial_weight.shape[0]
    spacing = basis_reach / (basis_count - 1)
    centres = spacing * jnp.arange(basis_count).astype(jnp.float32)
    scaled = (distance[None, :, :] - centres[:, None, None]) / spacing
    envelope = 1.0 / (1.0 + (distance / envelope_reach) ** 4)
    radial_basis = jnp.exp(-scaled * scaled) * envelope[None, :, :]
    filters = jnp.einsum("bma,bc->mac", radial_basis, radial_weight, precision=highest)
    gathered = jnp.take(outgoing, neighbour_rows, axis=0)
    message = jnp.sum(filters * gathered, axis=0)
    hidden = jax.nn.silu(jnp.dot(embedded[:own_atoms], self_weight, precision=highest) + message)
    own_live = ext_live[:own_atoms]
    readout = jnp.dot(
        jax.nn.silu(jnp.dot(hidden, readout_weight, precision=highest)),
        readout_vector,
        precision=highest,
    )
    charges = jnp.dot(hidden, charge_weight, precision=highest) * own_live[:, None]
    return (jnp.sum(readout * own_live), charges)


def structure_terms(wave_rows, own_pos, charges):
    phase = jnp.dot(wave_rows, own_pos, precision=highest)
    cosine_sum = jnp.dot(jnp.cos(phase), charges, precision=highest)
    sine_sum = jnp.dot(jnp.sin(phase), charges, precision=highest)
    return (cosine_sum, sine_sum)


def ewald_pullback(wave_rows, pos_block, charge_block, weight_cos, weight_sin):
    phase = jnp.dot(wave_rows, pos_block, precision=highest)
    cosine = jnp.cos(phase)
    sine = jnp.sin(phase)
    charge_grad = jnp.einsum("ka,kc->ac", cosine, weight_cos, precision=highest) + jnp.einsum(
        "ka,kc->ac", sine, weight_sin, precision=highest
    )
    along_cos = jnp.einsum("kc,ac->ka", weight_cos, charge_block, precision=highest)
    along_sin = jnp.einsum("kc,ac->ka", weight_sin, charge_block, precision=highest)
    phase_grad = cosine * along_sin - sine * along_cos
    pos_grad = jnp.einsum("kd,ka->da", wave_rows, phase_grad, precision=highest)
    return (charge_grad, pos_grad)


def inplane_halo(outgoing):
    return padded(outgoing, (("xy", 0),), 1, True)


def normal_halo(outgoing):
    return padded(outgoing, (("gz", 0),), 1, False)


def local(
    positions,
    velocities,
    forces,
    species,
    counts,
    neighbours,
    send_inplane,
    send_normal,
    embedding,
    inverse_mass,
    radial_weight,
    mix_weight,
    self_weight,
    charge_weight,
    readout_weight,
    readout_vector,
    kernel_filter,
):
    own_atoms = positions.shape[1]
    strips = lax.axis_size("xy")
    layers = lax.axis_size("gz")
    all_atoms = own_atoms * strips * layers
    inplane_count = send_inplane.shape[1]
    normal_count = send_normal.shape[1]
    kind_values = jnp.arange(inverse_mass.shape[0])
    mass_factor = jnp.sum(
        (species[None, :] == kind_values[:, None]).astype(jnp.float32) * inverse_mass[:, None],
        axis=0,
    )
    half_velocity = velocities + 0.5 * time_step * forces * mass_factor[None, :]
    moved = positions + time_step * half_velocity
    filled = counts[0]
    own_live = (jnp.arange(own_atoms) < filled).astype(jnp.float32)
    records = jnp.concatenate(
        [moved, species.astype(jnp.float32)[None, :], own_live[None, :]], axis=0
    )
    outgoing = jnp.stack(
        [jnp.take(records, send_inplane[0], axis=1), jnp.take(records, send_inplane[1], axis=1)]
    )
    arrived = inplane_halo(outgoing)
    strip_index = lax.axis_index("xy")
    box_x = strips * width_x
    row_pick = (jnp.arange(5) == 0).astype(jnp.float32)[:, None]
    from_lower = arrived[0] - row_pick * jnp.where(strip_index == 0, box_x, 0.0)
    from_upper = arrived[3] + row_pick * jnp.where(strip_index == strips - 1, box_x, 0.0)
    first_section = jnp.concatenate([records, from_lower, from_upper], axis=1)
    outgoing = jnp.stack(
        [
            jnp.take(first_section, send_normal[0], axis=1),
            jnp.take(first_section, send_normal[1], axis=1),
        ]
    )
    arrived = normal_halo(outgoing)
    padding = jnp.array([far_away, far_away, far_away, 0.0, 0.0], dtype=jnp.float32)[:, None]
    extended = jnp.concatenate([first_section, arrived[0], arrived[3], padding], axis=1)
    ext_kind = extended[3]
    ext_live = extended[4]

    def local_part(ext_pos):
        return local_terms(
            ext_pos,
            ext_kind,
            ext_live,
            neighbours,
            embedding,
            radial_weight,
            mix_weight,
            self_weight,
            readout_weight,
            readout_vector,
            charge_weight,
        )

    (local_sum, charges), pullback = jax.vjp(local_part, extended[:3])
    wave_rows, keeper = wave_vectors(KGRID, layers, strips)
    cosine_sum, sine_sum = structure_terms(wave_rows, moved, charges)
    cosine_sum, sine_sum = lax.psum((cosine_sum, sine_sum), ("gz", "xy"))
    weight_cos = keeper[:, None] * kernel_filter * cosine_sum / all_atoms
    weight_sin = keeper[:, None] * kernel_filter * sine_sum / all_atoms
    ewald_energy = 0.5 * jnp.sum(weight_cos * cosine_sum + weight_sin * sine_sum)
    charge_grad, pos_grad = ewald_pullback(wave_rows, moved, charges, weight_cos, weight_sin)
    ext_grad = pullback((jnp.ones((), jnp.float32), charge_grad))[0]
    split_one = own_atoms + 2 * inplane_count
    returning = jnp.stack(
        [
            ext_grad[:, split_one : split_one + normal_count],
            ext_grad[:, split_one + normal_count : split_one + 2 * normal_count],
        ]
    )
    came_back = normal_halo(returning)
    section_grad = ext_grad[:, :split_one]
    section_grad = (
        section_grad.at[:, send_normal[0]].add(came_back[0]).at[:, send_normal[1]].add(came_back[3])
    )
    returning = jnp.stack(
        [
            section_grad[:, own_atoms : own_atoms + inplane_count],
            section_grad[:, own_atoms + inplane_count : split_one],
        ]
    )
    came_back = inplane_halo(returning)
    own_grad = (
        section_grad[:, :own_atoms]
        .at[:, send_inplane[0]]
        .add(came_back[0])
        .at[:, send_inplane[1]]
        .add(came_back[3])
    )
    forces_new = -(own_grad + pos_grad)
    velocities_new = half_velocity + 0.5 * time_step * forces_new * mass_factor[None, :]
    local_total = lax.psum(local_sum, ("gz", "xy"))
    energy = (local_total + ewald_energy) / all_atoms
    return (moved, velocities_new, forces_new, energy)


def solution(mesh):
    return jax.shard_map(
        local,
        mesh=mesh,
        in_specs=(
            P(None, ("gz", "xy")),
            P(None, ("gz", "xy")),
            P(None, ("gz", "xy")),
            P(("gz", "xy")),
            P(("gz", "xy")),
            P(None, ("gz", "xy")),
            P(None, ("gz", "xy")),
            P(None, ("gz", "xy")),
            P(),
            P(),
            P(),
            P(),
            P(),
            P(),
            P(),
            P(),
            P(),
        ),
        out_specs=(P(None, ("gz", "xy")), P(None, ("gz", "xy")), P(None, ("gz", "xy")), P()),
        check_vma=False,
    )
```

profile of v0, /device:TPU:0, one launch (start us, length us, event | category | flops | bytes accessed | tf_op | source)
XLA Modules:
  0.0 241.4 jit_solution(3382150313143937419)
XLA Ops:
  7.2 0.7 convert_bitcast_fusion
  7.9 0.8 select_reduce_fusion
  8.7 0.7 broadcast_multiply_fusion
  9.4 0.1 copy.77
  9.5 0.8 copy.76
  10.3 0.8 copy.78
  11.7 0.1 copy.79
  11.8 0.8 compare_and_fusion.3
  12.7 0.6 gather_fusion.3
  13.4 3.3 %collective-permute-start.1 = (f32[1,5,32]{1,2,0:T(8,128)S(1)}, f32[1,5,32]{1,2,0:T(8,128)S(1)}, u32[]{:S(2)}, u32[]{:S(2)}) collective-permute-start(f32[1,5,32]{1,2,0:T(8,128)S(1)} %select_bitcast_fusion.2), channel_id=1, source_target_pairs={{1,0},{2,1},{3,2},{4,3},{5,4},{6,5},{7,6},{0,7},{9,8},{10,9},{11,1... | collective-permute-start | bytes 1928 | tf_op jit(solution)/shard_map/ppermute | solution.py:30
  16.7 0.6 gather_fusion.2
  17.4 0.7 broadcast_clamp_fusion
  18.1 0.7 compare_and_fusion
  18.9 0.7 fusion.57
  19.6 0.8 compare_and_fusion.1
  20.3 0.8 fusion.73
  21.1 0.8 fusion.75
  21.9 1.7 fusion.89
  23.6 0.1 pad_maximum_fusion
  23.7 0.6 gather_fusion.5
  24.4 1.3 collective-permute-start.3
  25.7 0.6 gather_fusion.4
  26.4 4.5 %collective-permute-start.2 = (f32[1,5,64]{1,2,0:T(8,128)S(1)}, f32[1,5,64]{1,2,0:T(8,128)S(1)}, u32[]{:S(2)}, u32[]{:S(2)}) collective-permute-start(f32[1,5,64]{1,2,0:T(8,128)S(1)} %select_bitcast_fusion.1), channel_id=1, source_target_pairs={{0,8},{8,16},{16,24},{1,9},{9,17},{17,25},{2,10},{10,18},{18,26},{... | collective-permute-start | bytes 3848 | tf_op jit(solution)/shard_map/ppermute | solution.py:28
  31.3 1.3 collective-permute-done.2
  32.7 0.1 copy.85
  32.9 0.3 fusion.19
  33.2 0.4 convolution_multiply_fusion.2
  33.6 10.8 %gather_fusion.1 = f32[3072,128]{1,0:T(8,128)} fusion(f32[321,128]{1,0:T(8,128)S(1)} %convolution_multiply_fusion.2, s32[3072]{0:T(1024)S(1)} %broadcast_clamp_fusion), kind=kCustom, calls=%fused_computation.5 | custom fusion | bytes 3158016 | tf_op jit(solution)/shard_map/jvp(jit(_take))/gather | solution.py:76
  44.5 8.1 %gather_fusion = f32[3072,3]{1,0:T(8,128)S(1)} fusion(f32[3,321]{0,1:T(8,128)S(1)} %copy.85, s32[3072]{0:T(1024)S(1)} %broadcast_clamp_fusion), kind=kCustom, calls=%fused_computation.4 | custom fusion | bytes 86016 | tf_op jit(solution)/shard_map/jvp(jit(_take))/gather | solution.py:66
  52.6 1.1 multiply_reduce_fusion.1
  53.8 0.2 copy-done.4
  54.0 3.2 %multiply_reduce_fusion = f32[128,128]{1,0:T(8,128)S(1)} fusion(f32[24,128,128]{2,1,0:T(8,128)S(1)} %bitcast.134, pred[24,128]{1,0:T(8,128)(4,1)S(1)} %compare_and_fusion, f32[24,128]{1,0:T(8,128)S(1)} %get-tuple-element.49, f32[16]{0:T(128)S(1)} %convert_multiply_fusion, f32[24,128]{1,0:T(8,128)S(1)} %get-tuple-element.48, f32[16,128]{1,0:T(8,128)S(1)} %copy-done.11), kind=kOutput, calls=%fused_computation.15 | convolution fusion | flops 76906496 | bytes 1674304 | tf_op jit(solution)/shard_map/jvp(bma,bc->mac)/dot_general | solution.py:75
  57.3 0.2 convolution_add_fusion.1
  57.5 0.2 convolution_multiply_fusion.3
  57.7 1.1 fusion.93
  58.8 1.1 fusion.92
  59.9 0.2 fusion.54
  60.1 0.8 fusion.12
  61.0 0.7 copy.92
  61.6 40.4 %psum.23 = f32[]{:T(128)} all-reduce(f32[]{:T(128)} %fusion.12), channel_id=1, replica_groups=mesh['gz'=4,'xy'=8] {'gz','xy'}, use_global_device_ids=true, to_apply=%region_14.17 | all-reduce | flops 1 | bytes 8 | tf_op jit(solution)/shard_map/psum | solution.py:229
  102.0 87.0 %all-reduce.4.cloned.1.call-done = (f32[512,128]{1,0:T(8,128)}, f32[512,128]{1,0:T(8,128)}) async-done(((f32[512,128]{1,0:T(8,128)}, f32[512,128]{1,0:T(8,128)}), (f32[512,128]{1,0:T(8,128)}, f32[512,128]{1,0:T(8,128)})) %all-reduce.4.cloned.1.call-update) | async-done | bytes 524304 | tf_op jit(solution)/shard_map/psum | solution.py:195
  189.1 1.4 convolution_multiply_fusion.1
  190.5 1.6 fusion.87
  192.2 0.4 fusion.3
  192.6 0.2 fusion.60
  192.9 0.7 fusion.7
  193.6 0.3 fusion.94
  193.8 0.3 fusion.32
  194.2 1.9 multiply_reduce_fusion.2
  196.1 2.4 %fusion.88 = (f32[3,128]{0,1:T(8,128)S(1)}, f32[3,24,128]{0,2,1:T(8,128)}) fusion(f32[24,128]{1,0:T(8,128)S(1)} %fusion.52, f32[3,128]{0,1:T(8,128)S(1)} %get-tuple-element.38, f32[24,128,3]{2,1,0:T(8,128)S(1)} %bitcast.132, pred[24,128]{1,0:T(8,128)(4,1)S(1)} %compare_and_fusion), kind=kLoop, calls=%fused_computation.175 | loop fusion | flops 45696 | bytes 92160 | tf_op jit(solution)/shard_map/transpose(jvp())/reduce_sum | solution.py:67
  198.6 17.6 %scatter_fusion = f32[3,321]{0,1:T(8,128)S(1)} fusion(f32[3,321]{0,1:T(8,128)S(1)} %pad.3, s32[3072]{0:T(1024)S(1)} %fusion.57, f32[3072,3]{1,0:T(8,128)} %bitcast.133), kind=kCustom, calls=%fused_computation.6 | custom fusion | flops 9216 | bytes 122880 | tf_op jit(solution)/shard_map/transpose(jvp(jit(_take)))/scatter-add | solution.py:66
  216.2 3.3 %collective-permute-start.4 = (f32[1,3,64]{1,2,0:T(8,128)S(1)}, f32[1,3,64]{1,2,0:T(8,128)S(1)}, u32[]{:S(2)}, u32[]{:S(2)}) collective-permute-start(f32[1,3,64]{1,2,0:T(8,128)S(1)} %get-tuple-element.43), channel_id=1, source_target_pairs={{0,8},{8,16},{16,24},{1,9},{9,17},{17,25},{2,10},{10,18},{18,26},{... | collective-permute-start | bytes 2312 | tf_op jit(solution)/shard_map/ppermute | solution.py:28
  219.4 1.3 collective-permute-start.5
  220.7 0.7 add_reduce_fusion
  222.8 1.0 scatter_custom_fusion.1
  223.8 1.5 collective-permute-done.5
  225.2 1.0 scatter_custom_fusion.2
  226.4 2.6 %collective-permute-start.7 = (f32[1,3,32]{2,1,0:T(4,128)S(1)}, f32[1,3,32]{2,1,0:T(4,128)S(1)}, u32[]{:S(2)}, u32[]{:S(2)}) collective-permute-start(f32[1,3,32]{2,1,0:T(4,128)S(1)} %bitcast.140), channel_id=1, source_target_pairs={{1,0},{2,1},{3,2},{4,3},{5,4},{6,5},{7,6},{0,7},{9,8},{10,9},{11,1... | collective-permute-start | bytes 1160 | tf_op jit(solution)/shard_map/ppermute | solution.py:30
  229.1 0.1 copy.88
  229.2 1.0 collective-permute-done.6
  230.4 0.8 scatter_fusion.1
  231.2 0.8 scatter_fusion.2
  232.1 0.7 copy.93
  232.8 0.7 copy.94
  (79 shorter events, 1.7 us)
Async XLA Ops:
  7.2 26.0 %copy-start = (f32[128,128]{1,0:T(8,128)S(1)}, f32[128,128]{1,0:T(8,128)}, u32[]{:S(2)}) copy-start(f32[128,128]{1,0:T(8,128)} %param.33) | copy-start | bytes 196612
  7.2 25.4 %copy-start.8 = (f32[5,1]{1,0:T(8,128)S(1)}, f32[5,1]{1,0:T(8,128)}, u32[]{:S(2)}) copy-start(f32[5,1]{1,0:T(8,128)} %constant.169) | copy-start | bytes 64
  7.2 25.7 %copy-start.9 = (f32[4,128]{1,0:T(4,128)S(1)}, f32[4,128]{1,0:T(4,128)}, u32[]{:S(2)}) copy-start(f32[4,128]{1,0:T(4,128)} %param.30) | copy-start | bytes 6148
  7.2 181.9 %all-reduce.4.cloned.1.call-start = ((), (), s32[]{:S(2)}) async-start(), calls=%async_computation | async-start | bytes 1048576 | tf_op jit(solution)/shard_map/psum | solution.py:195
  13.4 10.2 %collective-permute-start.1 = (f32[1,5,32]{1,2,0:T(8,128)S(1)}, f32[1,5,32]{1,2,0:T(8,128)S(1)}, u32[]{:S(2)}, u32[]{:S(2)}) collective-permute-start(f32[1,5,32]{1,2,0:T(8,128)S(1)} %select_bitcast_fusion.2), channel_id=1, source_target_pairs={{1,0},{2,1},{3,2},{4,3},{5,4},{6,5},{7,6},{0,7},{9,8},{10,9},{11,1... | collective-permute-start | bytes 1928 | tf_op jit(solution)/shard_map/ppermute | solution.py:30
  17.4 6.2 %collective-permute-start = (f32[1,5,32]{1,2,0:T(8,128)S(1)}, f32[1,5,32]{1,2,0:T(8,128)S(1)}, u32[]{:S(2)}, u32[]{:S(2)}) collective-permute-start(f32[1,5,32]{1,2,0:T(8,128)S(1)} %select_bitcast_fusion.3), channel_id=1, source_target_pairs={{0,1},{1,2},{2,3},{3,4},{4,5},{5,6},{6,7},{7,0},{8,9},{9,10},{10,1... | collective-permute-start | bytes 1928 | tf_op jit(solution)/shard_map/ppermute | solution.py:28
  24.4 6.7 %collective-permute-start.3 = (f32[1,5,64]{1,2,0:T(8,128)S(1)}, f32[1,5,64]{1,2,0:T(8,128)S(1)}, u32[]{:S(2)}, u32[]{:S(2)}) collective-permute-start(f32[1,5,64]{1,2,0:T(8,128)S(1)} %select_bitcast_fusion), channel_id=1, source_target_pairs={{8,0},{16,8},{24,16},{9,1},{17,9},{25,17},{10,2},{18,10},{26,18},{... | collective-permute-start | bytes 3848 | tf_op jit(solution)/shard_map/ppermute | solution.py:30
  26.4 6.1 %collective-permute-start.2 = (f32[1,5,64]{1,2,0:T(8,128)S(1)}, f32[1,5,64]{1,2,0:T(8,128)S(1)}, u32[]{:S(2)}, u32[]{:S(2)}) collective-permute-start(f32[1,5,64]{1,2,0:T(8,128)S(1)} %select_bitcast_fusion.1), channel_id=1, source_target_pairs={{0,8},{8,16},{16,24},{1,9},{9,17},{17,25},{2,10},{10,18},{18,26},{... | collective-permute-start | bytes 3848 | tf_op jit(solution)/shard_map/ppermute | solution.py:28
  44.5 9.3 %copy-start.11 = (f32[16,128]{1,0:T(8,128)S(1)}, f32[16,128]{1,0:T(8,128)}, u32[]{:S(2)}) copy-start(f32[16,128]{1,0:T(8,128)} %param.32) | copy-start | bytes 24580
  52.6 1.4 copy-start.4
  52.6 4.6 %copy-start.7 = (f32[128,128]{1,0:T(8,128)S(1)}, f32[128,128]{1,0:T(8,128)}, u32[]{:S(2)}) copy-start(f32[128,128]{1,0:T(8,128)} %param.34) | copy-start | bytes 196612
  52.6 4.9 %copy-start.6 = (f32[128,128]{1,0:T(8,128)S(1)}, f32[128,128]{1,0:T(8,128)}, u32[]{:S(2)}) copy-start(f32[128,128]{1,0:T(8,128)} %param.35) | copy-start | bytes 196612
  57.2 2.7 %copy-start.10 = (f32[128,128]{1,0:T(8,128)S(1)}, f32[128,128]{1,0:T(8,128)}, u32[]{:S(2)}) copy-start(f32[128,128]{1,0:T(8,128)} %param.36) | copy-start | bytes 196612
  57.2 2.9 %copy-start.12 = (f32[128]{0:T(128)S(1)}, f32[128]{0:T(128)}, u32[]{:S(2)}) copy-start(f32[128]{0:T(128)} %param.37) | copy-start | bytes 1540
  57.3 131.8 %copy-start.1 = (f32[512,128]{1,0:T(8,128)S(1)}, f32[512,128]{1,0:T(8,128)}, u32[]{:S(2)}) copy-start(f32[512,128]{1,0:T(8,128)} %param.38) | copy-start | bytes 786436
  189.1 3.1 %copy-start.3 = (f32[512,128]{1,0:T(8,128)S(1)}, f32[512,128]{1,0:T(8,128)}, u32[]{:S(2)}) copy-start(f32[512,128]{1,0:T(8,128)} %get-tuple-element.26) | copy-start | bytes 786436
  189.1 3.8 %copy-start.2 = (f32[512,128]{1,0:T(8,128)S(1)}, f32[512,128]{1,0:T(8,128)}, u32[]{:S(2)}) copy-start(f32[512,128]{1,0:T(8,128)} %get-tuple-element.27) | copy-start | bytes 786436
  192.2 2.0 copy-start.5
  216.2 6.6 %collective-permute-start.4 = (f32[1,3,64]{1,2,0:T(8,128)S(1)}, f32[1,3,64]{1,2,0:T(8,128)S(1)}, u32[]{:S(2)}, u32[]{:S(2)}) collective-permute-start(f32[1,3,64]{1,2,0:T(8,128)S(1)} %get-tuple-element.43), channel_id=1, source_target_pairs={{0,8},{8,16},{16,24},{1,9},{9,17},{17,25},{2,10},{10,18},{18,26},{... | collective-permute-start | bytes 2312 | tf_op jit(solution)/shard_map/ppermute | solution.py:28
  219.4 5.8 %collective-permute-start.5 = (f32[1,3,64]{1,2,0:T(8,128)S(1)}, f32[1,3,64]{1,2,0:T(8,128)S(1)}, u32[]{:S(2)}, u32[]{:S(2)}) collective-permute-start(f32[1,3,64]{1,2,0:T(8,128)S(1)} %get-tuple-element.42), channel_id=1, source_target_pairs={{8,0},{16,8},{24,16},{9,1},{17,9},{25,17},{10,2},{18,10},{26,18},{... | collective-permute-start | bytes 2312 | tf_op jit(solution)/shard_map/ppermute | solution.py:30
  226.3 3.9 %collective-permute-start.6 = (f32[1,3,32]{2,1,0:T(4,128)S(1)}, f32[1,3,32]{2,1,0:T(4,128)S(1)}, u32[]{:S(2)}, u32[]{:S(2)}) collective-permute-start(f32[1,3,32]{2,1,0:T(4,128)S(1)} %bitcast.138), channel_id=1, source_target_pairs={{0,1},{1,2},{2,3},{3,4},{4,5},{5,6},{6,7},{7,0},{8,9},{9,10},{10,1... | collective-permute-start | bytes 1160 | tf_op jit(solution)/shard_map/ppermute | solution.py:28
  226.4 4.0 %collective-permute-start.7 = (f32[1,3,32]{2,1,0:T(4,128)S(1)}, f32[1,3,32]{2,1,0:T(4,128)S(1)}, u32[]{:S(2)}, u32[]{:S(2)}) collective-permute-start(f32[1,3,32]{2,1,0:T(4,128)S(1)} %bitcast.140), channel_id=1, source_target_pairs={{1,0},{2,1},{3,2},{4,3},{5,4},{6,5},{7,6},{0,7},{9,8},{10,9},{11,1... | collective-permute-start | bytes 1160 | tf_op jit(solution)/shard_map/ppermute | solution.py:30
Sparse Core Ops, SparseCore 0:
  60.0 129.0 all-reduce.3
where the time goes:
time: 243 us; the launch traced here: 241 us
  waiting for transfers between devices  90.8 us (37%)
  blocking collectives  40.4 us (17%)
  other arithmetic  33.4 us (14%)
  local copies, waits for them, and re-layouts  26.5 us (11%)
  between operations  17.7 us (7%)
  starting transfers between devices  16.4 us (7%)
  matrix products  16.2 us (7%)
    psum x1, waiting for transfers between devices, local(): cosine_sum, sine_sum = lax.psum((cosine_sum, sine_sum), ('gz', 'xy'))  87 us
    psum x1, blocking collectives, local(): local_total = lax.psum(local_sum, ('gz', 'xy'))  40.4 us
    scatter-add x1, other arithmetic, local_terms(): partner = jnp.take(ext_pos, neighbour_rows, axis=1)  17.6 us
    gather x1, local copies, waits for them, and re-layouts, local_terms(): gathered = jnp.take(outgoing, neighbour_rows, axis=0)  10.8 us
    ppermute x4, starting transfers between devices, padded(): lax.ppermute(head, axis, [((i + 1) % count, i) for i in range(ends)])  8.56 us
    gather x1, local copies, waits for them, and re-layouts, local_terms(): partner = jnp.take(ext_pos, neighbour_rows, axis=1)  8.11 us
    ppermute x4, starting transfers between devices, padded(): lax.ppermute(tail, axis, [(i, (i + 1) % count) for i in range(ends)])  7.8 us
    dot_general x2, matrix products, local_terms(): jnp.einsum('bma,bc->mac', radial_basis, radial_weight, precision=highest)  5.14 us
  transfers between devices with their start and end apart: 9, of which 4 were waited for; matrix products, arithmetic and copies ran while one was open for 5% of the time, Pallas kernels for 0%

commit v1 on v0

v1 whole, which is shorter than its diff:
```python
import functools
import math

import jax
import jax.numpy as jnp
from jax import lax
from jax.experimental import pallas as pl
from jax.experimental.pallas import tpu as pltpu
from jax.sharding import PartitionSpec as P

KGRID = 8

time_step = 0.5
width_x = 2.0
width_y = 4.0
width_z = 2.0
far_away = 1000.0
softening = 0.25
basis_reach = 6.0
envelope_reach = 4.0
highest = lax.Precision.HIGHEST
f32 = jnp.float32
bf16 = jnp.bfloat16
i32 = jnp.int32

ROW_KIND = 3
ROW_ID = 4
ROW_INPLANE = 5
ROW_ABOVE = 6
ROW_BELOW = 7
ROW_LISTS = 8
PAIR_BLOCKS = 6


def split(x):
    high = x.astype(bf16)
    return high, (x - high.astype(f32)).astype(bf16)


def mm(a, b):
    return jnp.dot(a, b, preferred_element_type=f32)


def mm_nt(a, b):
    return lax.dot_general(a, b, (((1,), (1,)), ((), ())), preferred_element_type=f32)


def left3(x):
    high, low = split(x)
    return jnp.concatenate([high, high, low], axis=1)


def right3(x):
    high, low = split(x)
    return jnp.concatenate([high, low, high], axis=0)


def lanes(shape):
    return lax.broadcasted_iota(i32, shape, len(shape) - 1)


def rows(shape):
    return lax.broadcasted_iota(i32, shape, len(shape) - 2)


def pick(table, index):
    return jnp.take_along_axis(table, index, axis=1)


def sigmoid(x):
    return 1.0 / (1.0 + jnp.exp(-x))


def cos_sin(turns):
    half = math.pi * (turns - jnp.floor(turns + 0.5))
    sq = half * half
    sine = half * (
        1.0
        + sq
        * (
            -1.0 / 6
            + sq * (1.0 / 120 + sq * (-1.0 / 5040 + sq * (1.0 / 362880 - sq / 39916800.0)))
        )
    )
    cosine = 1.0 + sq * (
        -0.5
        + sq
        * (
            1.0 / 24
            + sq
            * (-1.0 / 720 + sq * (1.0 / 40320 + sq * (-1.0 / 3628800 + sq / 479001600.0)))
        )
    )
    return 1.0 - 2.0 * sine * sine, 2.0 * sine * cosine


def phase_tables(record, layers, strips):
    shape = (KGRID, record.shape[1])
    number = rows(shape).astype(f32)
    centred = number - float(KGRID // 2)
    cos_x, sin_x = cos_sin(number * record[0:1] / (strips * width_x))
    cos_y, sin_y = cos_sin(centred * record[1:2] / width_y)
    cos_z, sin_z = cos_sin(centred * record[2:3] / (layers * width_z))
    cos_yz, sin_yz = [], []
    for k in range(KGRID):
        c, s = cos_y[k : k + 1], sin_y[k : k + 1]
        cos_yz.append(c * cos_z - s * sin_z)
        sin_yz.append(s * cos_z + c * sin_z)
    return cos_x, sin_x, jnp.concatenate(cos_yz, axis=0), jnp.concatenate(sin_yz, axis=0)


def store_phases(record, layers, strips, high_ref, low_ref, column, keep=None):
    cos_x, sin_x, cos_yz, sin_yz = phase_tables(record, layers, strips)
    side = KGRID * KGRID
    half = KGRID * side
    at = pl.ds(column, record.shape[1])
    for k in range(KGRID):
        c, s = cos_x[k : k + 1], sin_x[k : k + 1]
        cosine = c * cos_yz - s * sin_yz
        sine = s * cos_yz + c * sin_yz
        if keep is not None:
            keep[k * side : (k + 1) * side, :] = cosine
            keep[half + k * side : half + (k + 1) * side, :] = sine
        for value, start in ((cosine, k * side), (sine, half + k * side)):
            high, low = split(value)
            high_ref[start : start + side, at] = high
            low_ref[start : start + side, at] = low


def domain_of(index, here, sizes):
    layer, strip, step = here
    layers, strips = sizes
    g = lax.rem(layer - 1 + lax.rem(index, layers) + layers, layers)
    p = lax.rem(strip + step * (index // layers) + strips, strips)
    return g, p


def slot_of(g, p, here, sizes):
    layer, strip, step = here
    layers, strips = sizes
    x = p ^ strip
    return (g ^ layer) + layers * ((x >> 1) + (strips // 2) * (x & 1))


def position_here(strips):
    layer = lax.axis_index("gz").astype(i32)
    strip = lax.axis_index("xy").astype(i32)
    return layer, strip, 2 * (strip & 1) - 1


def pack_kernel(sizes, pos, vel, frc, spec, cnt, nbr, inplane, normal, mass, out):
    layers, strips = sizes
    own = pos.shape[1]
    layer, strip, _ = position_here(strips)
    kind = spec[...]
    factor = jnp.zeros(kind.shape, f32)
    for s in range(mass.shape[0]):
        factor = factor + jnp.where(kind == s, mass[s], 0.0)
    half_velocity = vel[...] + 0.5 * time_step * frc[...] * factor
    moved = pos[...] + time_step * half_velocity
    lane = lanes((1, own))
    code = jnp.where(lane < cnt[0], kind, -1).astype(f32)
    number = ((layer * strips + strip) * own + lane).astype(f32)
    out[0:3, :] = moved
    out[ROW_KIND : ROW_KIND + 1, :] = code
    out[ROW_ID : ROW_ID + 1, :] = number
    lists = inplane[...].astype(f32)
    width = lists.shape[1]
    out[ROW_INPLANE : ROW_BELOW + 1, :] = jnp.zeros((3, own), f32)
    out[ROW_INPLANE : ROW_INPLANE + 1, 0:width] = lists[1:2]
    out[ROW_INPLANE : ROW_INPLANE + 1, width : 2 * width] = lists[0:1]
    lists = normal[...].astype(f32)
    tall = lists.shape[1]
    out[ROW_ABOVE : ROW_ABOVE + 1, 2 * width : 2 * width + tall] = lists[1:2]
    out[ROW_BELOW : ROW_BELOW + 1, 0:tall] = lists[0:1]
    out[ROW_LISTS:, :] = nbr[...].astype(f32)


def pair_basis(u, b):
    t = u - b
    return t, jnp.exp(-(t * t))


def forward_kernel(
    sizes,
    dims,
    chunk,
    data,
    embedding,
    radial,
    mix,
    self_w,
    charge_w,
    readout_w,
    readout_v,
    s_out,
    pair_out,
    slope_out,
    readout_out,
    charge_out,
    first,
    high_ref,
    low_ref,
    q_ref,
    u_ref,
    w_ref,
    rex3,
    wcu3,
    rv_ref,
    energy_ref,
    near_layers,
):
    layers, strips = sizes
    own, width, tall, slots = dims
    here = position_here(strips)
    kinds = embedding.shape[0]
    basis = radial.shape[0]
    channels = embedding.shape[1]
    total = layers * (strips // 2)
    lane8 = lanes((8, own))
    row8 = rows((8, own))

    emb = embedding[...]
    mixed = jnp.dot(emb, mix[...], precision=highest, preferred_element_type=f32)
    selfed = jnp.dot(emb, self_w[...], precision=highest, preferred_element_type=f32)
    table = [mixed[s : s + 1] * radial[...] for s in range(kinds)]
    tail = -(-kinds // 16) * 16
    table.append(selfed)
    table.append(jnp.zeros((channels - kinds * basis - kinds, channels), f32))
    wide = jnp.concatenate(table, axis=0).T[:, : kinds * basis + tail]
    rex3[...] = left3(wide)
    wcu3[...] = left3(jnp.concatenate([charge_w[...].T, readout_w[...].T], axis=0))
    rv_ref[...] = jnp.broadcast_to(readout_v[...], (channels, channels)).T
    energy_ref[...] = jnp.zeros_like(energy_ref)

    def get(g, p):
        return data[slot_of(g, p, here, sizes), 0:8, :]

    box = strips * width_x

    def first_step(i, carry):
        g, p = domain_of(i, here, sizes)
        lower = get(g, lax.rem(p + strips - 1, strips))
        upper = get(g, lax.rem(p + 1, strips))
        at = jnp.broadcast_to(lower[ROW_INPLANE : ROW_INPLANE + 1], (8, own)).astype(i32)
        from_lower = pick(lower, at)
        at = jnp.broadcast_to(upper[ROW_INPLANE : ROW_INPLANE + 1], (8, own)).astype(i32)
        from_upper = pick(upper, at)
        down = jnp.where(p == 0, -box, 0.0)
        up = jnp.where(p == strips - 1, box, 0.0)
        shift = jnp.where(row8 == 0, jnp.where(lane8 < width, down, up), 0.0)
        first[i] = jnp.where(lane8 < width, from_lower, from_upper) + shift
        return carry

    lax.fori_loop(0, total, first_step, 0)

    bound = jnp.where((row8 == ROW_KIND) | (row8 == ROW_ID), -1.0, 0.0)
    padding = jnp.where(row8 < 3, far_away, -1.0)
    spacing = basis_reach / (basis - 1)

    def normal_ghosts(i, g, p, move, row):
        other = lax.rem(g + move + layers, layers)
        strip_start = (i // layers) * layers
        j = strip_start + lax.rem(i - strip_start + move + layers, layers)
        near = get(other, p)
        at = jnp.broadcast_to(near[row : row + 1], (8, own)).astype(i32)
        inside = at < own
        at = at & (own - 1)
        found = jnp.where(inside, pick(near, at), pick(first[j], at))
        beyond = (g + move < 0) | (g + move >= layers)
        return jnp.where(beyond, bound, found)

    def domain_step(i, place):
        g, p = domain_of(i, here, sizes)
        slot = slot_of(g, p, here, sizes)
        record = data[slot, 0:8, :]
        below = normal_ghosts(i, g, p, -1, ROW_ABOVE)
        above = normal_ghosts(i, g, p, 1, ROW_BELOW)
        parts = (
            record,
            jnp.where(lane8 < 2 * width, first[i], below),
            jnp.where(lane8 < tall, above, padding),
        )
        index = data[slot, ROW_LISTS : ROW_LISTS + slots, :].astype(i32)
        part = index // own
        at = index & (own - 1)

        def gathered(r):
            a, b, c = [pick(jnp.broadcast_to(q[r : r + 1], (slots, own)), at) for q in parts]
            return jnp.where(part == 0, a, jnp.where(part == 1, b, c))

        dx = gathered(0) - record[0:1]
        dy = gathered(1) - record[1:2]
        dz = gathered(2) - record[2:3]
        code = gathered(ROW_KIND)
        d = jnp.sqrt(dx * dx + dy * dy + dz * dz + softening)
        quarter = d * (1.0 / envelope_reach)
        square = quarter * quarter
        envelope = 1.0 / (1.0 + square * square)
        u_ref[...] = d * (1.0 / spacing)
        for s in range(kinds):
            w_ref[s] = jnp.where(code == float(s), envelope, 0.0)
        centre = rows((basis, own)).astype(f32)
        sums = [jnp.zeros((basis, own), f32) for s in range(kinds)]
        for m in range(slots):
            t, e = pair_basis(u_ref[m : m + 1, :], centre)
            for s in range(kinds):
                sums[s] = sums[s] + e * w_ref[s, m : m + 1, :]
        kind_row = record[ROW_KIND : ROW_KIND + 1]
        one_hot = jnp.where(rows((tail, own)).astype(f32) == kind_row, 1.0, 0.0)
        pre = mm(rex3[...], right3(jnp.concatenate(sums + [one_hot], axis=0)))
        gate = sigmoid(pre)
        hidden = pre * gate
        both = mm(wcu3[...], right3(hidden))
        live = kind_row >= 0.0
        charges = jnp.where(live, both[:channels], 0.0)
        readout = both[channels:]
        readout_gate = sigmoid(readout)
        scaled = jnp.where(live, rv_ref[...] * readout_gate, 0.0)
        local = scaled * readout
        energy_ref[...] += jnp.sum(local.reshape(channels // 8, 8, own), axis=0)
        column = pl.multiple_of(place * own, own)
        high, low = split(charges)
        q_ref[0:channels, pl.ds(column, own)] = high
        q_ref[channels : 2 * channels, pl.ds(column, own)] = low
        store_phases(record, layers, strips, high_ref, low_ref, column)

        strip_step = i // layers
        layer_step = lax.rem(i, layers)

        @pl.when((strip_step < 2) & (layer_step < near_layers))
        def _():
            j = strip_step * near_layers + layer_step
            pair_out[j, 0] = dx
            pair_out[j, 1] = dy
            pair_out[j, 2] = dz
            pair_out[j, 3] = code
            pair_out[j, 4] = gathered(ROW_ID)
            pair_out[j, 5] = d
            slope_out[j] = gate * (1.0 + pre * (1.0 - gate))
            readout_out[j] = scaled * (1.0 + readout * (1.0 - readout_gate))

        @pl.when((strip_step == 0) & (layer_step == 1))
        def _():
            charge_out[...] = charges

    def chunk_step(n, carry):
        def body(k, c):
            domain_step(n * chunk + k, k)
            return c

        lax.fori_loop(0, chunk, body, 0)
        wide_sum = mm_nt(high_ref[...], q_ref[...])
        part_sum = wide_sum[:, :channels] + wide_sum[:, channels:]
        part_sum = part_sum + mm_nt(low_ref[...], q_ref[0:channels, :])

        @pl.when(n == 0)
        def _():
            s_out[...] = part_sum

        @pl.when(n > 0)
        def _():
            s_out[...] += part_sum

        return carry

    lax.fori_loop(0, total // chunk, chunk_step, 0)
    zero_row = (KGRID // 2) * KGRID + KGRID // 2
    s_out[zero_row : zero_row + 1, :] = jnp.sum(energy_ref[...], axis=0, keepdims=True)


def backward_kernel(
    sizes,
    dims,
    all_atoms,
    near_layers,
    data,
    s_own,
    s_other,
    kernel_filter,
    embedding,
    radial,
    mix,
    charge_w,
    readout_w,
    pair_in,
    slope_in,
    readout_in,
    charge_in,
    own_out,
    other_out,
    energy_out,
    high_ref,
    low_ref,
    keep_ref,
    weight_ref,
    wt_ref,
    cg_ref,
    wb3,
    re3,
    b_ref,
    f_ref,
    t_ref,
    hot_ref,
    col_ref,
    sum_ref,
    centre_ref,
):
    layers, strips = sizes
    own, width, tall, slots = dims
    here = position_here(strips)
    layer, strip, step = here
    kinds = embedding.shape[0]
    basis = radial.shape[0]
    channels = embedding.shape[1]
    waves = KGRID**3
    domains = 2 * near_layers
    spacing = basis_reach / (basis - 1)
    zero_row = (KGRID // 2) * KGRID + KGRID // 2

    sums = s_own[...] + s_other[...]
    local = sums[zero_row : zero_row + 1]
    keeper = jnp.where(rows((waves, channels)) == zero_row, 0.0, 1.0 / all_atoms)
    scale = keeper * kernel_filter[...]
    weights = jnp.concatenate([scale, scale], axis=0) * sums
    ewald = jnp.sum(weights * sums, axis=0, keepdims=True)
    energy = jnp.sum(local + 0.5 * ewald, axis=1, keepdims=True)
    energy_out[...] = jnp.broadcast_to(energy / all_atoms, energy_out.shape)
    high, low = split(weights)
    weight_ref[:, 0:channels] = high
    weight_ref[:, channels : 2 * channels] = high
    weight_ref[:, 2 * channels : 3 * channels] = low
    turned = weights.T
    high, low = split(turned)
    wt_ref[0:channels, :] = high
    wt_ref[channels : 2 * channels, :] = low

    emb = embedding[...]
    mixed = jnp.dot(emb, mix[...], precision=highest, preferred_element_type=f32)
    re3[...] = left3(
        jnp.concatenate([mixed[s : s + 1] * radial[...] for s in range(kinds)], axis=0)
    )
    wb3[...] = left3(jnp.concatenate([charge_w[...], readout_w[...]], axis=1))

    for j in range(domains):
        i = (j // near_layers) * layers + j % near_layers
        g, p = domain_of(jnp.int32(i), here, sizes)
        record = data[slot_of(g, p, here, sizes), 0:8, :]
        store_phases(
            record, layers, strips, high_ref, low_ref, j * own, keep_ref if j == 1 else None
        )
    wide = mm(wt_ref[...], high_ref[...])
    cg_ref[...] = (
        wide[:channels] + wide[channels:] + mm(wt_ref[0:channels, :], low_ref[...])
    )

    base = ((layer * strips + (strip - (strip & 1))) * own).astype(f32)
    groups = 2 * own // 16
    sum_ref[...] = jnp.zeros_like(sum_ref)

    def domain_step(j, carry):
        i = (j // near_layers) * layers + lax.rem(j, near_layers)
        g, p = domain_of(i, here, sizes)
        record = data[slot_of(g, p, here, sizes), 0:8, :]
        live = record[ROW_KIND : ROW_KIND + 1] >= 0.0
        column = pl.multiple_of(j * own, own)
        grad = jnp.where(live, cg_ref[:, pl.ds(column, own)], 0.0)
        grad = mm(wb3[...], right3(jnp.concatenate([grad, readout_in[j]], axis=0)))
        grad = grad * slope_in[j]
        b_ref[...] = mm(re3[...], right3(grad))
        code = pair_in[j, 3]
        d = pair_in[j, 5]
        quarter = d * (1.0 / envelope_reach)
        square = quarter * quarter
        envelope = 1.0 / (1.0 + square * square)
        slope = -envelope * envelope * (4.0 / envelope_reach) * square * quarter
        lean = envelope * (-2.0 / spacing)
        u = d * (1.0 / spacing)
        same = [code == float(s) for s in range(kinds)]
        force = jnp.zeros((slots, own), f32)
        for b in range(basis):
            t, e = pair_basis(u, float(b))
            chosen = jnp.zeros((slots, own), f32)
            for s in range(kinds):
                k = s * basis + b
                chosen = jnp.where(same[s], b_ref[k : k + 1, :], chosen)
            force = force + e * (lean * t + slope) * chosen
        force = force / d
        target = (pair_in[j, 4] - base).astype(i32)
        t_ref[0] = target // 16
        t_ref[1] = target & 15
        for r in range(3):
            part = force * pair_in[j, r]
            high = part.astype(bf16).astype(f32)
            f_ref[2 * r] = high
            f_ref[2 * r + 1] = part - high

            @pl.when(j == 1)
            def _():
                centre_ref[r : r + 1, :] = jnp.sum(part, axis=0, keepdims=True)

        group = rows((groups, own))
        lane16 = rows((16, own))
        for m in range(slots):
            at = slice(m * own, (m + 1) * own)
            hit = t_ref[0, m : m + 1, :] == group
            for r in range(6):
                hot = jnp.where(hit, f_ref[r, m : m + 1, :], 0.0)
                hot_ref[r * groups : (r + 1) * groups, at] = hot.astype(bf16)
            col_ref[:, at] = jnp.where(t_ref[1, m : m + 1, :] == lane16, 1.0, 0.0).astype(bf16)
        sum_ref[...] += mm_nt(hot_ref[...], col_ref[...])
        return carry

    lax.fori_loop(0, domains, domain_step, 0)

    along = mm(weight_ref[...], right3(charge_in[...]))
    turn = keep_ref[0:waves, :] * along[waves:] - keep_ref[waves:, :] * along[:waves]
    index = lanes((8, waves))
    axis = rows((8, waves))
    part_x = (index // (KGRID * KGRID)).astype(f32) / (strips * width_x)
    part_y = ((index // KGRID) % KGRID - KGRID // 2).astype(f32) / width_y
    part_z = (index % KGRID - KGRID // 2).astype(f32) / (layers * width_z)
    wave = jnp.where(axis == 0, part_x, jnp.where(axis == 1, part_y, part_z))
    wave = jnp.where(axis < 3, wave * (2.0 * math.pi), 0.0)
    ewald_grad = mm(left3(wave), right3(turn))

    spread = jnp.where(rows((16, own)) == (lanes((16, own)) & 15), 1.0, 0.0)
    wide = jnp.dot(sum_ref[...], spread, precision=highest, preferred_element_type=f32)
    half = groups // 2
    mine = rows((half, own)) == lanes((half, own)) // 16
    zero = jnp.zeros((1, own), f32)
    sides = [[], []]
    for r in range(3):
        both = wide[2 * r * groups : (2 * r + 1) * groups]
        both = both + wide[(2 * r + 1) * groups : (2 * r + 2) * groups]
        for side in range(2):
            part = both[side * half : (side + 1) * half]
            sides[side].append(jnp.sum(jnp.where(mine, part, 0.0), axis=0, keepdims=True))
    sides = [jnp.concatenate(side + [zero] * 5, axis=0) for side in sides]
    odd = (strip & 1) == 1
    own_grad = jnp.where(odd, sides[1], sides[0])
    own_out[...] = own_grad + ewald_grad
    own_out[0:3, :] += -centre_ref[0:3, :]
    other_out[...] = jnp.where(odd, sides[0], sides[1])


def final_kernel(pos, vel, frc, spec, mass, own, other, moved_out, vel_out, frc_out):
    kind = spec[...]
    factor = jnp.zeros(kind.shape, f32)
    for s in range(mass.shape[0]):
        factor = factor + jnp.where(kind == s, mass[s], 0.0)
    half_velocity = vel[...] + 0.5 * time_step * frc[...] * factor
    moved_out[...] = pos[...] + time_step * half_velocity
    forces_new = -(own[0:3, :] + other[0:3, :])
    frc_out[...] = forces_new
    vel_out[...] = half_velocity + 0.5 * time_step * forces_new * factor


def exchange(x, axis, bit):
    count = lax.axis_size(axis)
    return lax.ppermute(x, axis, [(i, i ^ bit) for i in range(count)])


def local(
    positions,
    velocities,
    forces,
    species,
    counts,
    neighbours,
    send_inplane,
    send_normal,
    embedding,
    inverse_mass,
    radial_weight,
    mix_weight,
    self_weight,
    charge_weight,
    readout_weight,
    readout_vector,
    kernel_filter,
):
    layers = lax.axis_size("gz")
    strips = lax.axis_size("xy")
    sizes = (layers, strips)
    own = positions.shape[1]
    slots = neighbours.shape[0]
    dims = (own, send_inplane.shape[1], send_normal.shape[1], slots)
    channels = embedding.shape[1]
    kinds = embedding.shape[0]
    basis = radial_weight.shape[0]
    all_atoms = own * layers * strips
    waves = KGRID**3
    vmem = pl.BlockSpec(memory_space=pltpu.VMEM)
    smem = pl.BlockSpec(memory_space=pltpu.SMEM)
    params = pltpu.CompilerParams(vmem_limit_bytes=48 * 1024 * 1024)
    kind_row = species[None, :]

    block = pl.pallas_call(
        functools.partial(pack_kernel, sizes),
        out_shape=jax.ShapeDtypeStruct((ROW_LISTS + slots, own), f32),
        in_specs=[vmem] * 4 + [smem] + [vmem] * 3 + [smem],
        out_specs=vmem,
        name="pack",
    )(
        positions,
        velocities,
        forces,
        kind_row,
        counts,
        neighbours,
        send_inplane,
        send_normal,
        inverse_mass,
    )
    data = block[None]
    bit = 1
    while bit < layers:
        data = jnp.concatenate([data, exchange(data, "gz", bit)], axis=0)
        bit *= 2
    bit = 2
    while bit < strips:
        data = jnp.concatenate([data, exchange(data, "xy", bit)], axis=0)
        bit *= 2
    data = jnp.concatenate([data, exchange(data, "xy", 1)], axis=0)

    total = layers * (strips // 2)
    chunk = min(16, total)
    near_layers = min(3, layers)
    near = 2 * near_layers
    tail = -(-kinds // 16) * 16
    depth = kinds * basis + tail
    sums, pairs, slope, readout, charges = pl.pallas_call(
        functools.partial(
            lambda *refs: forward_kernel(sizes, dims, chunk, *refs, near_layers)
        ),
        out_shape=[
            jax.ShapeDtypeStruct((2 * waves, channels), f32),
            jax.ShapeDtypeStruct((near, PAIR_BLOCKS, slots, own), f32),
            jax.ShapeDtypeStruct((near, channels, own), f32),
            jax.ShapeDtypeStruct((near, channels, own), f32),
            jax.ShapeDtypeStruct((channels, own), f32),
        ],
        in_specs=[vmem] * 8,
        out_specs=[vmem] * 5,
        scratch_shapes=[
            pltpu.VMEM((total, 8, own), f32),
            pltpu.VMEM((2 * waves, chunk * own), bf16),
            pltpu.VMEM((2 * waves, chunk * own), bf16),
            pltpu.VMEM((2 * channels, chunk * own), bf16),
            pltpu.VMEM((slots, own), f32),
            pltpu.VMEM((kinds, slots, own), f32),
            pltpu.VMEM((channels, 3 * depth), bf16),
            pltpu.VMEM((2 * channels, 3 * channels), bf16),
            pltpu.VMEM((channels, channels), f32),
            pltpu.VMEM((8, own), f32),
        ],
        compiler_params=params,
        name="forward",
    )(
        data,
        embedding,
        radial_weight,
        mix_weight,
        self_weight,
        charge_weight,
        readout_weight,
        readout_vector[None, :],
    )
    other_sums = exchange(sums, "xy", 1)
    groups = 2 * own // 16
    own_grad, other_grad, energy = pl.pallas_call(
        functools.partial(backward_kernel, sizes, dims, all_atoms, near_layers),
        out_shape=[
            jax.ShapeDtypeStruct((8, own), f32),
            jax.ShapeDtypeStruct((8, own), f32),
            jax.ShapeDtypeStruct((1, channels), f32),
        ],
        in_specs=[vmem] * 13,
        out_specs=[vmem] * 3,
        scratch_shapes=[
            pltpu.VMEM((2 * waves, near * own), bf16),
            pltpu.VMEM((2 * waves, near * own), bf16),
            pltpu.VMEM((2 * waves, own), f32),
            pltpu.VMEM((2 * waves, 3 * channels), bf16),
            pltpu.VMEM((2 * channels, 2 * waves), bf16),
            pltpu.VMEM((channels, near * own), f32),
            pltpu.VMEM((channels, 6 * channels), bf16),
            pltpu.VMEM((kinds * basis, 3 * channels), bf16),
            pltpu.VMEM((kinds * basis, own), f32),
            pltpu.VMEM((6, slots, own), f32),
            pltpu.VMEM((2, slots, own), i32),
            pltpu.VMEM((6 * groups, slots * own), bf16),
            pltpu.VMEM((16, slots * own), bf16),
            pltpu.VMEM((6 * groups, 16), f32),
            pltpu.VMEM((8, own), f32),
        ],
        compiler_params=params,
        name="backward",
    )(
        data,
        sums,
        other_sums,
        kernel_filter,
        embedding,
        radial_weight,
        mix_weight,
        charge_weight,
        readout_weight,
        pairs,
        slope,
        readout,
        charges,
    )
    arrived = exchange(other_grad, "xy", 1)
    moved, velocities_new, forces_new = pl.pallas_call(
        final_kernel,
        out_shape=[jax.ShapeDtypeStruct((3, own), f32)] * 3,
        in_specs=[vmem] * 4 + [smem] + [vmem] * 2,
        out_specs=[vmem] * 3,
        name="final",
    )(positions, velocities, forces, kind_row, inverse_mass, own_grad, arrived)
    return (moved, velocities_new, forces_new, energy[0, 0])


def solution(mesh):
    return jax.shard_map(
        local,
        mesh=mesh,
        in_specs=(
            P(None, ("gz", "xy")),
            P(None, ("gz", "xy")),
            P(None, ("gz", "xy")),
            P(("gz", "xy")),
            P(("gz", "xy")),
            P(None, ("gz", "xy")),
            P(None, ("gz", "xy")),
            P(None, ("gz", "xy")),
            P(),
            P(),
            P(),
            P(),
            P(),
            P(),
            P(),
            P(),
            P(),
        ),
        out_specs=(P(None, ("gz", "xy")), P(None, ("gz", "xy")), P(None, ("gz", "xy")), P()),
        check_vma=False,
    )
```

time: 243 us -> 56.9 us (0.23)
  waiting for transfers between devices: 90.8 us -> 13.7 us
  blocking collectives: 40.4 us -> 0 us
  other arithmetic: 33.4 us -> 0.73 us
  Pallas kernels: 0 us -> 28.4 us
  local copies, waits for them, and re-layouts: 26.5 us -> 2.13 us
  between operations: 17.7 us -> 1.37 us
  matrix products: 16.2 us -> 0 us
  starting transfers between devices: 16.4 us -> 10.1 us
    psum x1 -> x0, waiting for transfers between devices: 87 us -> none  [local(): cosine_sum, sine_sum = lax.psum((cosine_sum, sine_sum), ('gz', 'xy'))]
    psum x1 -> x0, blocking collectives: 40.4 us -> none  [local(): local_total = lax.psum(local_sum, ('gz', 'xy'))]
    pallas_call x0 -> x4, Pallas kernels: none -> 28.4 us  [the longest x1 18.3 us: local(): pl.pallas_call(functools.partial(lambda *refs: forward_kernel(sizes, dims...]
    gather x6 -> x0, local copies, waits for them, and re-layouts: 21.3 us -> none  [the longest x1 10.8 us: local_terms(): gathered = jnp.take(outgoing, neighbour_rows, axis=0)]
    scatter-add x5 -> x0, other arithmetic: 21.1 us -> none  [the longest x1 17.6 us: local_terms(): partner = jnp.take(ext_pos, neighbour_rows, axis=1)]
    dot_general x18 -> x0, matrix products: 16.2 us -> none  [the longest x2 5.14 us: local_terms(): jnp.einsum('bma,bc->mac', radial_basis, radial_weight, precision=highest)]
    ppermute x8 -> x7, waiting for transfers between devices: 3.74 us -> 13.7 us  [exchange(): return lax.ppermute(x, axis, [(i, i ^ bit) for i in range(count)])]
    ppermute x8 -> x7, starting transfers between devices: 16.4 us -> 10.1 us  [exchange(): return lax.ppermute(x, axis, [(i, i ^ bit) for i in range(count)])]
  transfers between devices with their start and end apart: 9 -> 7, of which waited for: 4 -> 7; matrix products, arithmetic and copies ran while one was open for 5% -> 0% of each run, Pallas kernels for 0% -> 0%
where the time goes in v1:
time: 56.9 us; the launch traced here: 56.5 us
  Pallas kernels  28.4 us (50%)
  waiting for transfers between devices  13.7 us (24%)
  starting transfers between devices  10.1 us (18%)
  local copies, waits for them, and re-layouts  2.13 us (4%)
  between operations  1.37 us (2%)
  other arithmetic  0.73 us (1%)
    pallas_call x1, Pallas kernels, local(): pl.pallas_call(functools.partial(lambda *refs: forward_kernel(sizes, dims...  18.3 us
    ppermute x7, waiting for transfers between devices, exchange(): return lax.ppermute(x, axis, [(i, i ^ bit) for i in range(count)])  13.7 us
    ppermute x7, starting transfers between devices, exchange(): return lax.ppermute(x, axis, [(i, i ^ bit) for i in range(count)])  10.1 us
    pallas_call x1, Pallas kernels, local(): pl.pallas_call(functools.partial(backward_kernel, sizes, dims, all_atoms,...  7.28 us
    unnamed x26, local copies, waits for them, and re-layouts  2.09 us
    pallas_call x1, Pallas kernels, local(): pl.pallas_call(functools.partial(pack_kernel, sizes), out_shape=jax.Shape...  1.48 us
    pallas_call x1, Pallas kernels, local(): pl.pallas_call(final_kernel, out_shape=[jax.ShapeDtypeStruct((3, own), f3...  1.4 us
  transfers between devices with their start and end apart: 7, of which 7 were waited for; matrix products, arithmetic and copies ran while one was open for 0% of the time, Pallas kernels for 0%

profile of v1, /device:TPU:0, one launch (start us, length us, event | category | flops | bytes accessed | tf_op | source)
XLA Modules:
  0.0 56.5 jit_solution(12684872195648614320)
XLA Ops:
  1.3 1.5 %pack.1 = f32[32,128]{1,0:T(8,128)} custom-call(f32[3,128]{1,0:T(4,128)} %pos.3, f32[3,128]{1,0:T(4,128)} %vel.3, f32[3,128]{1,0:T(4,128)} %frc.3, s32[1,128]{1,0:T(1,128)} %bitcast.12, s32[1]{0:T(128)S(6)} %copy.30.cnt, s32[24,128]{1,0:T(8,128)} %nbr.1, s32[2,32]{1,0:T(2,128)} %inplane.1, s32[2,64]{1,0:T(2,128)} %normal.1, f32[4]{0:T(128)} %mass.3), custom_call_target="tpu_custom_call" | custom-call | tf_op jit(solution)/shard_map/pack/pallas_call | solution.py:599
  2.8 0.0 copy-start.9
  2.8 3.0 %collective-permute-start = (f32[1,32,128]{2,1,0:T(8,128)}, f32[1,32,128]{2,1,0:T(8,128)S(1)}, u32[]{:S(2)}, u32[]{:S(2)}) collective-permute-start(f32[1,32,128]{2,1,0:T(8,128)} %bitcast.8), channel_id=1, source_target_pairs={{0,8},{8,0},{16,24},{24,16},{1,9},{9,1},{17,25},{25,17},{2,10},{10... | collective-permute-start | bytes 49160 | tf_op jit(solution)/shard_map/ppermute | solution.py:561
  5.8 2.0 %collective-permute-done = f32[1,32,128]{2,1,0:T(8,128)S(1)} collective-permute-done((f32[1,32,128]{2,1,0:T(8,128)}, f32[1,32,128]{2,1,0:T(8,128)S(1)}, u32[]{:S(2)}, u32[]{:S(2)}) %collective-permute-start) | collective-permute-done | bytes 16416 | tf_op jit(solution)/shard_map/ppermute | solution.py:561
  7.8 0.7 %pad_maximum_fusion.2 = f32[2,32,128]{2,1,0:T(8,128)S(1)} fusion(f32[1,32,128]{2,1,0:T(8,128)S(1)} %collective-permute-done, f32[1,32,128]{2,1,0:T(8,128)} %bitcast.9), kind=kLoop, calls=%fused_computation.2 | loop fusion | flops 8192 | bytes 65536 | tf_op jit(solution)/shard_map/concatenate | solution.py:619
  8.5 3.0 %collective-permute-start.1 = (f32[2,32,128]{2,1,0:T(8,128)S(1)}, f32[2,32,128]{2,1,0:T(8,128)S(1)}, u32[]{:S(2)}, u32[]{:S(2)}) collective-permute-start(f32[2,32,128]{2,1,0:T(8,128)S(1)} %pad_maximum_fusion.2), channel_id=1, source_target_pairs={{0,16},{8,24},{16,0},{24,8},{1,17},{9,25},{17,1},{25,9},{2,18},{10... | collective-permute-start | bytes 98312 | tf_op jit(solution)/shard_map/ppermute | solution.py:561
  11.5 0.0 copy-done.9
  11.5 1.9 %collective-permute-done.1 = f32[2,32,128]{2,1,0:T(8,128)S(1)} collective-permute-done((f32[2,32,128]{2,1,0:T(8,128)S(1)}, f32[2,32,128]{2,1,0:T(8,128)S(1)}, u32[]{:S(2)}, u32[]{:S(2)}) %collective-permute-start.1) | collective-permute-done | bytes 32800 | tf_op jit(solution)/shard_map/ppermute | solution.py:561
  13.4 1.8 %collective-permute-start.2 = (f32[4,32,128]{2,1,0:T(8,128)S(1)}, f32[4,32,128]{2,1,0:T(8,128)S(1)}, u32[]{:S(2)}, u32[]{:S(2)}) collective-permute-start(f32[4,32,128]{2,1,0:T(8,128)S(1)} %pad_maximum_fusion.1), channel_id=1, source_target_pairs={{0,2},{1,3},{2,0},{3,1},{4,6},{5,7},{6,4},{7,5},{8,10},{9,11},{10,... | collective-permute-start | bytes 196616 | tf_op jit(solution)/shard_map/ppermute | solution.py:561
  15.2 2.4 %collective-permute-done.2 = f32[4,32,128]{2,1,0:T(8,128)S(1)} collective-permute-done((f32[4,32,128]{2,1,0:T(8,128)S(1)}, f32[4,32,128]{2,1,0:T(8,128)S(1)}, u32[]{:S(2)}, u32[]{:S(2)}) %collective-permute-start.2) | collective-permute-done | bytes 65568 | tf_op jit(solution)/shard_map/ppermute | solution.py:561
  17.6 1.9 %collective-permute-start.3 = (f32[8,32,128]{2,1,0:T(8,128)S(1)}, f32[8,32,128]{2,1,0:T(8,128)S(1)}, u32[]{:S(2)}, u32[]{:S(2)}) collective-permute-start(f32[8,32,128]{2,1,0:T(8,128)S(1)} %pad_maximum_fusion), channel_id=1, source_target_pairs={{0,4},{1,5},{2,6},{3,7},{4,0},{5,1},{6,2},{7,3},{8,12},{9,13},{10,... | collective-permute-start | bytes 393224 | tf_op jit(solution)/shard_map/ppermute | solution.py:561
  19.6 3.1 %collective-permute-done.3 = f32[8,32,128]{2,1,0:T(8,128)S(1)} collective-permute-done((f32[8,32,128]{2,1,0:T(8,128)S(1)}, f32[8,32,128]{2,1,0:T(8,128)S(1)}, u32[]{:S(2)}, u32[]{:S(2)}) %collective-permute-start.3) | collective-permute-done | bytes 131104 | tf_op jit(solution)/shard_map/ppermute | solution.py:561
  22.7 0.1 collective-permute-start.4
  22.8 1.5 %collective-permute-done.4 = f32[16,32,128]{2,1,0:T(8,128)S(1)} collective-permute-done((f32[16,32,128]{2,1,0:T(8,128)S(1)}, f32[16,32,128]{2,1,0:T(8,128)S(1)}, u32[]{:S(2)}, u32[]{:S(2)}) %collective-permute-start.4) | collective-permute-done | bytes 262176 | tf_op jit(solution)/shard_map/ppermute | solution.py:561
  24.3 0.0 copy-start.1
  24.3 0.0 copy-start.2
  24.3 0.0 copy-start.3
  24.3 0.0 copy-start.4
  24.3 0.0 copy-start.5
  24.3 0.0 copy-start.6
  24.4 0.0 copy-start.8
  24.4 0.8 %copy-done.1 = f32[128,128]{1,0:T(8,128)S(1)} copy-done((f32[128,128]{1,0:T(8,128)S(1)}, f32[128,128]{1,0:T(8,128)}, u32[]{:S(2)}) %copy-start.1) | copy-done | bytes 65560
  25.1 0.0 copy-done.2
  25.2 0.0 copy-done.3
  25.2 0.0 copy-done.4
  25.2 0.0 copy-done.5
  25.2 0.0 copy-done.6
  25.2 0.0 copy-done.8
  25.2 0.0 copy-start
  25.3 18.3 %forward.1 = (f32[1024,128]{1,0:T(8,128)S(1)}, f32[6,6,24,128]{3,2,1,0:T(8,128)S(1)}, f32[6,128,128]{2,1,0:T(8,128)S(1)}, f32[6,128,128]{2,1,0:T(8,128)S(1)}, f32[128,128]{1,0:T(8,128)S(1)}) custom-call(f32[32,32,128]{2,1,0:T(8,128)S(1)} %constant_dynamic-update-slice_fusion.5.refs_0_.data, f32[4,128]{1,0:T(4,128)S(1)} %copy-done.6, ...), custom_call_target="tpu_custom_call" | custom-call | tf_op jit(solution)/shard_map/forward/pallas_call | solution.py:633
  43.5 0.2 collective-permute-start.5
  43.7 1.8 %collective-permute-done.5.s_other = f32[1024,128]{1,0:T(8,128)S(1)} collective-permute-done((f32[1024,128]{1,0:T(8,128)S(1)}, f32[1024,128]{1,0:T(8,128)S(1)}, u32[]{:S(2)}, u32[]{:S(2)}) %collective-permute-start.5) | collective-permute-done | bytes 524320 | tf_op jit(solution)/shard_map/ppermute | solution.py:561
  45.5 0.0 copy-done
  45.5 7.3 %backward.1 = (f32[8,128]{1,0:T(8,128)S(1)}, f32[8,128]{1,0:T(8,128)S(1)}, f32[1,128]{1,0:T(1,128)}) custom-call(f32[32,32,128]{2,1,0:T(8,128)S(1)} %constant_dynamic-update-slice_fusion.5.refs_0_.data, f32[1024,128]{1,0:T(8,128)S(1)} %get-tuple-element.15.s_own, f32[1024,128]{1,0:T(8,128)S(1)} %collective-permute-done.5.s_other, f32[512,128]{1,0:T(8,128)S(1)} %copy-done, ...), custom_call_target="tpu_custom_call" | custom-call | tf_op jit(solution)/shard_map/backward/pallas_call | solution.py:672
  52.8 0.0 copy-start.7
  52.8 0.6 %copy-done.7 = f32[8,128]{1,0:T(8,128)} copy-done((f32[8,128]{1,0:T(8,128)}, f32[8,128]{1,0:T(8,128)S(1)}, u32[]{:S(2)}) %copy-start.7) | copy-done | bytes 4120
  53.4 0.1 collective-permute-start.6
  53.5 1.0 %collective-permute-done.6.other = f32[8,128]{1,0:T(8,128)S(1)} collective-permute-done((f32[8,128]{1,0:T(8,128)S(1)}, f32[8,128]{1,0:T(8,128)S(1)}, u32[]{:S(2)}, u32[]{:S(2)}) %collective-permute-start.6) | collective-permute-done | bytes 4128 | tf_op jit(solution)/shard_map/ppermute | solution.py:561
  54.5 0.0 copy-start.10
  54.6 0.6 %copy-done.10 = f32[8,128]{1,0:T(8,128)} copy-done((f32[8,128]{1,0:T(8,128)}, f32[8,128]{1,0:T(8,128)S(1)}, u32[]{:S(2)}) %copy-start.10) | copy-done | bytes 4120
  55.1 1.4 %final.1 = (f32[3,128]{1,0:T(4,128)}, f32[3,128]{1,0:T(4,128)}, f32[3,128]{1,0:T(4,128)}) custom-call(f32[3,128]{1,0:T(4,128)} %pos.3, f32[3,128]{1,0:T(4,128)} %vel.3, f32[3,128]{1,0:T(4,128)} %frc.3, s32[1,128]{1,0:T(1,128)} %bitcast.13, f32[4]{0:T(128)} %mass.3, f32[8,128]{1,0:T(8,128)} %copy-done.7, f32[8,128]{1,0:T(8,128)} %copy-done.10), custom_call_target="tpu_custom_call" | custom-call | tf_op jit(solution)/shard_map/final/pallas_call | solution.py:716
  (8 shorter events, 0.1 us)
Async XLA Ops:
  2.8 8.7 %copy-start.9 = (f32[32,128]{1,0:T(8,128)S(1)}, f32[32,128]{1,0:T(8,128)}, u32[]{:S(2)}) copy-start(f32[32,128]{1,0:T(8,128)} %pack.1) | copy-start | bytes 49156
  2.8 5.0 %collective-permute-start = (f32[1,32,128]{2,1,0:T(8,128)}, f32[1,32,128]{2,1,0:T(8,128)S(1)}, u32[]{:S(2)}, u32[]{:S(2)}) collective-permute-start(f32[1,32,128]{2,1,0:T(8,128)} %bitcast.8), channel_id=1, source_target_pairs={{0,8},{8,0},{16,24},{24,16},{1,9},{9,1},{17,25},{25,17},{2,10},{10... | collective-permute-start | bytes 49160 | tf_op jit(solution)/shard_map/ppermute | solution.py:561
  8.5 4.9 %collective-permute-start.1 = (f32[2,32,128]{2,1,0:T(8,128)S(1)}, f32[2,32,128]{2,1,0:T(8,128)S(1)}, u32[]{:S(2)}, u32[]{:S(2)}) collective-permute-start(f32[2,32,128]{2,1,0:T(8,128)S(1)} %pad_maximum_fusion.2), channel_id=1, source_target_pairs={{0,16},{8,24},{16,0},{24,8},{1,17},{9,25},{17,1},{25,9},{2,18},{10... | collective-permute-start | bytes 98312 | tf_op jit(solution)/shard_map/ppermute | solution.py:561
  13.4 4.3 %collective-permute-start.2 = (f32[4,32,128]{2,1,0:T(8,128)S(1)}, f32[4,32,128]{2,1,0:T(8,128)S(1)}, u32[]{:S(2)}, u32[]{:S(2)}) collective-permute-start(f32[4,32,128]{2,1,0:T(8,128)S(1)} %pad_maximum_fusion.1), channel_id=1, source_target_pairs={{0,2},{1,3},{2,0},{3,1},{4,6},{5,7},{6,4},{7,5},{8,10},{9,11},{10,... | collective-permute-start | bytes 196616 | tf_op jit(solution)/shard_map/ppermute | solution.py:561
  17.6 5.0 %collective-permute-start.3 = (f32[8,32,128]{2,1,0:T(8,128)S(1)}, f32[8,32,128]{2,1,0:T(8,128)S(1)}, u32[]{:S(2)}, u32[]{:S(2)}) collective-permute-start(f32[8,32,128]{2,1,0:T(8,128)S(1)} %pad_maximum_fusion), channel_id=1, source_target_pairs={{0,4},{1,5},{2,6},{3,7},{4,0},{5,1},{6,2},{7,3},{8,12},{9,13},{10,... | collective-permute-start | bytes 393224 | tf_op jit(solution)/shard_map/ppermute | solution.py:561
  22.7 1.6 %collective-permute-start.4 = (f32[16,32,128]{2,1,0:T(8,128)S(1)}, f32[16,32,128]{2,1,0:T(8,128)S(1)}, u32[]{:S(2)}, u32[]{:S(2)}) collective-permute-start(f32[16,32,128]{2,1,0:T(8,128)S(1)} %get-tuple-element.26), channel_id=1, source_target_pairs={{0,1},{1,0},{2,3},{3,2},{4,5},{5,4},{6,7},{7,6},{8,9},{9,8},{10,11... | collective-permute-start | bytes 786440 | tf_op jit(solution)/shard_map/ppermute | solution.py:561
  24.3 0.8 %copy-start.1 = (f32[128,128]{1,0:T(8,128)S(1)}, f32[128,128]{1,0:T(8,128)}, u32[]{:S(2)}) copy-start(f32[128,128]{1,0:T(8,128)} %mix.1) | copy-start | bytes 196612
  24.3 0.9 %copy-start.2 = (f32[128,128]{1,0:T(8,128)S(1)}, f32[128,128]{1,0:T(8,128)}, u32[]{:S(2)}) copy-start(f32[128,128]{1,0:T(8,128)} %charge_w.1) | copy-start | bytes 196612
  24.3 0.9 %copy-start.3 = (f32[128,128]{1,0:T(8,128)S(1)}, f32[128,128]{1,0:T(8,128)}, u32[]{:S(2)}) copy-start(f32[128,128]{1,0:T(8,128)} %readout_w.1) | copy-start | bytes 196612
  24.3 0.9 %copy-start.4 = (f32[128,128]{1,0:T(8,128)S(1)}, f32[128,128]{1,0:T(8,128)}, u32[]{:S(2)}) copy-start(f32[128,128]{1,0:T(8,128)} %refs_4_.1) | copy-start | bytes 196612
  24.3 0.9 %copy-start.5 = (f32[16,128]{1,0:T(8,128)S(1)}, f32[16,128]{1,0:T(8,128)}, u32[]{:S(2)}) copy-start(f32[16,128]{1,0:T(8,128)} %radial.1) | copy-start | bytes 24580
  24.3 0.9 %copy-start.6 = (f32[4,128]{1,0:T(4,128)S(1)}, f32[4,128]{1,0:T(4,128)}, u32[]{:S(2)}) copy-start(f32[4,128]{1,0:T(4,128)} %embedding.1) | copy-start | bytes 6148
  24.4 0.9 %copy-start.8 = (f32[128]{0:T(128)S(1)}, f32[128]{0:T(128)}, u32[]{:S(2)}) copy-start(f32[128]{0:T(128)} %param.32) | copy-start | bytes 1540
  25.2 20.3 %copy-start = (f32[512,128]{1,0:T(8,128)S(1)}, f32[512,128]{1,0:T(8,128)}, u32[]{:S(2)}) copy-start(f32[512,128]{1,0:T(8,128)} %kernel_filter.1) | copy-start | bytes 786436
  43.5 2.0 %collective-permute-start.5 = (f32[1024,128]{1,0:T(8,128)S(1)}, f32[1024,128]{1,0:T(8,128)S(1)}, u32[]{:S(2)}, u32[]{:S(2)}) collective-permute-start(f32[1024,128]{1,0:T(8,128)S(1)} %get-tuple-element.15.s_own), channel_id=1, source_target_pairs={{0,1},{1,0},{2,3},{3,2},{4,5},{5,4},{6,7},{7,6},{8,9},{9,8},{10,11... | collective-permute-start | bytes 1572872 | tf_op jit(solution)/shard_map/ppermute | solution.py:561
  52.8 0.6 %copy-start.7 = (f32[8,128]{1,0:T(8,128)}, f32[8,128]{1,0:T(8,128)S(1)}, u32[]{:S(2)}) copy-start(f32[8,128]{1,0:T(8,128)S(1)} %get-tuple-element.20.own) | copy-start | bytes 12292
  53.4 1.2 %collective-permute-start.6 = (f32[8,128]{1,0:T(8,128)S(1)}, f32[8,128]{1,0:T(8,128)S(1)}, u32[]{:S(2)}, u32[]{:S(2)}) collective-permute-start(f32[8,128]{1,0:T(8,128)S(1)} %get-tuple-element.21), channel_id=1, source_target_pairs={{0,1},{1,0},{2,3},{3,2},{4,5},{5,4},{6,7},{7,6},{8,9},{9,8},{10,11... | collective-permute-start | bytes 12296 | tf_op jit(solution)/shard_map/ppermute | solution.py:561
  54.5 0.6 %copy-start.10 = (f32[8,128]{1,0:T(8,128)}, f32[8,128]{1,0:T(8,128)S(1)}, u32[]{:S(2)}) copy-start(f32[8,128]{1,0:T(8,128)S(1)} %collective-permute-done.6.other) | copy-start | bytes 12292

commit v2 on v1

v2 whole, which is shorter than its diff:
```python
import functools
import math

import jax
import jax.numpy as jnp
from jax import lax
from jax.experimental import pallas as pl
from jax.experimental.pallas import tpu as pltpu
from jax.sharding import PartitionSpec as P

KGRID = 8

time_step = 0.5
width_x = 2.0
width_y = 4.0
width_z = 2.0
far_away = 1000.0
softening = 0.25
basis_reach = 6.0
envelope_reach = 4.0
highest = lax.Precision.HIGHEST
f32 = jnp.float32
bf16 = jnp.bfloat16
i32 = jnp.int32

ROW_KIND = 3
ROW_ID = 4
ROW_INPLANE = 5
ROW_ABOVE = 6
ROW_BELOW = 7
ROW_LISTS = 8
PAIR_BLOCKS = 6


def split(x):
    high = x.astype(bf16)
    return high, (x - high.astype(f32)).astype(bf16)


def mm(a, b):
    return jnp.dot(a, b, preferred_element_type=f32)


def mm_nt(a, b):
    return lax.dot_general(a, b, (((1,), (1,)), ((), ())), preferred_element_type=f32)


def left3(x):
    high, low = split(x)
    return jnp.concatenate([high, high, low], axis=1)


def right3(x):
    high, low = split(x)
    return jnp.concatenate([high, low, high], axis=0)


def lanes(shape):
    return lax.broadcasted_iota(i32, shape, len(shape) - 1)


def rows(shape):
    return lax.broadcasted_iota(i32, shape, len(shape) - 2)


def pick(table, index):
    return jnp.take_along_axis(table, index, axis=1)


def sigmoid(x):
    return 1.0 / (1.0 + jnp.exp(-x))


def cos_sin(turns):
    half = math.pi * (turns - jnp.floor(turns + 0.5))
    sq = half * half
    sine = half * (
        1.0
        + sq
        * (
            -1.0 / 6
            + sq * (1.0 / 120 + sq * (-1.0 / 5040 + sq * (1.0 / 362880 - sq / 39916800.0)))
        )
    )
    cosine = 1.0 + sq * (
        -0.5
        + sq
        * (
            1.0 / 24
            + sq
            * (-1.0 / 720 + sq * (1.0 / 40320 + sq * (-1.0 / 3628800 + sq / 479001600.0)))
        )
    )
    return 1.0 - 2.0 * sine * sine, 2.0 * sine * cosine


def phase_tables(record, layers, strips):
    shape = (KGRID, record.shape[1])
    number = rows(shape).astype(f32)
    centred = number - float(KGRID // 2)
    cos_x, sin_x = cos_sin(number * record[0:1] / (strips * width_x))
    cos_y, sin_y = cos_sin(centred * record[1:2] / width_y)
    cos_z, sin_z = cos_sin(centred * record[2:3] / (layers * width_z))
    cos_yz, sin_yz = [], []
    for k in range(KGRID):
        c, s = cos_y[k : k + 1], sin_y[k : k + 1]
        cos_yz.append(c * cos_z - s * sin_z)
        sin_yz.append(s * cos_z + c * sin_z)
    return cos_x, sin_x, jnp.concatenate(cos_yz, axis=0), jnp.concatenate(sin_yz, axis=0)


def store_phases(record, layers, strips, refs, column):
    cos_high, cos_low, sin_high, sin_low = refs
    cos_x, sin_x, cos_yz, sin_yz = phase_tables(record, layers, strips)
    side = KGRID * KGRID
    at = pl.ds(column, record.shape[1])
    for k in range(KGRID):
        c, s = cos_x[k : k + 1], sin_x[k : k + 1]
        cosine = c * cos_yz - s * sin_yz
        sine = s * cos_yz + c * sin_yz
        here = slice(k * side, (k + 1) * side)
        cos_high[here, at], cos_low[here, at] = split(cosine)
        sin_high[here, at], sin_low[here, at] = split(sine)


def domain_at(slot, here, sizes):
    layer, strip = here
    layers, strips = sizes
    return layer ^ (slot & (layers - 1)), strip ^ (2 * (slot // layers))


def slot_of(g, p, here, sizes):
    layer, strip = here
    layers, strips = sizes
    return (g ^ layer) + layers * ((p ^ strip) >> 1)


def near_domain(j, here, sizes, near_layers):
    layer, strip = here
    layers, strips = sizes
    g = lax.rem(layer - 1 + j % near_layers + layers, layers)
    step = (j // near_layers) * (2 - 4 * (strip & 1))
    return g, lax.rem(strip + step + strips, strips)


def position_here():
    return lax.axis_index("gz").astype(i32), lax.axis_index("xy").astype(i32)


def mass_of(kind, mass):
    factor = jnp.zeros(kind.shape, f32)
    for s in range(mass.shape[0]):
        factor = factor + jnp.where(kind == s, mass[s], 0.0)
    return factor


def pack_kernel(sizes, pos, vel, frc, spec, cnt, nbr, inplane, normal, mass, out):
    layers, strips = sizes
    own = pos.shape[1]
    layer, strip = position_here()
    kind = spec[...]
    half_velocity = vel[...] + 0.5 * time_step * frc[...] * mass_of(kind, mass)
    moved = pos[...] + time_step * half_velocity
    lane = lanes((1, own))
    code = jnp.where(lane < cnt[0], kind, -1).astype(f32)
    number = ((layer * strips + strip) * own + lane).astype(f32)
    out[0:3, :] = moved
    out[ROW_KIND : ROW_KIND + 1, :] = code
    out[ROW_ID : ROW_ID + 1, :] = number
    lists = inplane[...].astype(f32)
    width = lists.shape[1]
    out[ROW_INPLANE : ROW_BELOW + 1, :] = jnp.zeros((3, own), f32)
    out[ROW_INPLANE : ROW_INPLANE + 1, 0:width] = lists[1:2]
    out[ROW_INPLANE : ROW_INPLANE + 1, width : 2 * width] = lists[0:1]
    lists = normal[...].astype(f32)
    tall = lists.shape[1]
    out[ROW_ABOVE : ROW_ABOVE + 1, 2 * width : 2 * width + tall] = lists[1:2]
    out[ROW_BELOW : ROW_BELOW + 1, 0:tall] = lists[0:1]
    out[ROW_LISTS:, :] = nbr[...].astype(f32)


def weights_kernel(
    embedding, radial, mix, self_w, charge_w, readout_w, readout_v, rex3, wcu3, wb3, re3, rv_out
):
    kinds, channels = embedding.shape
    basis = radial.shape[0]
    emb = embedding[...]
    mixed = jnp.dot(emb, mix[...], precision=highest, preferred_element_type=f32)
    selfed = jnp.dot(emb, self_w[...], precision=highest, preferred_element_type=f32)
    table = jnp.concatenate([mixed[s : s + 1] * radial[...] for s in range(kinds)], axis=0)
    re3[...] = left3(table)
    rest = jnp.zeros((channels - kinds * basis - kinds, channels), f32)
    wide = jnp.concatenate([table, selfed, rest], axis=0).T
    rex3[...] = left3(wide[:, : rex3.shape[1] // 3])
    wcu3[...] = left3(jnp.concatenate([charge_w[...].T, readout_w[...].T], axis=0))
    wb3[...] = left3(jnp.concatenate([charge_w[...], readout_w[...]], axis=1))
    rv_out[...] = jnp.broadcast_to(readout_v[...], (channels, channels)).T


def tables_kernel(sizes, data, *refs):
    own = data.shape[2]
    for n in range(data.shape[0]):
        store_phases(data[n, 0:8, :], *sizes, refs, n * own)


def pair_basis(u, b):
    t = u - b
    return t, jnp.exp(-(t * t))


def forward_kernel(
    sizes,
    dims,
    group,
    near_layers,
    early,
    mine,
    theirs,
    rex3,
    wcu3,
    rv_ref,
    radial,
    q_out,
    energy_out,
    pair_out,
    slope_out,
    readout_out,
    *rest,
):
    layers, strips = sizes
    own, width, tall, slots, kinds = dims
    if early:
        first, u_ref, w_ref, x_ref, energy_ref = rest
    else:
        cos_out, sin_out, first, u_ref, w_ref, x_ref, energy_ref, *tables = rest
    here = position_here()
    basis = radial.shape[0]
    channels = rv_ref.shape[0]
    total = mine.shape[0]
    near = 2 * near_layers
    lane8 = lanes((8, own))
    row8 = rows((8, own))
    energy_ref[...] = jnp.zeros_like(energy_ref)
    box = strips * width_x
    partner = (here[0], here[1] ^ 1)

    def first_step(i):
        g, p = domain_at(i, here, sizes)
        lower = theirs[slot_of(g, lax.rem(p + strips - 1, strips), partner, sizes)]
        upper = theirs[slot_of(g, lax.rem(p + 1, strips), partner, sizes)]
        at = jnp.broadcast_to(lower[ROW_INPLANE : ROW_INPLANE + 1], (8, own)).astype(i32)
        from_lower = pick(lower, at)
        at = jnp.broadcast_to(upper[ROW_INPLANE : ROW_INPLANE + 1], (8, own)).astype(i32)
        from_upper = pick(upper, at)
        down = jnp.where(p == 0, -box, 0.0)
        up = jnp.where(p == strips - 1, box, 0.0)
        shift = jnp.where(row8 == 0, jnp.where(lane8 < width, down, up), 0.0)
        first[i] = jnp.where(lane8 < width, from_lower, from_upper) + shift

    def first_steps(n, carry):
        for k in range(group):
            first_step(n * group + k)
        return carry

    lax.fori_loop(0, total // group, first_steps, 0)

    bound = jnp.where((row8 == ROW_KIND) | (row8 == ROW_ID), -1.0, 0.0)
    padding = jnp.where(row8 < 3, far_away, -1.0)
    spacing = basis_reach / (basis - 1)

    def normal_ghosts(g, p, move, row):
        other = lax.rem(g + move + layers, layers)
        j = slot_of(other, p, here, sizes)
        near_by = mine[j, 0:8, :]
        at = jnp.broadcast_to(near_by[row : row + 1], (8, own)).astype(i32)
        inside = at < own
        at = at & (own - 1)
        found = jnp.where(inside, pick(near_by, at), pick(first[j], at))
        beyond = (g + move < 0) | (g + move >= layers)
        return jnp.where(beyond, bound, found)

    def geometry(i, k):
        g, p = domain_at(i, here, sizes)
        record = mine[i, 0:8, :]
        below = normal_ghosts(g, p, -1, ROW_ABOVE)
        above = normal_ghosts(g, p, 1, ROW_BELOW)
        parts = (
            record,
            jnp.where(lane8 < 2 * width, first[i], below),
            jnp.where(lane8 < tall, above, padding),
        )
        index = mine[i, ROW_LISTS : ROW_LISTS + slots, :].astype(i32)
        part = index // own
        at = index & (own - 1)

        def gathered(r):
            a, b, c = [pick(jnp.broadcast_to(q[r : r + 1], (slots, own)), at) for q in parts]
            return jnp.where(part == 0, a, jnp.where(part == 1, b, c))

        dx = gathered(0) - record[0:1]
        dy = gathered(1) - record[1:2]
        dz = gathered(2) - record[2:3]
        code = gathered(ROW_KIND)
        d = jnp.sqrt(dx * dx + dy * dy + dz * dz + softening)
        quarter = d * (1.0 / envelope_reach)
        square = quarter * quarter
        envelope = 1.0 / (1.0 + square * square)
        u_ref[k] = d * (1.0 / spacing)
        for s in range(kinds):
            w_ref[k, s] = jnp.where(code == float(s), envelope, 0.0)
        turn = lax.rem(g - here[0] + 1 + layers, layers)
        side = here[1] + 2 - 4 * (here[1] & 1)
        strip_step = jnp.where(p == here[1], 0, jnp.where(p == lax.rem(side + strips, strips), 1, 2))
        j = jnp.where((turn < near_layers) & (strip_step < 2), strip_step * near_layers + turn, near)
        pair_out[j, 0] = dx
        pair_out[j, 1] = dy
        pair_out[j, 2] = dz
        pair_out[j, 3] = code
        pair_out[j, 4] = gathered(ROW_ID)
        pair_out[j, 5] = d
        return record[ROW_KIND : ROW_KIND + 1], j

    def basis_sums(k, kind_row):
        centre = rows((basis, own)).astype(f32)
        sums = [jnp.zeros((basis, own), f32) for s in range(kinds)]
        for m in range(slots):
            t, e = pair_basis(u_ref[k, m : m + 1, :], centre)
            for s in range(kinds):
                sums[s] = sums[s] + e * w_ref[k, s, m : m + 1, :]
        tail = x_ref.shape[0] // 3 - kinds * basis
        one_hot = jnp.where(rows((tail, own)).astype(f32) == kind_row, 1.0, 0.0)
        x_ref[:, k * own : (k + 1) * own] = right3(jnp.concatenate(sums + [one_hot], axis=0))

    def group_step(n, place):
        start = n * group
        found = [geometry(start + k, k) for k in range(group)]
        for k in range(group):
            basis_sums(k, found[k][0])
        live = jnp.concatenate([kind_row for kind_row, _ in found], axis=1) >= 0.0
        pre = mm(rex3[...], x_ref[...])
        gate = sigmoid(pre)
        hidden = pre * gate
        both = mm(wcu3[...], right3(hidden))
        charges = jnp.where(live, both[:channels], 0.0)
        readout = both[channels:]
        readout_gate = sigmoid(readout)
        rv = jnp.concatenate([rv_ref[...]] * group, axis=1)
        scaled = jnp.where(live, rv * readout_gate, 0.0)
        local = scaled * readout
        slope = gate * (1.0 + pre * (1.0 - gate))
        back = scaled * (1.0 + readout * (1.0 - readout_gate))
        wide = jnp.sum(local.reshape(channels // 8, 8, group * own), axis=0)
        for k in range(group):
            energy_ref[...] += wide[:, k * own : (k + 1) * own]
        column = pl.multiple_of(place * own, own)
        high, low = split(charges)
        q_out[0:channels, pl.ds(column, group * own)] = high
        q_out[channels : 2 * channels, pl.ds(column, group * own)] = low
        for k in range(group):
            column = pl.multiple_of(found[k][1] * own, own)
            slope_out[:, pl.ds(column, own)] = slope[:, k * own : (k + 1) * own]
            readout_out[:, pl.ds(column, own)] = back[:, k * own : (k + 1) * own]

    if early:

        def steps(n, carry):
            group_step(n, n * group)
            return carry

        lax.fori_loop(0, total // group, steps, 0)
    else:
        chunk = q_out.shape[1] // own

        def chunk_step(c, carry):
            def steps(n, inner):
                group_step(c * (chunk // group) + n, n * group)
                return inner

            def phases(n, inner):
                record = mine[c * chunk + n, 0:8, :]
                store_phases(record, layers, strips, tables, pl.multiple_of(n * own, own))
                return inner

            lax.fori_loop(0, chunk // group, steps, 0)
            lax.fori_loop(0, chunk, phases, 0)
            for out, high, low in ((cos_out, *tables[:2]), (sin_out, *tables[2:])):
                part = structure_part(high, low, q_out, 0)

                @pl.when(c == 0)
                def _():
                    out[...] = part

                @pl.when(c > 0)
                def _():
                    out[...] += part

            return carry

        lax.fori_loop(0, total // chunk, chunk_step, 0)
    energy_out[...] = jnp.sum(energy_ref[...], axis=0, keepdims=True)
    if not early:
        cos_out[zero_row : zero_row + 1, :] = energy_out[...]


zero_row = (KGRID // 2) * KGRID + KGRID // 2


def structure_part(high, low, q, column):
    channels = q.shape[0] // 2
    at = slice(column, column + high.shape[1])
    wide = mm_nt(high[...], q[:, at])
    return wide[:, :channels] + wide[:, channels:] + mm_nt(low[...], q[0:channels, at])


def structure_kernel(first_half, chunks, *refs):
    *tables, q, energy, out = refs
    column = 0
    part = None
    for n in range(chunks):
        high, low = tables[2 * n : 2 * n + 2]
        more = structure_part(high, low, q, column)
        part = more if part is None else part + more
        column += high.shape[1]
    out[...] = part
    if first_half:
        out[zero_row : zero_row + 1, :] = energy[...]


def near_kernel(sizes, near_layers, basis, kinds, starts, mine, pairs, *refs):
    layers, strips = sizes
    *tables, cos_high, cos_low, sin_high, sin_low, live_out, fall_out = refs
    own = mine.shape[2]
    here = position_here()
    spacing = basis_reach / (basis - 1)
    outs = (cos_high, cos_low, sin_high, sin_low)
    for j in range(2 * near_layers):
        at = slice(j * own, (j + 1) * own)
        slot = slot_of(*near_domain(j, here, sizes, near_layers), here, sizes)
        record = mine[slot, 0:8, :]
        live = jnp.where(record[ROW_KIND : ROW_KIND + 1] >= 0.0, 1.0, 0.0)
        live_out[:, at] = jnp.broadcast_to(live, (8, own))
        if not starts:
            store_phases(record, layers, strips, outs, j * own)
        for n, start in enumerate(starts):
            parts = tables[4 * n : 4 * n + 4]
            if j < near_layers and n > 0:
                continue
            if j >= near_layers and n == 0:
                continue
            end = start + parts[0].shape[1] // own

            @pl.when((slot >= start) & (slot < end))
            def _():
                column = pl.multiple_of((slot - start) * own, own)
                for part, out in zip(parts, outs):
                    out[:, at] = part[:, pl.ds(column, own)]

        d = pairs[j, 5]
        quarter = d * (1.0 / envelope_reach)
        square = quarter * quarter
        envelope = 1.0 / (1.0 + square * square)
        over = 1.0 / d
        slope = -envelope * envelope * (4.0 / envelope_reach) * square * quarter * over
        lean = envelope * (-2.0 / spacing) * over
        u = d * (1.0 / spacing)
        for b in range(basis):
            t, e = pair_basis(u, float(b))
            fall_out[j, b] = e * (lean * t + slope)


def backward_kernel(
    sizes,
    dims,
    all_atoms,
    near_layers,
    cos_own,
    cos_other,
    sin_own,
    sin_other,
    kernel_filter,
    cos_high,
    cos_low,
    sin_high,
    sin_low,
    live_in,
    fall_in,
    wb3,
    re3,
    pair_in,
    slope_in,
    readout_in,
    q_in,
    own_out,
    other_out,
    energy_out,
    weight_ref,
    b_ref,
    f_ref,
    t_ref,
    hot_ref,
    col_ref,
):
    layers, strips = sizes
    own, width, tall, slots, kinds = dims
    layer, strip = position_here()
    basis = fall_in.shape[1]
    channels = slope_in.shape[0]
    waves = KGRID**3
    domains = 2 * near_layers
    lanes_all = domains * own

    cos_sum = cos_own[...] + cos_other[...]
    sin_sum = sin_own[...] + sin_other[...]
    local = cos_sum[zero_row : zero_row + 1]
    keeper = jnp.where(rows((waves, channels)) == zero_row, 0.0, 1.0 / all_atoms)
    scale = keeper * kernel_filter[...]
    weight_cos = scale * cos_sum
    weight_sin = scale * sin_sum
    ewald = jnp.sum(weight_cos * cos_sum + weight_sin * sin_sum, axis=0, keepdims=True)
    energy = jnp.sum(local + 0.5 * ewald, axis=1, keepdims=True)
    energy_out[...] = jnp.broadcast_to(energy / all_atoms, energy_out.shape)

    grad = None
    for n, (weight, high, low) in enumerate(
        ((weight_cos, cos_high, cos_low), (weight_sin, sin_high, sin_low))
    ):
        top, bottom = split(weight.T)
        wide = mm(jnp.concatenate([top, bottom], axis=0), high[...])
        part = wide[:channels] + wide[channels:] + mm(top, low[...])
        grad = part if grad is None else grad + part
        weight_ref[n * waves : (n + 1) * waves, :] = left3(weight)
    grad = grad * live_in[0:1, :]
    both = jnp.concatenate([grad, readout_in[:, 0:lanes_all]], axis=0)
    grad = mm(wb3[...], right3(both)) * slope_in[:, 0:lanes_all]
    b_ref[...] = mm(re3[...], right3(grad))

    mine = slice(own, 2 * own)
    charge_high = q_in[0:channels, 0:own]
    charge_low = q_in[channels : 2 * channels, 0:own]
    along = mm(
        weight_ref[...], jnp.concatenate([charge_high, charge_low, charge_high], axis=0)
    )
    cosine = cos_high[:, mine].astype(f32) + cos_low[:, mine].astype(f32)
    sine = sin_high[:, mine].astype(f32) + sin_low[:, mine].astype(f32)
    turn = cosine * along[waves:] - sine * along[:waves]
    index = lanes((8, waves))
    axis = rows((8, waves))
    part_x = (index // (KGRID * KGRID)).astype(f32) / (strips * width_x)
    part_y = ((index // KGRID) % KGRID - KGRID // 2).astype(f32) / width_y
    part_z = (index % KGRID - KGRID // 2).astype(f32) / (layers * width_z)
    wave = jnp.where(axis == 0, part_x, jnp.where(axis == 1, part_y, part_z))
    wave = jnp.where(axis < 3, wave * (2.0 * math.pi), 0.0)
    own_out[...] = mm(left3(wave), right3(turn))

    base = ((layer * strips + (strip - (strip & 1))) * own).astype(f32)
    groups = 2 * own // 16
    group = rows((groups, own))
    lane16 = rows((16, own))
    for j in range(domains):
        code = pair_in[j, 3]
        same = [code == float(s) for s in range(kinds)]
        force = jnp.zeros((slots, own), f32)
        for b in range(basis):
            chosen = jnp.zeros((slots, own), f32)
            for s in range(kinds):
                k = s * basis + b
                row = b_ref[k : k + 1, j * own : (j + 1) * own]
                chosen = jnp.where(same[s], row, chosen)
            force = force + fall_in[j, b] * chosen
        target = (pair_in[j, 4] - base).astype(i32)
        t_ref[j, 0] = target // 16
        t_ref[j, 1] = target & 15
        for r in range(3):
            part = force * pair_in[j, r]
            high = part.astype(bf16).astype(f32)
            f_ref[j, 2 * r] = high
            f_ref[j, 2 * r + 1] = part - high
            if j == 1:
                own_out[r : r + 1, :] += -jnp.sum(part, axis=0, keepdims=True)
    for j in range(domains):
        for m in range(slots):
            at = slice((j * slots + m) * own, (j * slots + m + 1) * own)
            hit = t_ref[j, 0, m : m + 1, :] == group
            for r in range(6):
                hot = jnp.where(hit, f_ref[j, r, m : m + 1, :], 0.0)
                hot_ref[r * groups : (r + 1) * groups, at] = hot.astype(bf16)
            one = jnp.where(t_ref[j, 1, m : m + 1, :] == lane16, 1.0, 0.0)
            col_ref[:, at] = one.astype(bf16)
    found = mm_nt(hot_ref[...], col_ref[...])

    spread = jnp.where(rows((16, own)) == (lanes((16, own)) & 15), 1.0, 0.0)
    wide = jnp.dot(found, spread, precision=highest, preferred_element_type=f32)
    half = groups // 2
    fits = rows((half, own)) == lanes((half, own)) // 16
    odd = (strip & 1) == 1
    other_out[...] = jnp.zeros_like(other_out)
    for r in range(3):
        both = wide[2 * r * groups : (2 * r + 1) * groups]
        both = both + wide[(2 * r + 1) * groups : (2 * r + 2) * groups]
        sides = [
            jnp.sum(jnp.where(fits, both[n * half : (n + 1) * half], 0.0), axis=0, keepdims=True)
            for n in range(2)
        ]
        own_out[r : r + 1, :] += jnp.where(odd, sides[1], sides[0])
        other_out[r : r + 1, :] = jnp.where(odd, sides[0], sides[1])


def final_kernel(pos, vel, frc, spec, mass, own, other, moved_out, vel_out, frc_out):
    factor = mass_of(spec[...], mass)
    half_velocity = vel[...] + 0.5 * time_step * frc[...] * factor
    moved_out[...] = pos[...] + time_step * half_velocity
    forces_new = -(own[0:3, :] + other[0:3, :])
    frc_out[...] = forces_new
    vel_out[...] = half_velocity + 0.5 * time_step * forces_new * factor


def exchange(x, axis, bit):
    count = lax.axis_size(axis)
    return lax.ppermute(x, axis, [(i, i ^ bit) for i in range(count)])


MIB = 1024 * 1024
vmem = pl.BlockSpec(memory_space=pltpu.VMEM)
smem = pl.BlockSpec(memory_space=pltpu.SMEM)


def call(kernel, name, outs, ins, scratch=(), limit=8, scalars=(), work=10**8):
    return pl.pallas_call(
        kernel,
        out_shape=[jax.ShapeDtypeStruct(shape, dtype) for shape, dtype in outs],
        in_specs=[smem if n in scalars else vmem for n in range(len(ins))],
        out_specs=[vmem] * len(outs),
        scratch_shapes=[pltpu.VMEM(shape, dtype) for shape, dtype in scratch],
        compiler_params=pltpu.CompilerParams(vmem_limit_bytes=limit * MIB),
        cost_estimate=pl.CostEstimate(flops=work, bytes_accessed=MIB, transcendentals=0),
        name=name,
    )(*ins)


def local(
    positions,
    velocities,
    forces,
    species,
    counts,
    neighbours,
    send_inplane,
    send_normal,
    embedding,
    inverse_mass,
    radial_weight,
    mix_weight,
    self_weight,
    charge_weight,
    readout_weight,
    readout_vector,
    kernel_filter,
):
    layers = lax.axis_size("gz")
    strips = lax.axis_size("xy")
    sizes = (layers, strips)
    own = positions.shape[1]
    slots = neighbours.shape[0]
    kinds, channels = embedding.shape
    basis = radial_weight.shape[0]
    dims = (own, send_inplane.shape[1], send_normal.shape[1], slots, kinds)
    all_atoms = own * layers * strips
    waves = KGRID**3
    kind_row = species[None, :]
    total = layers * (strips // 2)
    early = total <= 16
    group = min(4, total)
    near_layers = min(3, layers)
    near = 2 * near_layers
    depth = kinds * basis + -(-kinds // 16) * 16

    (block,) = call(
        functools.partial(pack_kernel, sizes),
        "pack",
        [((ROW_LISTS + slots, own), f32)],
        (
            positions,
            velocities,
            forces,
            kind_row,
            counts,
            neighbours,
            send_inplane,
            send_normal,
            inverse_mass,
        ),
        scalars=(4, 8),
        limit=1,
    )
    rex3, wcu3, wb3, re3, rv = call(
        weights_kernel,
        "weights",
        [
            ((channels, 3 * depth), bf16),
            ((2 * channels, 3 * channels), bf16),
            ((channels, 6 * channels), bf16),
            ((kinds * basis, 3 * channels), bf16),
            ((channels, channels), f32),
        ],
        (
            embedding,
            radial_weight,
            mix_weight,
            self_weight,
            charge_weight,
            readout_weight,
            readout_vector[None, :],
        ),
    )

    def phases(data):
        wide = data.shape[0] * own
        return call(
            functools.partial(tables_kernel, sizes),
            "tables",
            [((waves, wide), bf16)] * 4,
            (data,),
        )

    data = block[None]
    bit = 1
    while bit < layers:
        data = jnp.concatenate([data, exchange(data, "gz", bit)], axis=0)
        bit *= 2
    tables, starts = [], []
    if early:
        tables.append(phases(data))
        starts.append(0)
    bit = 2
    while bit < strips:
        arrived = exchange(data, "xy", bit)
        if early:
            tables.append(phases(arrived))
            starts.append(data.shape[0])
        data = jnp.concatenate([data, arrived], axis=0)
        bit *= 2
    theirs = exchange(data[:, 0:8, :], "xy", 1)

    chunk = min(16, total)
    outs = [
        ((2 * channels, chunk * own), bf16),
        ((1, channels), f32),
        ((near + 1, PAIR_BLOCKS, slots, own), f32),
        ((channels, (near + 1) * own), f32),
        ((channels, (near + 1) * own), f32),
    ]
    scratch = [
        ((total, 8, own), f32),
        ((group, slots, own), f32),
        ((group, kinds, slots, own), f32),
        ((3 * depth, group * own), bf16),
        ((8, own), f32),
    ]
    if not early:
        outs += [((waves, channels), f32)] * 2
        scratch += [((waves, chunk * own), bf16)] * 4
    q, energy_row, pairs, slope, readout, *sums = call(
        functools.partial(forward_kernel, sizes, dims, group, near_layers, early),
        "forward",
        outs,
        (data, theirs, rex3, wcu3, rv, radial_weight),
        scratch,
        limit=16 if early else 48,
    )
    for n in range(2 if early else 0):
        parts = [t for table in tables for t in table[2 * n : 2 * n + 2]]
        sums += call(
            functools.partial(structure_kernel, n == 0, len(tables)),
            "structure",
            [((waves, channels), f32)],
            (*parts, q, energy_row),
            limit=16,
            work=10**9,
        )
    others = [exchange(part, "xy", 1) for part in sums]
    near_parts = call(
        functools.partial(near_kernel, sizes, near_layers, basis, kinds, starts),
        "near",
        [((waves, near * own), bf16)] * 4
        + [((8, near * own), f32), ((near, basis, slots, own), f32)],
        (data, pairs, *[t for table in tables for t in table]),
        limit=8 if early else 32,
    )
    groups = 2 * own // 16
    own_grad, other_grad, energy = call(
        functools.partial(backward_kernel, sizes, dims, all_atoms, near_layers),
        "backward",
        [((8, own), f32), ((8, own), f32), ((1, channels), f32)],
        (
            sums[0],
            others[0],
            sums[1],
            others[1],
            kernel_filter,
            *near_parts,
            wb3,
            re3,
            pairs,
            slope,
            readout,
            q,
        ),
        [
            ((2 * waves, 3 * channels), bf16),
            ((kinds * basis, near * own), f32),
            ((near, 6, slots, own), f32),
            ((near, 2, slots, own), i32),
            ((6 * groups, near * slots * own), bf16),
            ((16, near * slots * own), bf16),
        ],
        limit=24,
    )
    arrived = exchange(other_grad, "xy", 1)
    moved, velocities_new, forces_new = call(
        final_kernel,
        "final",
        [((3, own), f32)] * 3,
        (positions, velocities, forces, kind_row, inverse_mass, own_grad, arrived),
        scalars=(4,),
        limit=1,
    )
    return (moved, velocities_new, forces_new, energy[0, 0])


def solution(mesh):
    return jax.shard_map(
        local,
        mesh=mesh,
        in_specs=(
            P(None, ("gz", "xy")),
            P(None, ("gz", "xy")),
            P(None, ("gz", "xy")),
            P(("gz", "xy")),
            P(("gz", "xy")),
            P(None, ("gz", "xy")),
            P(None, ("gz", "xy")),
            P(None, ("gz", "xy")),
            P(),
            P(),
            P(),
            P(),
            P(),
            P(),
            P(),
            P(),
            P(),
        ),
        out_specs=(P(None, ("gz", "xy")), P(None, ("gz", "xy")), P(None, ("gz", "xy")), P()),
        check_vma=False,
    )
```

time: 56.9 us -> 48.1 us (0.85)
  Pallas kernels: 28.4 us -> 19.2 us
  local copies, waits for them, and re-layouts: 2.13 us -> 5.5 us
  waiting for transfers between devices: 13.7 us -> 10.7 us
  other arithmetic: 0.73 us -> 0.02 us
  starting transfers between devices: 10.1 us -> 10.7 us
    pallas_call x4 -> x11, Pallas kernels: 28.4 us -> 19.2 us  [call(): pl.pallas_call(kernel, out_shape=[jax.ShapeDtypeStruct(shape, dtype) for...]
    unnamed x26 -> x46, local copies, waits for them, and re-layouts: 2.09 us -> 5.48 us
    ppermute x7 -> x8, waiting for transfers between devices: 13.7 us -> 10.7 us  [exchange(): return lax.ppermute(x, axis, [(i, i ^ bit) for i in range(count)])]
    concatenate x2, other arithmetic: 0.73 us -> 0.01 us  [local(): data = jnp.concatenate([data, exchange(data, 'gz', bit)], axis=0)]
    ppermute x7 -> x8, starting transfers between devices: 10.1 us -> 10.7 us  [exchange(): return lax.ppermute(x, axis, [(i, i ^ bit) for i in range(count)])]
  transfers between devices with their start and end apart: 7 -> 8, of which waited for: 7 -> 6; matrix products, arithmetic and copies ran while one was open for 0% -> 0% of each run, Pallas kernels for 0% -> 11%
where the time goes in v2:
time: 48.1 us; the launch traced here: 47.7 us
  Pallas kernels  19.2 us (40%)
  starting transfers between devices  10.7 us (22%)
  waiting for transfers between devices  10.7 us (22%)
  local copies, waits for them, and re-layouts  5.5 us (11%)
  between operations  1.57 us (3%)
    pallas_call x11, Pallas kernels, call(): pl.pallas_call(kernel, out_shape=[jax.ShapeDtypeStruct(shape, dtype) for...  19.2 us
    ppermute x8, waiting for transfers between devices, exchange(): return lax.ppermute(x, axis, [(i, i ^ bit) for i in range(count)])  10.7 us
    ppermute x8, starting transfers between devices, exchange(): return lax.ppermute(x, axis, [(i, i ^ bit) for i in range(count)])  10.7 us
    unnamed x46, local copies, waits for them, and re-layouts  5.48 us
  transfers between devices with their start and end apart: 8, of which 6 were waited for; matrix products, arithmetic and copies ran while one was open for 0% of the time, Pallas kernels for 11%

profile of v2, /device:TPU:0, one launch (start us, length us, event | category | flops | bytes accessed | tf_op | source)
XLA Modules:
  0.0 47.7 jit_solution(15479209551864712146)
XLA Ops:
  0.6 0.0 copy-start.1
  0.6 0.0 copy-start.2
  0.7 0.0 copy-start.3
  0.7 0.0 copy-start.4
  0.7 0.0 copy-start.5
  1.4 0.0 copy-start.6
  1.4 0.7 %copy-done.6 = s32[24,128]{1,0:T(8,128)S(1)} copy-done((s32[24,128]{1,0:T(8,128)S(1)}, s32[24,128]{1,0:T(8,128)}, u32[]{:S(2)}) %copy-start.6) | copy-done | bytes 12312
  2.1 0.0 copy-start.8
  2.1 0.7 %copy-done.8 = f32[3,128]{1,0:T(4,128)S(1)} copy-done((f32[3,128]{1,0:T(4,128)S(1)}, f32[3,128]{1,0:T(4,128)}, u32[]{:S(2)}) %copy-start.8) | copy-done | bytes 1560
  2.8 0.0 copy-start.10
  2.8 0.7 %copy-done.10 = f32[3,128]{1,0:T(4,128)S(1)} copy-done((f32[3,128]{1,0:T(4,128)S(1)}, f32[3,128]{1,0:T(4,128)}, u32[]{:S(2)}) %copy-start.10) | copy-done | bytes 1560
  3.5 0.0 copy-start.12
  3.5 0.7 %copy-done.12 = f32[3,128]{1,0:T(4,128)S(1)} copy-done((f32[3,128]{1,0:T(4,128)S(1)}, f32[3,128]{1,0:T(4,128)}, u32[]{:S(2)}) %copy-start.12) | copy-done | bytes 1560
  4.1 0.7 %copy-done.14 = s32[2,32]{1,0:T(2,128)S(1)} copy-done((s32[2,32]{1,0:T(2,128)S(1)}, s32[2,32]{1,0:T(2,128)}, u32[]{:S(2)}) %copy-start.14) | copy-done | bytes 280
  4.8 0.0 copy-start.15
  4.8 0.7 %copy-done.15 = s32[2,64]{1,0:T(2,128)S(1)} copy-done((s32[2,64]{1,0:T(2,128)S(1)}, s32[2,64]{1,0:T(2,128)}, u32[]{:S(2)}) %copy-start.15) | copy-done | bytes 536
  5.5 0.0 copy-start.17
  5.5 0.7 %copy-done.17 = s32[128]{0:T(128)S(1)} copy-done((s32[128]{0:T(128)S(1)}, s32[128]{0:T(128)}, u32[]{:S(2)}) %copy-start.17) | copy-done | bytes 536
  6.1 0.0 copy-start.19
  6.2 0.7 %copy-done.19 = f32[4]{0:T(128)S(1)} copy-done((f32[4]{0:T(128)S(1)}, f32[4]{0:T(128)}, u32[]{:S(2)}) %copy-start.19) | copy-done | bytes 40
  6.8 0.0 copy-start.7
  6.8 0.0 copy-start.16
  6.8 0.6 %pack.1 = f32[32,128]{1,0:T(8,128)S(1)} custom-call(f32[3,128]{1,0:T(4,128)S(1)} %copy-done.8, f32[3,128]{1,0:T(4,128)S(1)} %copy-done.10, f32[3,128]{1,0:T(4,128)S(1)} %copy-done.12, s32[1,128]{1,0:T(1,128)S(1)} %bitcast.11, s32[1]{0:T(128)S(6)} %copy.25.cnt, s32[24,128]{1,0:T(8,128)S(1)} %copy-done.6, s32[2,32]{1,0:T(2,128)S(1)} %copy-done.14, ...), custom_call_target="tpu_custom_call" | custom-call | flops 100000000 | bytes 1048576 | tf_op jit(solution)/shard_map/pack/pallas_call | solution.py:628
  7.4 3.0 %collective-permute-start = (f32[1,32,128]{2,1,0:T(8,128)S(1)}, f32[1,32,128]{2,1,0:T(8,128)S(1)}, u32[]{:S(2)}, u32[]{:S(2)}) collective-permute-start(f32[1,32,128]{2,1,0:T(8,128)S(1)} %bitcast.6), channel_id=1, source_target_pairs={{0,8},{8,0},{16,24},{24,16},{1,9},{9,1},{17,25},{25,17},{2,10},{10... | collective-permute-start | bytes 49160 | tf_op jit(solution)/shard_map/ppermute | solution.py:619
  10.5 1.7 %collective-permute-done = f32[1,32,128]{2,1,0:T(8,128)S(1)} collective-permute-done((f32[1,32,128]{2,1,0:T(8,128)S(1)}, f32[1,32,128]{2,1,0:T(8,128)S(1)}, u32[]{:S(2)}, u32[]{:S(2)}) %collective-permute-start) | collective-permute-done | bytes 16416 | tf_op jit(solution)/shard_map/ppermute | solution.py:619
  12.2 3.0 %collective-permute-start.1 = (f32[2,32,128]{2,1,0:T(8,128)S(1)}, f32[2,32,128]{2,1,0:T(8,128)S(1)}, u32[]{:S(2)}, u32[]{:S(2)}) collective-permute-start(f32[2,32,128]{2,1,0:T(8,128)S(1)} %pad_maximum_fusion.2), channel_id=1, source_target_pairs={{0,16},{8,24},{16,0},{24,8},{1,17},{9,25},{17,1},{25,9},{2,18},{10... | collective-permute-start | bytes 98312 | tf_op jit(solution)/shard_map/ppermute | solution.py:619
  15.2 1.9 %collective-permute-done.1 = f32[2,32,128]{2,1,0:T(8,128)S(1)} collective-permute-done((f32[2,32,128]{2,1,0:T(8,128)S(1)}, f32[2,32,128]{2,1,0:T(8,128)S(1)}, u32[]{:S(2)}, u32[]{:S(2)}) %collective-permute-start.1) | collective-permute-done | bytes 32800 | tf_op jit(solution)/shard_map/ppermute | solution.py:619
  17.1 1.8 %collective-permute-start.2 = (f32[4,32,128]{2,1,0:T(8,128)S(1)}, f32[4,32,128]{2,1,0:T(8,128)S(1)}, u32[]{:S(2)}, u32[]{:S(2)}) collective-permute-start(f32[4,32,128]{2,1,0:T(8,128)S(1)} %pad_maximum_fusion.1.data), channel_id=1, source_target_pairs={{0,2},{1,3},{2,0},{3,1},{4,6},{5,7},{6,4},{7,5},{8,10},{9,11},{10,... | collective-permute-start | bytes 196616 | tf_op jit(solution)/shard_map/ppermute | solution.py:619
  18.9 2.4 %collective-permute-done.2.data = f32[4,32,128]{2,1,0:T(8,128)S(1)} collective-permute-done((f32[4,32,128]{2,1,0:T(8,128)S(1)}, f32[4,32,128]{2,1,0:T(8,128)S(1)}, u32[]{:S(2)}, u32[]{:S(2)}) %collective-permute-start.2) | collective-permute-done | bytes 65568 | tf_op jit(solution)/shard_map/ppermute | solution.py:619
  21.4 1.9 %collective-permute-start.3 = (f32[8,32,128]{2,1,0:T(8,128)S(1)}, f32[8,32,128]{2,1,0:T(8,128)S(1)}, u32[]{:S(2)}, u32[]{:S(2)}) collective-permute-start(f32[8,32,128]{2,1,0:T(8,128)S(1)} %pad_maximum_fusion), channel_id=1, source_target_pairs={{0,4},{1,5},{2,6},{3,7},{4,0},{5,1},{6,2},{7,3},{8,12},{9,13},{10,... | collective-permute-start | bytes 393224 | tf_op jit(solution)/shard_map/ppermute | solution.py:619
  23.3 3.1 %collective-permute-done.3.data = f32[8,32,128]{2,1,0:T(8,128)S(1)} collective-permute-done((f32[8,32,128]{2,1,0:T(8,128)S(1)}, f32[8,32,128]{2,1,0:T(8,128)S(1)}, u32[]{:S(2)}, u32[]{:S(2)}) %collective-permute-start.3) | collective-permute-done | bytes 131104 | tf_op jit(solution)/shard_map/ppermute | solution.py:619
  26.5 0.1 collective-permute-start.4
  26.5 0.0 copy-done.1
  26.5 0.0 copy-done.2
  26.6 0.0 copy-done.3
  26.6 0.0 copy-done.4
  26.6 0.0 copy-done.5
  26.6 0.0 copy-done.7
  26.6 0.0 copy-done.16
  26.6 0.4 weights.1
  27.1 0.7 %tables.3 = (bf16[512,512]{1,0:T(8,128)(2,1)S(1)}, bf16[512,512]{1,0:T(8,128)(2,1)S(1)}, bf16[512,512]{1,0:T(8,128)(2,1)S(1)}, bf16[512,512]{1,0:T(8,128)(2,1)S(1)}) custom-call(f32[4,32,128]{2,1,0:T(8,128)S(1)} %pad_maximum_fusion.1.data), custom_call_target="tpu_custom_call" | custom-call | flops 100000000 | bytes 1048576 | tf_op jit(solution)/shard_map/tables/pallas_call | solution.py:628
  27.7 0.7 %tables.4 = (bf16[512,512]{1,0:T(8,128)(2,1)S(1)}, bf16[512,512]{1,0:T(8,128)(2,1)S(1)}, bf16[512,512]{1,0:T(8,128)(2,1)S(1)}, bf16[512,512]{1,0:T(8,128)(2,1)S(1)}) custom-call(f32[4,32,128]{2,1,0:T(8,128)S(1)} %collective-permute-done.2.data), custom_call_target="tpu_custom_call" | custom-call | flops 100000000 | bytes 1048576 | tf_op jit(solution)/shard_map/tables/pallas_call | solution.py:628
  28.4 1.5 %tables.5 = (bf16[512,1024]{1,0:T(8,128)(2,1)S(1)}, bf16[512,1024]{1,0:T(8,128)(2,1)S(1)}, bf16[512,1024]{1,0:T(8,128)(2,1)S(1)}, bf16[512,1024]{1,0:T(8,128)(2,1)S(1)}) custom-call(f32[8,32,128]{2,1,0:T(8,128)S(1)} %collective-permute-done.3.data), custom_call_target="tpu_custom_call" | custom-call | flops 100000000 | bytes 1048576 | tf_op jit(solution)/shard_map/tables/pallas_call | solution.py:628
  29.9 0.0 collective-permute-done.4.theirs
  29.9 5.6 %forward.1 = (bf16[256,2048]{1,0:T(8,128)(2,1)S(1)}, f32[1,128]{1,0:T(1,128)S(1)}, f32[7,6,24,128]{3,2,1,0:T(8,128)S(1)}, f32[128,896]{1,0:T(8,128)S(1)}, f32[128,896]{1,0:T(8,128)S(1)}) custom-call(f32[16,32,128]{2,1,0:T(8,128)S(1)} %constant_dynamic-update-slice_fusion.mine, f32[16,8,128]{2,1,0:T(8,128)S(1)} %collective-permute-done.4.theirs, ...), custom_call_target="tpu_custom_call" | custom-call | flops 100000000 | bytes 1048576 | tf_op jit(solution)/shard_map/forward/pallas_call | solution.py:628
  35.5 1.3 %structure.3.sin_own = f32[512,128]{1,0:T(8,128)S(1)} custom-call(bf16[512,512]{1,0:T(8,128)(2,1)S(1)} %get-tuple-element.49.refs_0_.refs_2_, bf16[512,512]{1,0:T(8,128)(2,1)S(1)} %get-tuple-element.50.refs_1_.refs_3_, bf16[512,512]{1,0:T(8,128)(2,1)S(1)} %get-tuple-element.51.refs_2_.refs_6_, bf16[512,512]{1,0:T(8,128)(2,1)S(1)} %get-tuple-element.52.refs_3_.refs_7_, ...), custom_call_target="tpu_custom_call" | custom-call | flops 1000000000 | bytes 1048576 | tf_op jit(solution)/shard_map/structure/pallas_call | solution.py:628
  36.8 0.5 %collective-permute-start.6 = (f32[512,128]{1,0:T(8,128)S(1)}, f32[512,128]{1,0:T(8,128)S(1)}, u32[]{:S(2)}, u32[]{:S(2)}) collective-permute-start(f32[512,128]{1,0:T(8,128)S(1)} %structure.3.sin_own), channel_id=1, source_target_pairs={{0,1},{1,0},{2,3},{3,2},{4,5},{5,4},{6,7},{7,6},{8,9},{9,8},{10,11... | collective-permute-start | bytes 786440 | tf_op jit(solution)/shard_map/ppermute | solution.py:619
  37.4 1.3 %structure.2.cos_own = f32[512,128]{1,0:T(8,128)S(1)} custom-call(bf16[512,512]{1,0:T(8,128)(2,1)S(1)} %get-tuple-element.38.refs_0_, bf16[512,512]{1,0:T(8,128)(2,1)S(1)} %get-tuple-element.39.refs_1_, bf16[512,512]{1,0:T(8,128)(2,1)S(1)} %get-tuple-element.40.refs_2_.refs_4_, bf16[512,512]{1,0:T(8,128)(2,1)S(1)} %get-tuple-element.41.refs_3_.refs_5_, ...), custom_call_target="tpu_custom_call" | custom-call | flops 1000000000 | bytes 1048576 | tf_op jit(solution)/shard_map/structure/pallas_call | solution.py:628
  38.6 0.1 collective-permute-start.5
  38.7 0.9 %near.1 = (bf16[512,768]{1,0:T(8,128)(2,1)S(1)}, bf16[512,768]{1,0:T(8,128)(2,1)S(1)}, bf16[512,768]{1,0:T(8,128)(2,1)S(1)}, bf16[512,768]{1,0:T(8,128)(2,1)S(1)...) custom-call(f32[16,32,128]{2,1,0:T(8,128)S(1)} %constant_dynamic-update-slice_fusion.mine, ...), custom_call_target="tpu_custom_call" | custom-call | flops 100000000 | bytes 1048576 | tf_op jit(solution)/shard_map/near/pallas_call | solution.py:628
  39.7 0.0 collective-permute-done.6.sin_other
  39.7 0.6 %collective-permute-done.5.cos_other = f32[512,128]{1,0:T(8,128)S(1)} collective-permute-done((f32[512,128]{1,0:T(8,128)S(1)}, f32[512,128]{1,0:T(8,128)S(1)}, u32[]{:S(2)}, u32[]{:S(2)}) %collective-permute-start.5) | collective-permute-done | bytes 262176 | tf_op jit(solution)/shard_map/ppermute | solution.py:619
  40.2 0.0 copy-done
  40.2 0.0 copy-start.18
  40.3 0.0 copy-start.20
  40.3 5.1 %backward.1 = (f32[8,128]{1,0:T(8,128)S(1)}, f32[8,128]{1,0:T(8,128)S(1)}, f32[1,128]{1,0:T(1,128)}) custom-call(f32[512,128]{1,0:T(8,128)S(1)} %structure.2.cos_own, f32[512,128]{1,0:T(8,128)S(1)} %collective-permute-done.5.cos_other, f32[512,128]{1,0:T(8,128)S(1)} %structure.3.sin_own, f32[512,128]{1,0:T(8,128)S(1)} %collective-permute-done.6.sin_other, ...), custom_call_target="tpu_custom_call" | custom-call | flops 100000000 | bytes 1048576 | tf_op jit(solution)/shard_map/backward/pallas_call | solution.py:628
  45.4 0.1 collective-permute-start.7
  45.5 1.0 %collective-permute-done.7.other = f32[8,128]{1,0:T(8,128)S(1)} collective-permute-done((f32[8,128]{1,0:T(8,128)S(1)}, f32[8,128]{1,0:T(8,128)S(1)}, u32[]{:S(2)}, u32[]{:S(2)}) %collective-permute-start.7) | collective-permute-done | bytes 4128 | tf_op jit(solution)/shard_map/ppermute | solution.py:619
  46.6 0.0 copy-done.9
  46.6 0.0 copy-done.11
  46.6 0.0 copy-done.13
  46.6 0.0 copy-done.18
  46.6 0.0 copy-done.20
  46.6 1.1 %final.1 = (f32[3,128]{1,0:T(4,128)}, f32[3,128]{1,0:T(4,128)}, f32[3,128]{1,0:T(4,128)}) custom-call(f32[3,128]{1,0:T(4,128)S(1)} %copy-done.9, f32[3,128]{1,0:T(4,128)S(1)} %copy-done.11, f32[3,128]{1,0:T(4,128)S(1)} %copy-done.13, s32[1,128]{1,0:T(1,128)S(1)} %bitcast.12, f32[4]{0:T(128)S(1)} %copy-done.20, f32[8,128]{1,0:T(8,128)S(1)} %get-tuple-element.66.own, ...), custom_call_target="tpu_custom_call" | custom-call | flops 100000000 | bytes 1048576 | tf_op jit(solution)/shard_map/final/pallas_call | solution.py:628
  (14 shorter events, 0.1 us)
Async XLA Ops:
  0.6 25.9 %copy-start.1 = (f32[16,128]{1,0:T(8,128)S(1)}, f32[16,128]{1,0:T(8,128)}, u32[]{:S(2)}) copy-start(f32[16,128]{1,0:T(8,128)} %radial.3) | copy-start | bytes 24580
  0.6 25.9 %copy-start.2 = (f32[128,128]{1,0:T(8,128)S(1)}, f32[128,128]{1,0:T(8,128)}, u32[]{:S(2)}) copy-start(f32[128,128]{1,0:T(8,128)} %mix.1) | copy-start | bytes 196612
  0.7 25.9 %copy-start.3 = (f32[128,128]{1,0:T(8,128)S(1)}, f32[128,128]{1,0:T(8,128)}, u32[]{:S(2)}) copy-start(f32[128,128]{1,0:T(8,128)} %self_w.1) | copy-start | bytes 196612
  0.7 25.9 %copy-start.4 = (f32[128,128]{1,0:T(8,128)S(1)}, f32[128,128]{1,0:T(8,128)}, u32[]{:S(2)}) copy-start(f32[128,128]{1,0:T(8,128)} %charge_w.1) | copy-start | bytes 196612
  0.7 25.9 %copy-start.5 = (f32[128,128]{1,0:T(8,128)S(1)}, f32[128,128]{1,0:T(8,128)}, u32[]{:S(2)}) copy-start(f32[128,128]{1,0:T(8,128)} %readout_w.1) | copy-start | bytes 196612
  1.4 0.7 %copy-start.6 = (s32[24,128]{1,0:T(8,128)S(1)}, s32[24,128]{1,0:T(8,128)}, u32[]{:S(2)}) copy-start(s32[24,128]{1,0:T(8,128)} %nbr.1) | copy-start | bytes 36868
  2.1 0.7 %copy-start.8 = (f32[3,128]{1,0:T(4,128)S(1)}, f32[3,128]{1,0:T(4,128)}, u32[]{:S(2)}) copy-start(f32[3,128]{1,0:T(4,128)} %pos.3) | copy-start | bytes 4612
  2.8 0.7 %copy-start.10 = (f32[3,128]{1,0:T(4,128)S(1)}, f32[3,128]{1,0:T(4,128)}, u32[]{:S(2)}) copy-start(f32[3,128]{1,0:T(4,128)} %vel.3) | copy-start | bytes 4612
  3.5 0.7 %copy-start.12 = (f32[3,128]{1,0:T(4,128)S(1)}, f32[3,128]{1,0:T(4,128)}, u32[]{:S(2)}) copy-start(f32[3,128]{1,0:T(4,128)} %frc.3) | copy-start | bytes 4612
  4.1 0.7 %copy-start.14 = (s32[2,32]{1,0:T(2,128)S(1)}, s32[2,32]{1,0:T(2,128)}, u32[]{:S(2)}) copy-start(s32[2,32]{1,0:T(2,128)} %inplane.1) | copy-start | bytes 772
  4.8 0.7 %copy-start.15 = (s32[2,64]{1,0:T(2,128)S(1)}, s32[2,64]{1,0:T(2,128)}, u32[]{:S(2)}) copy-start(s32[2,64]{1,0:T(2,128)} %normal.1) | copy-start | bytes 1540
  5.5 0.7 %copy-start.17 = (s32[128]{0:T(128)S(1)}, s32[128]{0:T(128)}, u32[]{:S(2)}) copy-start(s32[128]{0:T(128)} %param.20) | copy-start | bytes 1540
  6.1 0.7 %copy-start.19 = (f32[4]{0:T(128)S(1)}, f32[4]{0:T(128)}, u32[]{:S(2)}) copy-start(f32[4]{0:T(128)} %mass.3) | copy-start | bytes 52
  6.8 19.8 %copy-start.7 = (f32[4,128]{1,0:T(4,128)S(1)}, f32[4,128]{1,0:T(4,128)}, u32[]{:S(2)}) copy-start(f32[4,128]{1,0:T(4,128)} %embedding.1) | copy-start | bytes 6148
  6.8 19.8 %copy-start.16 = (f32[128]{0:T(128)S(1)}, f32[128]{0:T(128)}, u32[]{:S(2)}) copy-start(f32[128]{0:T(128)} %param.32) | copy-start | bytes 1540
  7.4 4.8 %collective-permute-start = (f32[1,32,128]{2,1,0:T(8,128)S(1)}, f32[1,32,128]{2,1,0:T(8,128)S(1)}, u32[]{:S(2)}, u32[]{:S(2)}) collective-permute-start(f32[1,32,128]{2,1,0:T(8,128)S(1)} %bitcast.6), channel_id=1, source_target_pairs={{0,8},{8,0},{16,24},{24,16},{1,9},{9,1},{17,25},{25,17},{2,10},{10... | collective-permute-start | bytes 49160 | tf_op jit(solution)/shard_map/ppermute | solution.py:619
  12.2 4.9 %collective-permute-start.1 = (f32[2,32,128]{2,1,0:T(8,128)S(1)}, f32[2,32,128]{2,1,0:T(8,128)S(1)}, u32[]{:S(2)}, u32[]{:S(2)}) collective-permute-start(f32[2,32,128]{2,1,0:T(8,128)S(1)} %pad_maximum_fusion.2), channel_id=1, source_target_pairs={{0,16},{8,24},{16,0},{24,8},{1,17},{9,25},{17,1},{25,9},{2,18},{10... | collective-permute-start | bytes 98312 | tf_op jit(solution)/shard_map/ppermute | solution.py:619
  17.1 4.3 %collective-permute-start.2 = (f32[4,32,128]{2,1,0:T(8,128)S(1)}, f32[4,32,128]{2,1,0:T(8,128)S(1)}, u32[]{:S(2)}, u32[]{:S(2)}) collective-permute-start(f32[4,32,128]{2,1,0:T(8,128)S(1)} %pad_maximum_fusion.1.data), channel_id=1, source_target_pairs={{0,2},{1,3},{2,0},{3,1},{4,6},{5,7},{6,4},{7,5},{8,10},{9,11},{10,... | collective-permute-start | bytes 196616 | tf_op jit(solution)/shard_map/ppermute | solution.py:619
  21.4 5.0 %collective-permute-start.3 = (f32[8,32,128]{2,1,0:T(8,128)S(1)}, f32[8,32,128]{2,1,0:T(8,128)S(1)}, u32[]{:S(2)}, u32[]{:S(2)}) collective-permute-start(f32[8,32,128]{2,1,0:T(8,128)S(1)} %pad_maximum_fusion), channel_id=1, source_target_pairs={{0,4},{1,5},{2,6},{3,7},{4,0},{5,1},{6,2},{7,3},{8,12},{9,13},{10,... | collective-permute-start | bytes 393224 | tf_op jit(solution)/shard_map/ppermute | solution.py:619
  26.5 3.5 %collective-permute-start.4 = (f32[16,8,128]{2,1,0:T(8,128)S(1)}, f32[16,8,128]{2,1,0:T(8,128)S(1)}, u32[]{:S(2)}, u32[]{:S(2)}) collective-permute-start(f32[16,8,128]{2,1,0:T(8,128)S(1)} %slice.8), channel_id=1, source_target_pairs={{0,1},{1,0},{2,3},{3,2},{4,5},{5,4},{6,7},{7,6},{8,9},{9,8},{10,11... | collective-permute-start | bytes 196616 | tf_op jit(solution)/shard_map/ppermute | solution.py:619
  36.8 2.8 %collective-permute-start.6 = (f32[512,128]{1,0:T(8,128)S(1)}, f32[512,128]{1,0:T(8,128)S(1)}, u32[]{:S(2)}, u32[]{:S(2)}) collective-permute-start(f32[512,128]{1,0:T(8,128)S(1)} %structure.3.sin_own), channel_id=1, source_target_pairs={{0,1},{1,0},{2,3},{3,2},{4,5},{5,4},{6,7},{7,6},{8,9},{9,8},{10,11... | collective-permute-start | bytes 786440 | tf_op jit(solution)/shard_map/ppermute | solution.py:619
  38.6 1.6 %collective-permute-start.5 = (f32[512,128]{1,0:T(8,128)S(1)}, f32[512,128]{1,0:T(8,128)S(1)}, u32[]{:S(2)}, u32[]{:S(2)}) collective-permute-start(f32[512,128]{1,0:T(8,128)S(1)} %structure.2.cos_own), channel_id=1, source_target_pairs={{0,1},{1,0},{2,3},{3,2},{4,5},{5,4},{6,7},{7,6},{8,9},{9,8},{10,11... | collective-permute-start | bytes 786440 | tf_op jit(solution)/shard_map/ppermute | solution.py:619
  38.7 1.5 %copy-start = (f32[512,128]{1,0:T(8,128)S(1)}, f32[512,128]{1,0:T(8,128)}, u32[]{:S(2)}) copy-start(f32[512,128]{1,0:T(8,128)} %kernel_filter.1) | copy-start | bytes 786436
  40.2 6.3 %copy-start.9 = (f32[3,128]{1,0:T(4,128)S(1)}, f32[3,128]{1,0:T(4,128)}, u32[]{:S(2)}) copy-start(f32[3,128]{1,0:T(4,128)} %pos.3) | copy-start | bytes 4612
  40.2 6.3 %copy-start.11 = (f32[3,128]{1,0:T(4,128)S(1)}, f32[3,128]{1,0:T(4,128)}, u32[]{:S(2)}) copy-start(f32[3,128]{1,0:T(4,128)} %vel.3) | copy-start | bytes 4612
  40.2 6.3 %copy-start.13 = (f32[3,128]{1,0:T(4,128)S(1)}, f32[3,128]{1,0:T(4,128)}, u32[]{:S(2)}) copy-start(f32[3,128]{1,0:T(4,128)} %frc.3) | copy-start | bytes 4612
  40.2 6.3 %copy-start.18 = (s32[128]{0:T(128)S(1)}, s32[128]{0:T(128)}, u32[]{:S(2)}) copy-start(s32[128]{0:T(128)} %param.20) | copy-start | bytes 1540
  40.3 6.3 %copy-start.20 = (f32[4]{0:T(128)S(1)}, f32[4]{0:T(128)}, u32[]{:S(2)}) copy-start(f32[4]{0:T(128)} %mass.3) | copy-start | bytes 52
  45.4 1.2 %collective-permute-start.7 = (f32[8,128]{1,0:T(8,128)S(1)}, f32[8,128]{1,0:T(8,128)S(1)}, u32[]{:S(2)}, u32[]{:S(2)}) collective-permute-start(f32[8,128]{1,0:T(8,128)S(1)} %get-tuple-element.67), channel_id=1, source_target_pairs={{0,1},{1,0},{2,3},{3,2},{4,5},{5,4},{6,7},{7,6},{8,9},{9,8},{10,11... | collective-permute-start | bytes 12296 | tf_op jit(solution)/shard_map/ppermute | solution.py:619

commit v3 on v2

--- a/solution.py
+++ b/solution.py
@@ -154,7 +154,7 @@
     return factor
 
 
-def pack_kernel(sizes, pos, vel, frc, spec, cnt, nbr, inplane, normal, mass, out):
+def pack_kernel(sizes, cnt, mass, pos, vel, frc, spec, nbr, inplane, normal, out):
     layers, strips = sizes
     own = pos.shape[1]
     layer, strip = position_here()
@@ -180,7 +180,7 @@
 
 
 def weights_kernel(
-    embedding, radial, mix, self_w, charge_w, readout_w, readout_v, rex3, wcu3, wb3, re3, rv_out
+    embedding, radial, mix, self_w, charge_w, readout_w, readout_v, step, rex3, wcu3, wb3, re3, rv_out
 ):
     kinds, channels = embedding.shape
     basis = radial.shape[0]
@@ -195,6 +195,10 @@
     wcu3[...] = left3(jnp.concatenate([charge_w[...].T, readout_w[...].T], axis=0))
     wb3[...] = left3(jnp.concatenate([charge_w[...], readout_w[...]], axis=1))
     rv_out[...] = jnp.broadcast_to(readout_v[...], (channels, channels)).T
+
+
+def lift_kernel(block, out):
+    out[0] = block[...]
 
 
 def tables_kernel(sizes, data, *refs):
@@ -624,14 +628,19 @@
 smem = pl.BlockSpec(memory_space=pltpu.SMEM)
 
 
-def call(kernel, name, outs, ins, scratch=(), limit=8, scalars=(), work=10**8):
+def call(kernel, name, outs, ins, scratch=(), limit=8, scalars=(), unread=(), work=10**8):
+    def spec(n):
+        if n in unread:
+            return pl.BlockSpec(memory_space=pl.ANY)
+        return smem if n in scalars else vmem
+
     return pl.pallas_call(
         kernel,
         out_shape=[jax.ShapeDtypeStruct(shape, dtype) for shape, dtype in outs],
-        in_specs=[smem if n in scalars else vmem for n in range(len(ins))],
+        in_specs=[spec(n) for n in range(len(ins))],
         out_specs=[vmem] * len(outs),
         scratch_shapes=[pltpu.VMEM(shape, dtype) for shape, dtype in scratch],
-        compiler_params=pltpu.CompilerParams(vmem_limit_bytes=limit * MIB),
+        compiler_params=pltpu.CompilerParams(vmem_limit_bytes=limit and limit * MIB),
         cost_estimate=pl.CostEstimate(flops=work, bytes_accessed=MIB, transcendentals=0),
         name=name,
     )(*ins)
@@ -679,19 +688,34 @@
         "pack",
         [((ROW_LISTS + slots, own), f32)],
         (
+            counts,
+            inverse_mass,
             positions,
             velocities,
             forces,
             kind_row,
-            counts,
             neighbours,
             send_inplane,
             send_normal,
-            inverse_mass,
         ),
-        scalars=(4, 8),
-        limit=1,
-    )
+        scalars=(0, 1),
+        limit=None,
+    )
+    def phases(data):
+        wide = data.shape[0] * own
+        return call(
+            functools.partial(tables_kernel, sizes),
+            "tables",
+            [((waves, wide), bf16)] * 4,
+            (data,),
+            work=4 * 10**9,
+        )
+
+    arrived = exchange(block, "gz", 1)[None]
+    (data,) = call(
+        lift_kernel, "lift", [((1, *block.shape), f32)], (block,), limit=1, work=8 * 10**9
+    )
+    data = jnp.concatenate([data, arrived], axis=0)
     rex3, wcu3, wb3, re3, rv = call(
         weights_kernel,
         "weights",
@@ -710,36 +734,32 @@
             charge_weight,
             readout_weight,
             readout_vector[None, :],
+            data,
         ),
-    )
-
-    def phases(data):
-        wide = data.shape[0] * own
-        return call(
-            functools.partial(tables_kernel, sizes),
-            "tables",
-            [((waves, wide), bf16)] * 4,
-            (data,),
-        )
-
-    data = block[None]
-    bit = 1
+        limit=None,
+        unread=(7,),
+        work=4 * 10**9,
+    )
+
+    bit = 2
     while bit < layers:
         data = jnp.concatenate([data, exchange(data, "gz", bit)], axis=0)
         bit *= 2
     tables, starts = [], []
-    if early:
-        tables.append(phases(data))
-        starts.append(0)
-    bit = 2
+    bit, fresh, start = 2, data, 0
     while bit < strips:
         arrived = exchange(data, "xy", bit)
         if early:
-            tables.append(phases(arrived))
-            starts.append(data.shape[0])
+            tables.append(phases(fresh))
+            starts.append(start)
+            start = data.shape[0]
         data = jnp.concatenate([data, arrived], axis=0)
+        fresh = arrived
         bit *= 2
     theirs = exchange(data[:, 0:8, :], "xy", 1)
+    if early:
+        tables.append(phases(fresh))
+        starts.append(start)
 
     chunk = min(16, total)
     outs = [

time: 48.1 us -> 42.3 us (0.88)
  local copies, waits for them, and re-layouts: 5.5 us -> 0.86 us
  waiting for transfers between devices: 10.7 us -> 7.59 us
  Pallas kernels: 19.2 us -> 21.9 us
  starting transfers between devices: 10.7 us -> 10.1 us
    unnamed x46 -> x32, local copies, waits for them, and re-layouts: 5.48 us -> 0.84 us
    ppermute x8, waiting for transfers between devices: 10.7 us -> 7.59 us  [exchange(): return lax.ppermute(x, axis, [(i, i ^ bit) for i in range(count)])]
    pallas_call x11 -> x12, Pallas kernels: 19.2 us -> 21.9 us  [call(): pl.pallas_call(kernel, out_shape=[jax.ShapeDtypeStruct(shape, dtype) for...]
    ppermute x8, starting transfers between devices: 10.7 us -> 10.1 us  [exchange(): return lax.ppermute(x, axis, [(i, i ^ bit) for i in range(count)])]
  transfers between devices with their start and end apart: 8 -> 8, of which waited for: 6 -> 5; matrix products, arithmetic and copies ran while one was open for 0% -> 0% of each run, Pallas kernels for 11% -> 17%
where the time goes in v3:
time: 42.3 us; the launch traced here: 42 us
  Pallas kernels  21.9 us (52%)
  starting transfers between devices  10.1 us (24%)
  waiting for transfers between devices  7.59 us (18%)
  between operations  1.53 us (4%)
  local copies, waits for them, and re-layouts  0.86 us (2%)
    pallas_call x12, Pallas kernels, call(): pl.pallas_call(kernel, out_shape=[jax.ShapeDtypeStruct(shape, dtype) for...  21.9 us
    ppermute x8, starting transfers between devices, exchange(): return lax.ppermute(x, axis, [(i, i ^ bit) for i in range(count)])  10.1 us
    ppermute x8, waiting for transfers between devices, exchange(): return lax.ppermute(x, axis, [(i, i ^ bit) for i in range(count)])  7.59 us
  transfers between devices with their start and end apart: 8, of which 5 were waited for; matrix products, arithmetic and copies ran while one was open for 0% of the time, Pallas kernels for 17%

profile of v3, /device:TPU:0, one launch (start us, length us, event | category | flops | bytes accessed | tf_op | source)
XLA Modules:
  0.0 42.0 jit_solution(1985949425832961545)
XLA Ops:
  1.3 1.5 %pack.1.block = f32[32,128]{1,0:T(8,128)} custom-call(s32[1]{0:T(128)S(6)} %copy.25.cnt, f32[4]{0:T(128)} %mass.3, f32[3,128]{1,0:T(4,128)} %pos.3, f32[3,128]{1,0:T(4,128)} %vel.3, f32[3,128]{1,0:T(4,128)} %frc.3, s32[1,128]{1,0:T(1,128)} %bitcast.6, s32[24,128]{1,0:T(8,128)} %nbr.1, s32[2,32]{1,0:T(2,128)} %inplane.1, s32[2,64]{1,0:T(2,128)} %normal.1), custom_call_target="tpu_custom_call" | custom-call | flops 100000000 | bytes 1048576 | tf_op jit(solution)/shard_map/pack/pallas_call | solution.py:637
  2.8 3.0 %collective-permute-start = (f32[32,128]{1,0:T(8,128)}, f32[32,128]{1,0:T(8,128)S(1)}, u32[]{:S(2)}, u32[]{:S(2)}) collective-permute-start(f32[32,128]{1,0:T(8,128)} %pack.1.block), channel_id=1, source_target_pairs={{0,8},{8,0},{16,24},{24,16},{1,9},{9,1},{17,25},{25,17},{2,10},{10... | collective-permute-start | bytes 49160 | tf_op jit(solution)/shard_map/ppermute | solution.py:623
  5.8 0.0 copy-start.7
  5.8 0.7 %copy-done.7 = f32[32,128]{1,0:T(8,128)S(1)} copy-done((f32[32,128]{1,0:T(8,128)S(1)}, f32[32,128]{1,0:T(8,128)}, u32[]{:S(2)}) %copy-start.7) | copy-done | bytes 16408
  6.5 1.2 %collective-permute-done = f32[32,128]{1,0:T(8,128)S(1)} collective-permute-done((f32[32,128]{1,0:T(8,128)}, f32[32,128]{1,0:T(8,128)S(1)}, u32[]{:S(2)}, u32[]{:S(2)}) %collective-permute-start) | collective-permute-done | bytes 16416 | tf_op jit(solution)/shard_map/ppermute | solution.py:623
  7.7 0.0 copy-start.13
  7.7 3.0 %collective-permute-start.1 = (f32[2,32,128]{2,1,0:T(8,128)S(1)}, f32[2,32,128]{2,1,0:T(8,128)S(1)}, u32[]{:S(2)}, u32[]{:S(2)}) collective-permute-start(f32[2,32,128]{2,1,0:T(8,128)S(1)} %pad_maximum_fusion.2.step), channel_id=1, source_target_pairs={{0,16},{8,24},{16,0},{24,8},{1,17},{9,25},{17,1},{25,9},{2,18},{10... | collective-permute-start | bytes 98312 | tf_op jit(solution)/shard_map/ppermute | solution.py:623
  10.7 0.0 copy-done.13
  10.7 2.2 %weights.1 = (bf16[128,240]{1,0:T(8,128)(2,1)}, bf16[256,384]{1,0:T(8,128)(2,1)}, bf16[128,768]{1,0:T(8,128)(2,1)}, bf16[64,384]{1,0:T(8,128)(2,1)}, f32[128,128]{1,0:T(8,128)}) custom-call(f32[4,128]{1,0:T(4,128)} %embedding.1, f32[16,128]{1,0:T(8,128)} %radial.3, f32[128,128]{1,0:T(8,128)} %mix.1, f32[128,128]{1,0:T(8,128)} %self_w.1, ...), custom_call_target="tpu_custom_call" | custom-call | flops 4000000000 | bytes 1048576 | tf_op jit(solution)/shard_map/weights/pallas_call | solution.py:637
  12.9 0.0 collective-permute-done.1
  12.9 1.6 %collective-permute-start.2 = (f32[4,32,128]{2,1,0:T(8,128)S(1)}, f32[4,32,128]{2,1,0:T(8,128)S(1)}, u32[]{:S(2)}, u32[]{:S(2)}) collective-permute-start(f32[4,32,128]{2,1,0:T(8,128)S(1)} %pad_maximum_fusion.1.data), channel_id=1, source_target_pairs={{0,2},{1,3},{2,0},{3,1},{4,6},{5,7},{6,4},{7,5},{8,10},{9,11},{10,... | collective-permute-start | bytes 196616 | tf_op jit(solution)/shard_map/ppermute | solution.py:623
  14.5 0.7 %tables.3 = (bf16[512,512]{1,0:T(8,128)(2,1)S(1)}, bf16[512,512]{1,0:T(8,128)(2,1)S(1)}, bf16[512,512]{1,0:T(8,128)(2,1)S(1)}, bf16[512,512]{1,0:T(8,128)(2,1)S(1)}) custom-call(f32[4,32,128]{2,1,0:T(8,128)S(1)} %pad_maximum_fusion.1.data), custom_call_target="tpu_custom_call" | custom-call | flops 4000000000 | bytes 1048576 | tf_op jit(solution)/shard_map/tables/pallas_call | solution.py:637
  15.2 2.1 %collective-permute-done.2.data = f32[4,32,128]{2,1,0:T(8,128)S(1)} collective-permute-done((f32[4,32,128]{2,1,0:T(8,128)S(1)}, f32[4,32,128]{2,1,0:T(8,128)S(1)}, u32[]{:S(2)}, u32[]{:S(2)}) %collective-permute-start.2) | collective-permute-done | bytes 65568 | tf_op jit(solution)/shard_map/ppermute | solution.py:623
  17.3 1.6 %collective-permute-start.3 = (f32[8,32,128]{2,1,0:T(8,128)S(1)}, f32[8,32,128]{2,1,0:T(8,128)S(1)}, u32[]{:S(2)}, u32[]{:S(2)}) collective-permute-start(f32[8,32,128]{2,1,0:T(8,128)S(1)} %pad_maximum_fusion), channel_id=1, source_target_pairs={{0,4},{1,5},{2,6},{3,7},{4,0},{5,1},{6,2},{7,3},{8,12},{9,13},{10,... | collective-permute-start | bytes 393224 | tf_op jit(solution)/shard_map/ppermute | solution.py:623
  18.9 0.7 %tables.4 = (bf16[512,512]{1,0:T(8,128)(2,1)S(1)}, bf16[512,512]{1,0:T(8,128)(2,1)S(1)}, bf16[512,512]{1,0:T(8,128)(2,1)S(1)}, bf16[512,512]{1,0:T(8,128)(2,1)S(1)}) custom-call(f32[4,32,128]{2,1,0:T(8,128)S(1)} %collective-permute-done.2.data), custom_call_target="tpu_custom_call" | custom-call | flops 4000000000 | bytes 1048576 | tf_op jit(solution)/shard_map/tables/pallas_call | solution.py:637
  19.6 2.8 %collective-permute-done.3.data = f32[8,32,128]{2,1,0:T(8,128)S(1)} collective-permute-done((f32[8,32,128]{2,1,0:T(8,128)S(1)}, f32[8,32,128]{2,1,0:T(8,128)S(1)}, u32[]{:S(2)}, u32[]{:S(2)}) %collective-permute-start.3) | collective-permute-done | bytes 131104 | tf_op jit(solution)/shard_map/ppermute | solution.py:623
  22.4 0.0 copy-start.1
  22.4 0.0 copy-start.3
  22.4 0.0 copy-start.4
  22.4 0.0 copy-start.6
  22.4 0.1 collective-permute-start.4
  22.5 1.5 %tables.5 = (bf16[512,1024]{1,0:T(8,128)(2,1)S(1)}, bf16[512,1024]{1,0:T(8,128)(2,1)S(1)}, bf16[512,1024]{1,0:T(8,128)(2,1)S(1)}, bf16[512,1024]{1,0:T(8,128)(2,1)S(1)}) custom-call(f32[8,32,128]{2,1,0:T(8,128)S(1)} %collective-permute-done.3.data), custom_call_target="tpu_custom_call" | custom-call | flops 4000000000 | bytes 1048576 | tf_op jit(solution)/shard_map/tables/pallas_call | solution.py:637
  24.0 0.0 collective-permute-done.4.theirs
  24.0 0.0 copy-done.1
  24.0 0.0 copy-done.3
  24.0 0.0 copy-done.4
  24.0 0.0 copy-done.6
  24.0 5.6 %forward.1 = (bf16[256,2048]{1,0:T(8,128)(2,1)S(1)}, f32[1,128]{1,0:T(1,128)S(1)}, f32[7,6,24,128]{3,2,1,0:T(8,128)S(1)}, f32[128,896]{1,0:T(8,128)S(1)}, f32[128,896]{1,0:T(8,128)S(1)}) custom-call(f32[16,32,128]{2,1,0:T(8,128)S(1)} %constant_dynamic-update-slice_fusion.mine, f32[16,8,128]{2,1,0:T(8,128)S(1)} %collective-permute-done.4.theirs, ...), custom_call_target="tpu_custom_call" | custom-call | flops 100000000 | bytes 1048576 | tf_op jit(solution)/shard_map/forward/pallas_call | solution.py:637
  29.7 1.3 %structure.3.sin_own = f32[512,128]{1,0:T(8,128)S(1)} custom-call(bf16[512,512]{1,0:T(8,128)(2,1)S(1)} %get-tuple-element.49.refs_0_.refs_2_, bf16[512,512]{1,0:T(8,128)(2,1)S(1)} %get-tuple-element.50.refs_1_.refs_3_, bf16[512,512]{1,0:T(8,128)(2,1)S(1)} %get-tuple-element.51.refs_2_.refs_6_, bf16[512,512]{1,0:T(8,128)(2,1)S(1)} %get-tuple-element.52.refs_3_.refs_7_, ...), custom_call_target="tpu_custom_call" | custom-call | flops 1000000000 | bytes 1048576 | tf_op jit(solution)/shard_map/structure/pallas_call | solution.py:637
  30.9 0.6 %collective-permute-start.6 = (f32[512,128]{1,0:T(8,128)S(1)}, f32[512,128]{1,0:T(8,128)S(1)}, u32[]{:S(2)}, u32[]{:S(2)}) collective-permute-start(f32[512,128]{1,0:T(8,128)S(1)} %structure.3.sin_own), channel_id=1, source_target_pairs={{0,1},{1,0},{2,3},{3,2},{4,5},{5,4},{6,7},{7,6},{8,9},{9,8},{10,11... | collective-permute-start | bytes 786440 | tf_op jit(solution)/shard_map/ppermute | solution.py:623
  31.5 1.3 %structure.2.cos_own = f32[512,128]{1,0:T(8,128)S(1)} custom-call(bf16[512,512]{1,0:T(8,128)(2,1)S(1)} %get-tuple-element.38.refs_0_, bf16[512,512]{1,0:T(8,128)(2,1)S(1)} %get-tuple-element.39.refs_1_, bf16[512,512]{1,0:T(8,128)(2,1)S(1)} %get-tuple-element.40.refs_2_.refs_4_, bf16[512,512]{1,0:T(8,128)(2,1)S(1)} %get-tuple-element.41.refs_3_.refs_5_, ...), custom_call_target="tpu_custom_call" | custom-call | flops 1000000000 | bytes 1048576 | tf_op jit(solution)/shard_map/structure/pallas_call | solution.py:637
  32.7 0.1 collective-permute-start.5
  32.8 0.0 copy-start
  32.8 0.0 copy-start.2
  32.8 0.0 copy-start.5
  32.9 0.9 %near.1 = (bf16[512,768]{1,0:T(8,128)(2,1)S(1)}, bf16[512,768]{1,0:T(8,128)(2,1)S(1)}, bf16[512,768]{1,0:T(8,128)(2,1)S(1)}, bf16[512,768]{1,0:T(8,128)(2,1)S(1)...) custom-call(f32[16,32,128]{2,1,0:T(8,128)S(1)} %constant_dynamic-update-slice_fusion.mine, ...), custom_call_target="tpu_custom_call" | custom-call | flops 100000000 | bytes 1048576 | tf_op jit(solution)/shard_map/near/pallas_call | solution.py:637
  33.8 0.0 collective-permute-done.6.sin_other
  33.8 0.5 %collective-permute-done.5.cos_other = f32[512,128]{1,0:T(8,128)S(1)} collective-permute-done((f32[512,128]{1,0:T(8,128)S(1)}, f32[512,128]{1,0:T(8,128)S(1)}, u32[]{:S(2)}, u32[]{:S(2)}) %collective-permute-start.5) | collective-permute-done | bytes 262176 | tf_op jit(solution)/shard_map/ppermute | solution.py:623
  34.3 0.0 copy-done
  34.3 0.0 copy-done.2
  34.4 0.0 copy-done.5
  34.4 0.0 copy-start.8
  34.4 0.0 copy-start.9
  34.4 0.0 copy-start.10
  34.4 0.0 copy-start.11
  34.4 0.0 copy-start.12
  34.4 5.2 %backward.1 = (f32[8,128]{1,0:T(8,128)S(1)}, f32[8,128]{1,0:T(8,128)S(1)}, f32[1,128]{1,0:T(1,128)}) custom-call(f32[512,128]{1,0:T(8,128)S(1)} %structure.2.cos_own, f32[512,128]{1,0:T(8,128)S(1)} %collective-permute-done.5.cos_other, f32[512,128]{1,0:T(8,128)S(1)} %structure.3.sin_own, f32[512,128]{1,0:T(8,128)S(1)} %collective-permute-done.6.sin_other, ...), custom_call_target="tpu_custom_call" | custom-call | flops 100000000 | bytes 1048576 | tf_op jit(solution)/shard_map/backward/pallas_call | solution.py:637
  39.6 0.1 collective-permute-start.7
  39.8 1.0 %collective-permute-done.7.other = f32[8,128]{1,0:T(8,128)S(1)} collective-permute-done((f32[8,128]{1,0:T(8,128)S(1)}, f32[8,128]{1,0:T(8,128)S(1)}, u32[]{:S(2)}, u32[]{:S(2)}) %collective-permute-start.7) | collective-permute-done | bytes 4128 | tf_op jit(solution)/shard_map/ppermute | solution.py:623
  40.8 0.0 copy-done.8
  40.8 0.0 copy-done.9
  40.8 0.0 copy-done.10
  40.8 0.0 copy-done.11
  40.8 0.0 copy-done.12
  40.8 1.1 %final.1 = (f32[3,128]{1,0:T(4,128)}, f32[3,128]{1,0:T(4,128)}, f32[3,128]{1,0:T(4,128)}) custom-call(f32[3,128]{1,0:T(4,128)S(1)} %copy-done.8, f32[3,128]{1,0:T(4,128)S(1)} %copy-done.9, f32[3,128]{1,0:T(4,128)S(1)} %copy-done.10, s32[1,128]{1,0:T(1,128)S(1)} %bitcast.7, f32[4]{0:T(128)S(1)} %copy-done.12, f32[8,128]{1,0:T(8,128)S(1)} %get-tuple-element.66.own, ...), custom_call_target="tpu_custom_call" | custom-call | flops 100000000 | bytes 1048576 | tf_op jit(solution)/shard_map/final/pallas_call | solution.py:637
  (10 shorter events, 0.1 us)
Async XLA Ops:
  2.8 5.0 %collective-permute-start = (f32[32,128]{1,0:T(8,128)}, f32[32,128]{1,0:T(8,128)S(1)}, u32[]{:S(2)}, u32[]{:S(2)}) collective-permute-start(f32[32,128]{1,0:T(8,128)} %pack.1.block), channel_id=1, source_target_pairs={{0,8},{8,0},{16,24},{24,16},{1,9},{9,1},{17,25},{25,17},{2,10},{10... | collective-permute-start | bytes 49160 | tf_op jit(solution)/shard_map/ppermute | solution.py:623
  5.8 0.8 %copy-start.7 = (f32[32,128]{1,0:T(8,128)S(1)}, f32[32,128]{1,0:T(8,128)}, u32[]{:S(2)}) copy-start(f32[32,128]{1,0:T(8,128)} %pack.1.block) | copy-start | bytes 49156
  7.7 3.0 %copy-start.13 = (f32[2,32,128]{2,1,0:T(8,128)}, f32[2,32,128]{2,1,0:T(8,128)S(1)}, u32[]{:S(2)}) copy-start(f32[2,32,128]{2,1,0:T(8,128)S(1)} %pad_maximum_fusion.2.step) | copy-start | bytes 98308
  7.7 5.2 %collective-permute-start.1 = (f32[2,32,128]{2,1,0:T(8,128)S(1)}, f32[2,32,128]{2,1,0:T(8,128)S(1)}, u32[]{:S(2)}, u32[]{:S(2)}) collective-permute-start(f32[2,32,128]{2,1,0:T(8,128)S(1)} %pad_maximum_fusion.2.step), channel_id=1, source_target_pairs={{0,16},{8,24},{16,0},{24,8},{1,17},{9,25},{17,1},{25,9},{2,18},{10... | collective-permute-start | bytes 98312 | tf_op jit(solution)/shard_map/ppermute | solution.py:623
  12.9 4.3 %collective-permute-start.2 = (f32[4,32,128]{2,1,0:T(8,128)S(1)}, f32[4,32,128]{2,1,0:T(8,128)S(1)}, u32[]{:S(2)}, u32[]{:S(2)}) collective-permute-start(f32[4,32,128]{2,1,0:T(8,128)S(1)} %pad_maximum_fusion.1.data), channel_id=1, source_target_pairs={{0,2},{1,3},{2,0},{3,1},{4,6},{5,7},{6,4},{7,5},{8,10},{9,11},{10,... | collective-permute-start | bytes 196616 | tf_op jit(solution)/shard_map/ppermute | solution.py:623
  17.3 5.0 %collective-permute-start.3 = (f32[8,32,128]{2,1,0:T(8,128)S(1)}, f32[8,32,128]{2,1,0:T(8,128)S(1)}, u32[]{:S(2)}, u32[]{:S(2)}) collective-permute-start(f32[8,32,128]{2,1,0:T(8,128)S(1)} %pad_maximum_fusion), channel_id=1, source_target_pairs={{0,4},{1,5},{2,6},{3,7},{4,0},{5,1},{6,2},{7,3},{8,12},{9,13},{10,... | collective-permute-start | bytes 393224 | tf_op jit(solution)/shard_map/ppermute | solution.py:623
  22.4 1.6 %copy-start.1 = (bf16[256,384]{1,0:T(8,128)(2,1)S(1)}, bf16[256,384]{1,0:T(8,128)(2,1)}, u32[]{:S(2)}) copy-start(bf16[256,384]{1,0:T(8,128)(2,1)} %get-tuple-element.45.wcu3) | copy-start | bytes 589828
  22.4 1.6 %copy-start.3 = (bf16[128,240]{1,0:T(8,128)(2,1)S(1)}, bf16[128,240]{1,0:T(8,128)(2,1)}, u32[]{:S(2)}) copy-start(bf16[128,240]{1,0:T(8,128)(2,1)} %get-tuple-element.44.rex3) | copy-start | bytes 184324
  22.4 1.6 %copy-start.4 = (f32[128,128]{1,0:T(8,128)S(1)}, f32[128,128]{1,0:T(8,128)}, u32[]{:S(2)}) copy-start(f32[128,128]{1,0:T(8,128)} %get-tuple-element.46.rv_ref) | copy-start | bytes 196612
  22.4 1.6 %copy-start.6 = (f32[16,128]{1,0:T(8,128)S(1)}, f32[16,128]{1,0:T(8,128)}, u32[]{:S(2)}) copy-start(f32[16,128]{1,0:T(8,128)} %radial.3) | copy-start | bytes 24580
  22.4 1.6 %collective-permute-start.4 = (f32[16,8,128]{2,1,0:T(8,128)S(1)}, f32[16,8,128]{2,1,0:T(8,128)S(1)}, u32[]{:S(2)}, u32[]{:S(2)}) collective-permute-start(f32[16,8,128]{2,1,0:T(8,128)S(1)} %slice.8), channel_id=1, source_target_pairs={{0,1},{1,0},{2,3},{3,2},{4,5},{5,4},{6,7},{7,6},{8,9},{9,8},{10,11... | collective-permute-start | bytes 196616 | tf_op jit(solution)/shard_map/ppermute | solution.py:623
  30.9 2.9 %collective-permute-start.6 = (f32[512,128]{1,0:T(8,128)S(1)}, f32[512,128]{1,0:T(8,128)S(1)}, u32[]{:S(2)}, u32[]{:S(2)}) collective-permute-start(f32[512,128]{1,0:T(8,128)S(1)} %structure.3.sin_own), channel_id=1, source_target_pairs={{0,1},{1,0},{2,3},{3,2},{4,5},{5,4},{6,7},{7,6},{8,9},{9,8},{10,11... | collective-permute-start | bytes 786440 | tf_op jit(solution)/shard_map/ppermute | solution.py:623
  32.7 1.6 %collective-permute-start.5 = (f32[512,128]{1,0:T(8,128)S(1)}, f32[512,128]{1,0:T(8,128)S(1)}, u32[]{:S(2)}, u32[]{:S(2)}) collective-permute-start(f32[512,128]{1,0:T(8,128)S(1)} %structure.2.cos_own), channel_id=1, source_target_pairs={{0,1},{1,0},{2,3},{3,2},{4,5},{5,4},{6,7},{7,6},{8,9},{9,8},{10,11... | collective-permute-start | bytes 786440 | tf_op jit(solution)/shard_map/ppermute | solution.py:623
  32.8 1.5 %copy-start = (f32[512,128]{1,0:T(8,128)S(1)}, f32[512,128]{1,0:T(8,128)}, u32[]{:S(2)}) copy-start(f32[512,128]{1,0:T(8,128)} %kernel_filter.1) | copy-start | bytes 786436
  32.8 1.5 %copy-start.2 = (bf16[128,768]{1,0:T(8,128)(2,1)S(1)}, bf16[128,768]{1,0:T(8,128)(2,1)}, u32[]{:S(2)}) copy-start(bf16[128,768]{1,0:T(8,128)(2,1)} %get-tuple-element.62.wb3) | copy-start | bytes 589828
  32.8 1.5 %copy-start.5 = (bf16[64,384]{1,0:T(8,128)(2,1)S(1)}, bf16[64,384]{1,0:T(8,128)(2,1)}, u32[]{:S(2)}) copy-start(bf16[64,384]{1,0:T(8,128)(2,1)} %get-tuple-element.63.re3) | copy-start | bytes 147460
  34.4 6.5 %copy-start.8 = (f32[3,128]{1,0:T(4,128)S(1)}, f32[3,128]{1,0:T(4,128)}, u32[]{:S(2)}) copy-start(f32[3,128]{1,0:T(4,128)} %pos.3) | copy-start | bytes 4612
  34.4 6.4 %copy-start.9 = (f32[3,128]{1,0:T(4,128)S(1)}, f32[3,128]{1,0:T(4,128)}, u32[]{:S(2)}) copy-start(f32[3,128]{1,0:T(4,128)} %vel.3) | copy-start | bytes 4612
  34.4 6.4 %copy-start.10 = (f32[3,128]{1,0:T(4,128)S(1)}, f32[3,128]{1,0:T(4,128)}, u32[]{:S(2)}) copy-start(f32[3,128]{1,0:T(4,128)} %frc.3) | copy-start | bytes 4612
  34.4 6.4 %copy-start.11 = (s32[128]{0:T(128)S(1)}, s32[128]{0:T(128)}, u32[]{:S(2)}) copy-start(s32[128]{0:T(128)} %param.20) | copy-start | bytes 1540
  34.4 6.4 %copy-start.12 = (f32[4]{0:T(128)S(1)}, f32[4]{0:T(128)}, u32[]{:S(2)}) copy-start(f32[4]{0:T(128)} %mass.3) | copy-start | bytes 52
  39.6 1.2 %collective-permute-start.7 = (f32[8,128]{1,0:T(8,128)S(1)}, f32[8,128]{1,0:T(8,128)S(1)}, u32[]{:S(2)}, u32[]{:S(2)}) collective-permute-start(f32[8,128]{1,0:T(8,128)S(1)} %get-tuple-element.67), channel_id=1, source_target_pairs={{0,1},{1,0},{2,3},{3,2},{4,5},{5,4},{6,7},{7,6},{8,9},{9,8},{10,11... | collective-permute-start | bytes 12296 | tf_op jit(solution)/shard_map/ppermute | solution.py:623

commit v4 on v3

--- a/solution.py
+++ b/solution.py
@@ -123,16 +123,33 @@
         sin_high[here, at], sin_low[here, at] = split(sine)
 
 
+def by_digits(x, strips, change):
+    result, shift = 0, 0
+    while 1 << (shift + 2) < strips:
+        result = result | (change((x >> shift) & 3) << shift)
+        shift += 2
+    return result | ((x >> shift) << shift)
+
+
+def to_place(d):
+    return jnp.where(d == 0, 0, jnp.where(d == 3, 1, d + 1))
+
+
+def from_place(d):
+    return jnp.where(d == 0, 0, jnp.where(d == 1, 3, d - 1))
+
+
 def domain_at(slot, here, sizes):
     layer, strip = here
     layers, strips = sizes
-    return layer ^ (slot & (layers - 1)), strip ^ (2 * (slot // layers))
+    x = by_digits(slot // layers, strips, from_place)
+    return layer ^ (slot & (layers - 1)), strip ^ (2 * x)
 
 
 def slot_of(g, p, here, sizes):
     layer, strip = here
     layers, strips = sizes
-    return (g ^ layer) + layers * ((p ^ strip) >> 1)
+    return (g ^ layer) + layers * by_digits((p ^ strip) >> 1, strips, to_place)
 
 
 def near_domain(j, here, sizes, near_layers):
@@ -203,13 +220,18 @@
 
 def tables_kernel(sizes, data, *refs):
     own = data.shape[2]
+    refs[4][...] = jnp.zeros_like(refs[4])
+    refs = refs[:4]
     for n in range(data.shape[0]):
         store_phases(data[n, 0:8, :], *sizes, refs, n * own)
 
 
+root = math.sqrt(math.log2(math.e))
+
+
 def pair_basis(u, b):
-    t = u - b
-    return t, jnp.exp(-(t * t))
+    t = u - b * root
+    return t, jnp.exp2(-(t * t))
 
 
 def forward_kernel(
@@ -309,7 +331,7 @@
         quarter = d * (1.0 / envelope_reach)
         square = quarter * quarter
         envelope = 1.0 / (1.0 + square * square)
-        u_ref[k] = d * (1.0 / spacing)
+        u_ref[k] = d * (root / spacing)
         for s in range(kinds):
             w_ref[k, s] = jnp.where(code == float(s), envelope, 0.0)
         turn = lax.rem(g - here[0] + 1 + layers, layers)
@@ -465,8 +487,8 @@
         envelope = 1.0 / (1.0 + square * square)
         over = 1.0 / d
         slope = -envelope * envelope * (4.0 / envelope_reach) * square * quarter * over
-        lean = envelope * (-2.0 / spacing) * over
-        u = d * (1.0 / spacing)
+        lean = envelope * (-2.0 / (spacing * root)) * over
+        u = d * (root / spacing)
         for b in range(basis):
             t, e = pair_basis(u, float(b))
             fall_out[j, b] = e * (lean * t + slope)
@@ -493,7 +515,6 @@
     pair_in,
     slope_in,
     readout_in,
-    q_in,
     own_out,
     other_out,
     energy_out,
@@ -538,28 +559,13 @@
     grad = mm(wb3[...], right3(both)) * slope_in[:, 0:lanes_all]
     b_ref[...] = mm(re3[...], right3(grad))
 
-    mine = slice(own, 2 * own)
-    charge_high = q_in[0:channels, 0:own]
-    charge_low = q_in[channels : 2 * channels, 0:own]
-    along = mm(
-        weight_ref[...], jnp.concatenate([charge_high, charge_low, charge_high], axis=0)
-    )
-    cosine = cos_high[:, mine].astype(f32) + cos_low[:, mine].astype(f32)
-    sine = sin_high[:, mine].astype(f32) + sin_low[:, mine].astype(f32)
-    turn = cosine * along[waves:] - sine * along[:waves]
-    index = lanes((8, waves))
-    axis = rows((8, waves))
-    part_x = (index // (KGRID * KGRID)).astype(f32) / (strips * width_x)
-    part_y = ((index // KGRID) % KGRID - KGRID // 2).astype(f32) / width_y
-    part_z = (index % KGRID - KGRID // 2).astype(f32) / (layers * width_z)
-    wave = jnp.where(axis == 0, part_x, jnp.where(axis == 1, part_y, part_z))
-    wave = jnp.where(axis < 3, wave * (2.0 * math.pi), 0.0)
-    own_out[...] = mm(left3(wave), right3(turn))
-
     base = ((layer * strips + (strip - (strip & 1))) * own).astype(f32)
-    groups = 2 * own // 16
+    groups = 8
+    size = 2 * own // groups
     group = rows((groups, own))
-    lane16 = rows((16, own))
+    member = rows((size, own))
+    found = None
+    own_out[...] = jnp.zeros_like(own_out)
     for j in range(domains):
         code = pair_in[j, 3]
         same = [code == float(s) for s in range(kinds)]
@@ -572,30 +578,33 @@
                 chosen = jnp.where(same[s], row, chosen)
             force = force + fall_in[j, b] * chosen
         target = (pair_in[j, 4] - base).astype(i32)
-        t_ref[j, 0] = target // 16
-        t_ref[j, 1] = target & 15
+        t_ref[j, 0] = target // size
+        t_ref[j, 1] = target & (size - 1)
         for r in range(3):
             part = force * pair_in[j, r]
             high = part.astype(bf16).astype(f32)
             f_ref[j, 2 * r] = high
             f_ref[j, 2 * r + 1] = part - high
             if j == 1:
-                own_out[r : r + 1, :] += -jnp.sum(part, axis=0, keepdims=True)
-    for j in range(domains):
+                own_out[r : r + 1, :] = -jnp.sum(part, axis=0, keepdims=True)
         for m in range(slots):
-            at = slice((j * slots + m) * own, (j * slots + m + 1) * own)
+            at = slice(m * own, (m + 1) * own)
             hit = t_ref[j, 0, m : m + 1, :] == group
-            for r in range(6):
-                hot = jnp.where(hit, f_ref[j, r, m : m + 1, :], 0.0)
-                hot_ref[r * groups : (r + 1) * groups, at] = hot.astype(bf16)
-            one = jnp.where(t_ref[j, 1, m : m + 1, :] == lane16, 1.0, 0.0)
-            col_ref[:, at] = one.astype(bf16)
-    found = mm_nt(hot_ref[...], col_ref[...])
-
-    spread = jnp.where(rows((16, own)) == (lanes((16, own)) & 15), 1.0, 0.0)
+            for r in range(3):
+                hot = [
+                    jnp.where(hit, f_ref[j, 2 * r + n, m : m + 1, :], 0.0) for n in range(2)
+                ]
+                here = slice(2 * r * groups, 2 * (r + 1) * groups)
+                hot_ref[j, here, at] = jnp.concatenate(hot, axis=0).astype(bf16)
+            one = jnp.where(t_ref[j, 1, m : m + 1, :] == member, 1.0, 0.0)
+            col_ref[j, :, at] = one.astype(bf16)
+        more = mm_nt(hot_ref[j], col_ref[j])
+        found = more if found is None else found + more
+
+    spread = jnp.where(rows((size, own)) == (lanes((size, own)) & (size - 1)), 1.0, 0.0)
     wide = jnp.dot(found, spread, precision=highest, preferred_element_type=f32)
     half = groups // 2
-    fits = rows((half, own)) == lanes((half, own)) // 16
+    fits = rows((half, own)) == lanes((half, own)) // size
     odd = (strip & 1) == 1
     other_out[...] = jnp.zeros_like(other_out)
     for r in range(3):
@@ -609,11 +618,33 @@
         other_out[r : r + 1, :] = jnp.where(odd, sides[0], sides[1])
 
 
-def final_kernel(pos, vel, frc, spec, mass, own, other, moved_out, vel_out, frc_out):
+def ewald_kernel(sizes, weights, cos_high, cos_low, sin_high, sin_low, q_in, out):
+    layers, strips = sizes
+    channels = q_in.shape[0] // 2
+    waves = cos_high.shape[0]
+    own = out.shape[1]
+    mine = slice(own, 2 * own)
+    charge_high = q_in[0:channels, 0:own]
+    charge_low = q_in[channels : 2 * channels, 0:own]
+    along = mm(weights[...], jnp.concatenate([charge_high, charge_low, charge_high], axis=0))
+    cosine = cos_high[:, mine].astype(f32) + cos_low[:, mine].astype(f32)
+    sine = sin_high[:, mine].astype(f32) + sin_low[:, mine].astype(f32)
+    turn = cosine * along[waves:] - sine * along[:waves]
+    index = lanes((8, waves))
+    axis = rows((8, waves))
+    part_x = (index // (KGRID * KGRID)).astype(f32) / (strips * width_x)
+    part_y = ((index // KGRID) % KGRID - KGRID // 2).astype(f32) / width_y
+    part_z = (index % KGRID - KGRID // 2).astype(f32) / (layers * width_z)
+    wave = jnp.where(axis == 0, part_x, jnp.where(axis == 1, part_y, part_z))
+    wave = jnp.where(axis < 3, wave * (2.0 * math.pi), 0.0)
+    out[...] = mm(left3(wave), right3(turn))
+
+
+def final_kernel(pos, vel, frc, spec, mass, own, ewald, other, moved_out, vel_out, frc_out):
     factor = mass_of(spec[...], mass)
     half_velocity = vel[...] + 0.5 * time_step * frc[...] * factor
     moved_out[...] = pos[...] + time_step * half_velocity
-    forces_new = -(own[0:3, :] + other[0:3, :])
+    forces_new = -(own[0:3, :] + ewald[0:3, :] + other[0:3, :])
     frc_out[...] = forces_new
     vel_out[...] = half_velocity + 0.5 * time_step * forces_new * factor
 
@@ -678,7 +709,7 @@
     kind_row = species[None, :]
     total = layers * (strips // 2)
     early = total <= 16
-    group = min(4, total)
+    group = min(8, total)
     near_layers = min(3, layers)
     near = 2 * near_layers
     depth = kinds * basis + -(-kinds // 16) * 16
@@ -706,7 +737,7 @@
         return call(
             functools.partial(tables_kernel, sizes),
             "tables",
-            [((waves, wide), bf16)] * 4,
+            [((waves, wide), bf16)] * 4 + [((8, own), f32)],
             (data,),
             work=4 * 10**9,
         )
@@ -745,21 +776,27 @@
     while bit < layers:
         data = jnp.concatenate([data, exchange(data, "gz", bit)], axis=0)
         bit *= 2
-    tables, starts = [], []
-    bit, fresh, start = 2, data, 0
+    tables, starts, zeros = [], [], []
+    if early:
+        *table, zero = phases(data)
+        tables.append(table)
+        starts.append(0)
+    bit = 2
     while bit < strips:
-        arrived = exchange(data, "xy", bit)
-        if early:
-            tables.append(phases(fresh))
-            starts.append(start)
-            start = data.shape[0]
-        data = jnp.concatenate([data, arrived], axis=0)
-        fresh = arrived
-        bit *= 2
-    theirs = exchange(data[:, 0:8, :], "xy", 1)
-    if early:
-        tables.append(phases(fresh))
-        starts.append(start)
+        bits = [3 * bit, bit, 2 * bit] if 2 * bit < strips else [bit]
+        parts = [exchange(data, "xy", n) for n in bits]
+        for n, part in enumerate(parts):
+            if early:
+                *table, zero = phases(part)
+                zeros.append(zero)
+                tables.append(table)
+                starts.append((n + 1) * data.shape[0])
+        data = jnp.concatenate([data] + parts, axis=0)
+        bit *= 4
+    records = data[:, 0:8, :]
+    for zero in zeros[:2]:
+        records = records + zero
+    theirs = exchange(records, "xy", 1)
 
     chunk = min(16, total)
     outs = [
@@ -806,11 +843,16 @@
         (data, pairs, *[t for table in tables for t in table]),
         limit=8 if early else 32,
     )
-    groups = 2 * own // 16
-    own_grad, other_grad, energy = call(
+    groups = 8
+    own_grad, other_grad, energy, weights3 = call(
         functools.partial(backward_kernel, sizes, dims, all_atoms, near_layers),
         "backward",
-        [((8, own), f32), ((8, own), f32), ((1, channels), f32)],
+        [
+            ((8, own), f32),
+            ((8, own), f32),
+            ((1, channels), f32),
+            ((2 * waves, 3 * channels), bf16),
+        ],
         (
             sums[0],
             others[0],
@@ -823,24 +865,29 @@
             pairs,
             slope,
             readout,
-            q,
         ),
         [
-            ((2 * waves, 3 * channels), bf16),
             ((kinds * basis, near * own), f32),
             ((near, 6, slots, own), f32),
             ((near, 2, slots, own), i32),
-            ((6 * groups, near * slots * own), bf16),
-            ((16, near * slots * own), bf16),
+            ((near, 6 * groups, slots * own), bf16),
+            ((near, 2 * own // groups, slots * own), bf16),
         ],
-        limit=24,
+        limit=16,
     )
     arrived = exchange(other_grad, "xy", 1)
+    (ewald_grad,) = call(
+        functools.partial(ewald_kernel, sizes),
+        "ewald",
+        [((8, own), f32)],
+        (weights3, *near_parts[:4], q),
+        work=4 * 10**9,
+    )
     moved, velocities_new, forces_new = call(
         final_kernel,
         "final",
         [((3, own), f32)] * 3,
-        (positions, velocities, forces, kind_row, inverse_mass, own_grad, arrived),
+        (positions, velocities, forces, kind_row, inverse_mass, own_grad, ewald_grad, arrived),
         scalars=(4,),
         limit=1,
     )

time: 42.3 us -> 37.2 us (0.88)
  waiting for transfers between devices: 7.59 us -> 3.85 us
  Pallas kernels: 21.9 us -> 20 us
  starting transfers between devices: 10.1 us -> 10.7 us
    ppermute x8 -> x9, waiting for transfers between devices: 7.59 us -> 3.85 us  [exchange(): return lax.ppermute(x, axis, [(i, i ^ bit) for i in range(count)])]
    pallas_call x12 -> x14, Pallas kernels: 21.9 us -> 20 us  [call(): pl.pallas_call(kernel, out_shape=[jax.ShapeDtypeStruct(shape, dtype) for...]
    ppermute x8 -> x9, starting transfers between devices: 10.1 us -> 10.7 us  [exchange(): return lax.ppermute(x, axis, [(i, i ^ bit) for i in range(count)])]
  transfers between devices with their start and end apart: 8 -> 9, of which waited for: 5 -> 6; matrix products, arithmetic and copies ran while one was open for 0% -> 0% of each run, Pallas kernels for 17% -> 21%
where the time goes in v4:
time: 37.2 us; the launch traced here: 36.9 us
  Pallas kernels  20 us (54%)
  starting transfers between devices  10.7 us (29%)
  waiting for transfers between devices  3.85 us (10%)
  between operations  1.47 us (4%)
  local copies, waits for them, and re-layouts  0.84 us (2%)
    pallas_call x14, Pallas kernels, call(): pl.pallas_call(kernel, out_shape=[jax.ShapeDtypeStruct(shape, dtype) for...  20 us
    ppermute x9, starting transfers between devices, exchange(): return lax.ppermute(x, axis, [(i, i ^ bit) for i in range(count)])  10.7 us
    ppermute x9, waiting for transfers between devices, exchange(): return lax.ppermute(x, axis, [(i, i ^ bit) for i in range(count)])  3.85 us
    unnamed x33, local copies, waits for them, and re-layouts  0.83 us
  transfers between devices with their start and end apart: 9, of which 6 were waited for; matrix products, arithmetic and copies ran while one was open for 0% of the time, Pallas kernels for 21%

profile of v4, /device:TPU:0, one launch (start us, length us, event | category | flops | bytes accessed | tf_op | source)
XLA Modules:
  0.0 36.9 jit_solution(16992783079926329159)
XLA Ops:
  1.3 1.5 %pack.1.block = f32[32,128]{1,0:T(8,128)} custom-call(s32[1]{0:T(128)S(6)} %copy.26.cnt, f32[4]{0:T(128)} %mass.3, f32[3,128]{1,0:T(4,128)} %pos.3, f32[3,128]{1,0:T(4,128)} %vel.3, f32[3,128]{1,0:T(4,128)} %frc.3, s32[1,128]{1,0:T(1,128)} %bitcast.6, s32[24,128]{1,0:T(8,128)} %nbr.1, s32[2,32]{1,0:T(2,128)} %inplane.1, s32[2,64]{1,0:T(2,128)} %normal.1), custom_call_target="tpu_custom_call" | custom-call | flops 100000000 | bytes 1048576 | tf_op jit(solution)/shard_map/pack/pallas_call | solution.py:668
  2.8 3.0 %collective-permute-start = (f32[32,128]{1,0:T(8,128)}, f32[32,128]{1,0:T(8,128)S(1)}, u32[]{:S(2)}, u32[]{:S(2)}) collective-permute-start(f32[32,128]{1,0:T(8,128)} %pack.1.block), channel_id=1, source_target_pairs={{0,8},{8,0},{16,24},{24,16},{1,9},{9,1},{17,25},{25,17},{2,10},{10... | collective-permute-start | bytes 49160 | tf_op jit(solution)/shard_map/ppermute | solution.py:654
  5.8 0.0 copy-start.7
  5.8 0.7 %copy-done.7 = f32[32,128]{1,0:T(8,128)S(1)} copy-done((f32[32,128]{1,0:T(8,128)S(1)}, f32[32,128]{1,0:T(8,128)}, u32[]{:S(2)}) %copy-start.7) | copy-done | bytes 16408
  6.5 1.2 %collective-permute-done = f32[32,128]{1,0:T(8,128)S(1)} collective-permute-done((f32[32,128]{1,0:T(8,128)}, f32[32,128]{1,0:T(8,128)S(1)}, u32[]{:S(2)}, u32[]{:S(2)}) %collective-permute-start) | collective-permute-done | bytes 16416 | tf_op jit(solution)/shard_map/ppermute | solution.py:654
  7.7 0.0 copy-start.13
  7.7 3.0 %collective-permute-start.1 = (f32[2,32,128]{2,1,0:T(8,128)S(1)}, f32[2,32,128]{2,1,0:T(8,128)S(1)}, u32[]{:S(2)}, u32[]{:S(2)}) collective-permute-start(f32[2,32,128]{2,1,0:T(8,128)S(1)} %pad_maximum_fusion.1.step), channel_id=1, source_target_pairs={{0,16},{8,24},{16,0},{24,8},{1,17},{9,25},{17,1},{25,9},{2,18},{10... | collective-permute-start | bytes 98312 | tf_op jit(solution)/shard_map/ppermute | solution.py:654
  10.7 0.0 copy-done.13
  10.8 2.2 %weights.1 = (bf16[128,240]{1,0:T(8,128)(2,1)}, bf16[256,384]{1,0:T(8,128)(2,1)}, bf16[128,768]{1,0:T(8,128)(2,1)}, bf16[64,384]{1,0:T(8,128)(2,1)}, f32[128,128]{1,0:T(8,128)}) custom-call(f32[4,128]{1,0:T(4,128)} %embedding.1, f32[16,128]{1,0:T(8,128)} %radial.3, f32[128,128]{1,0:T(8,128)} %mix.1, f32[128,128]{1,0:T(8,128)} %self_w.1, ...), custom_call_target="tpu_custom_call" | custom-call | flops 4000000000 | bytes 1048576 | tf_op jit(solution)/shard_map/weights/pallas_call | solution.py:668
  12.9 0.0 collective-permute-done.1
  12.9 2.5 %collective-permute-start.2 = (f32[4,32,128]{2,1,0:T(8,128)S(1)}, f32[4,32,128]{2,1,0:T(8,128)S(1)}, u32[]{:S(2)}, u32[]{:S(2)}) collective-permute-start(f32[4,32,128]{2,1,0:T(8,128)S(1)} %pad_maximum_fusion.data), channel_id=1, source_target_pairs={{0,6},{1,7},{2,4},{3,5},{4,2},{5,3},{6,0},{7,1},{8,14},{9,15},{10,... | collective-permute-start | bytes 196616 | tf_op jit(solution)/shard_map/ppermute | solution.py:654
  15.5 0.5 %collective-permute-start.3 = (f32[4,32,128]{2,1,0:T(8,128)S(1)}, f32[4,32,128]{2,1,0:T(8,128)S(1)}, u32[]{:S(2)}, u32[]{:S(2)}) collective-permute-start(f32[4,32,128]{2,1,0:T(8,128)S(1)} %pad_maximum_fusion.data), channel_id=1, source_target_pairs={{0,2},{1,3},{2,0},{3,1},{4,6},{5,7},{6,4},{7,5},{8,10},{9,11},{10,... | collective-permute-start | bytes 196616 | tf_op jit(solution)/shard_map/ppermute | solution.py:654
  16.0 0.5 %collective-permute-start.4 = (f32[4,32,128]{2,1,0:T(8,128)S(1)}, f32[4,32,128]{2,1,0:T(8,128)S(1)}, u32[]{:S(2)}, u32[]{:S(2)}) collective-permute-start(f32[4,32,128]{2,1,0:T(8,128)S(1)} %pad_maximum_fusion.data), channel_id=1, source_target_pairs={{0,4},{1,5},{2,6},{3,7},{4,0},{5,1},{6,2},{7,3},{8,12},{9,13},{10,... | collective-permute-start | bytes 196616 | tf_op jit(solution)/shard_map/ppermute | solution.py:654
  16.5 0.7 %tables.4 = (bf16[512,512]{1,0:T(8,128)(2,1)S(1)}, bf16[512,512]{1,0:T(8,128)(2,1)S(1)}, bf16[512,512]{1,0:T(8,128)(2,1)S(1)}, bf16[512,512]{1,0:T(8,128)(2,1)S(1)}, f32[8,128]{1,0:T(8,128)}) custom-call(f32[4,32,128]{2,1,0:T(8,128)S(1)} %pad_maximum_fusion.data), custom_call_target="tpu_custom_call" | custom-call | flops 4000000000 | bytes 1048576 | tf_op jit(solution)/shard_map/tables/pallas_call | solution.py:668
  17.2 1.0 %collective-permute-done.2.data = f32[4,32,128]{2,1,0:T(8,128)S(1)} collective-permute-done((f32[4,32,128]{2,1,0:T(8,128)S(1)}, f32[4,32,128]{2,1,0:T(8,128)S(1)}, u32[]{:S(2)}, u32[]{:S(2)}) %collective-permute-start.2) | collective-permute-done | bytes 65568 | tf_op jit(solution)/shard_map/ppermute | solution.py:654
  18.2 0.7 %tables.5 = (bf16[512,512]{1,0:T(8,128)(2,1)S(1)}, bf16[512,512]{1,0:T(8,128)(2,1)S(1)}, bf16[512,512]{1,0:T(8,128)(2,1)S(1)}, bf16[512,512]{1,0:T(8,128)(2,1)S(1)}, f32[8,128]{1,0:T(8,128)S(1)}) custom-call(f32[4,32,128]{2,1,0:T(8,128)S(1)} %collective-permute-done.2.data), custom_call_target="tpu_custom_call" | custom-call | flops 4000000000 | bytes 1048576 | tf_op jit(solution)/shard_map/tables/pallas_call | solution.py:668
  18.9 0.9 %collective-permute-done.3.data = f32[4,32,128]{2,1,0:T(8,128)S(1)} collective-permute-done((f32[4,32,128]{2,1,0:T(8,128)S(1)}, f32[4,32,128]{2,1,0:T(8,128)S(1)}, u32[]{:S(2)}, u32[]{:S(2)}) %collective-permute-start.3) | collective-permute-done | bytes 65568 | tf_op jit(solution)/shard_map/ppermute | solution.py:654
  19.7 0.7 %tables.6 = (bf16[512,512]{1,0:T(8,128)(2,1)S(1)}, bf16[512,512]{1,0:T(8,128)(2,1)S(1)}, bf16[512,512]{1,0:T(8,128)(2,1)S(1)}, bf16[512,512]{1,0:T(8,128)(2,1)S(1)}, f32[8,128]{1,0:T(8,128)S(1)}) custom-call(f32[4,32,128]{2,1,0:T(8,128)S(1)} %collective-permute-done.3.data), custom_call_target="tpu_custom_call" | custom-call | flops 4000000000 | bytes 1048576 | tf_op jit(solution)/shard_map/tables/pallas_call | solution.py:668
  20.4 0.0 collective-permute-done.4.data
  20.5 0.0 copy-start.1
  20.5 0.0 copy-start.3
  20.5 0.0 copy-start.4
  20.5 0.0 copy-start.6
  20.5 0.1 collective-permute-start.5
  20.6 0.7 %tables.7 = (bf16[512,512]{1,0:T(8,128)(2,1)S(1)}, bf16[512,512]{1,0:T(8,128)(2,1)S(1)}, bf16[512,512]{1,0:T(8,128)(2,1)S(1)}, bf16[512,512]{1,0:T(8,128)(2,1)S(1)}, f32[8,128]{1,0:T(8,128)}) custom-call(f32[4,32,128]{2,1,0:T(8,128)S(1)} %collective-permute-done.4.data), custom_call_target="tpu_custom_call" | custom-call | flops 4000000000 | bytes 1048576 | tf_op jit(solution)/shard_map/tables/pallas_call | solution.py:668
  21.3 0.6 %collective-permute-done.5.theirs = f32[16,8,128]{2,1,0:T(8,128)S(1)} collective-permute-done((f32[16,8,128]{2,1,0:T(8,128)S(1)}, f32[16,8,128]{2,1,0:T(8,128)S(1)}, u32[]{:S(2)}, u32[]{:S(2)}) %collective-permute-start.5) | collective-permute-done | bytes 65568 | tf_op jit(solution)/shard_map/ppermute | solution.py:654
  21.8 0.0 copy-done.1
  21.8 0.0 copy-done.3
  21.8 0.0 copy-done.4
  21.8 0.0 copy-done.6
  21.8 4.5 %forward.1 = (bf16[256,2048]{1,0:T(8,128)(2,1)S(1)}, f32[1,128]{1,0:T(1,128)S(1)}, f32[7,6,24,128]{3,2,1,0:T(8,128)S(1)}, f32[128,896]{1,0:T(8,128)S(1)}, f32[128,896]{1,0:T(8,128)S(1)}) custom-call(f32[16,32,128]{2,1,0:T(8,128)S(1)} %constant_dynamic-update-slice_fusion.mine, f32[16,8,128]{2,1,0:T(8,128)S(1)} %collective-permute-done.5.theirs, ...), custom_call_target="tpu_custom_call" | custom-call | flops 100000000 | bytes 1048576 | tf_op jit(solution)/shard_map/forward/pallas_call | solution.py:668
  26.4 1.3 %structure.3.sin_own = f32[512,128]{1,0:T(8,128)S(1)} custom-call(bf16[512,512]{1,0:T(8,128)(2,1)S(1)} %get-tuple-element.60.refs_0_.refs_2_, bf16[512,512]{1,0:T(8,128)(2,1)S(1)} %get-tuple-element.61.refs_1_.refs_3_, bf16[512,512]{1,0:T(8,128)(2,1)S(1)} %get-tuple-element.62.refs_2_.refs_6_, bf16[512,512]{1,0:T(8,128)(2,1)S(1)} %get-tuple-element.63.refs_3_.refs_7_, ...), custom_call_target="tpu_custom_call" | custom-call | flops 1000000000 | bytes 1048576 | tf_op jit(solution)/shard_map/structure/pallas_call | solution.py:668
  27.6 0.2 collective-permute-start.7
  27.9 1.3 %structure.2.cos_own = f32[512,128]{1,0:T(8,128)S(1)} custom-call(bf16[512,512]{1,0:T(8,128)(2,1)S(1)} %get-tuple-element.45.refs_0_, bf16[512,512]{1,0:T(8,128)(2,1)S(1)} %get-tuple-element.46.refs_1_, bf16[512,512]{1,0:T(8,128)(2,1)S(1)} %get-tuple-element.47.refs_2_.refs_4_, bf16[512,512]{1,0:T(8,128)(2,1)S(1)} %get-tuple-element.48.refs_3_.refs_5_, ...), custom_call_target="tpu_custom_call" | custom-call | flops 1000000000 | bytes 1048576 | tf_op jit(solution)/shard_map/structure/pallas_call | solution.py:668
  29.1 0.4 %collective-permute-start.6 = (f32[512,128]{1,0:T(8,128)S(1)}, f32[512,128]{1,0:T(8,128)S(1)}, u32[]{:S(2)}, u32[]{:S(2)}) collective-permute-start(f32[512,128]{1,0:T(8,128)S(1)} %structure.2.cos_own), channel_id=1, source_target_pairs={{0,1},{1,0},{2,3},{3,2},{4,5},{5,4},{6,7},{7,6},{8,9},{9,8},{10,11... | collective-permute-start | bytes 786440 | tf_op jit(solution)/shard_map/ppermute | solution.py:654
  29.5 0.0 copy-start
  29.5 0.0 copy-start.2
  29.6 0.0 copy-start.5
  29.6 1.1 %near.1 = (bf16[512,768]{1,0:T(8,128)(2,1)S(1)}, bf16[512,768]{1,0:T(8,128)(2,1)S(1)}, bf16[512,768]{1,0:T(8,128)(2,1)S(1)}, bf16[512,768]{1,0:T(8,128)(2,1)S(1)...) custom-call(f32[16,32,128]{2,1,0:T(8,128)S(1)} %constant_dynamic-update-slice_fusion.mine, ...), custom_call_target="tpu_custom_call" | custom-call | flops 100000000 | bytes 1048576 | tf_op jit(solution)/shard_map/near/pallas_call | solution.py:668
  30.7 0.0 collective-permute-done.7.sin_other
  30.7 0.1 collective-permute-done.6.cos_other
  30.7 0.0 copy-done
  30.7 0.0 copy-done.2
  30.7 0.0 copy-done.5
  30.7 3.8 %backward.1 = (f32[8,128]{1,0:T(8,128)S(1)}, f32[8,128]{1,0:T(8,128)S(1)}, f32[1,128]{1,0:T(1,128)}, bf16[1024,384]{1,0:T(8,128)(2,1)S(1)}) custom-call(f32[512,128]{1,0:T(8,128)S(1)} %structure.2.cos_own, f32[512,128]{1,0:T(8,128)S(1)} %collective-permute-done.6.cos_other, f32[512,128]{1,0:T(8,128)S(1)} %structure.3.sin_own, ...), custom_call_target="tpu_custom_call" | custom-call | flops 100000000 | bytes 1048576 | tf_op jit(solution)/shard_map/backward/pallas_call | solution.py:668
  34.6 0.4 collective-permute-start.8
  34.9 0.0 copy-start.8
  34.9 0.0 copy-start.9
  34.9 0.0 copy-start.10
  34.9 0.0 copy-start.11
  34.9 0.0 copy-start.12
  34.9 0.6 %ewald.1 = f32[8,128]{1,0:T(8,128)S(1)} custom-call(bf16[1024,384]{1,0:T(8,128)(2,1)S(1)} %get-tuple-element.80.weights, bf16[512,768]{1,0:T(8,128)(2,1)S(1)} %get-tuple-element.69.cos_high, bf16[512,768]{1,0:T(8,128)(2,1)S(1)} %get-tuple-element.70.cos_low, bf16[512,768]{1,0:T(8,128)(2,1)S(1)} %get-tuple-element.71.sin_high, ...), custom_call_target="tpu_custom_call" | custom-call | flops 4000000000 | bytes 1048576 | tf_op jit(solution)/shard_map/ewald/pallas_call | solution.py:668
  35.5 0.2 collective-permute-done.8.other
  35.7 0.0 copy-done.8
  35.7 0.0 copy-done.9
  35.7 0.0 copy-done.10
  35.7 0.0 copy-done.11
  35.7 0.0 copy-done.12
  35.8 1.1 %final.1 = (f32[3,128]{1,0:T(4,128)}, f32[3,128]{1,0:T(4,128)}, f32[3,128]{1,0:T(4,128)}) custom-call(f32[3,128]{1,0:T(4,128)S(1)} %copy-done.8, f32[3,128]{1,0:T(4,128)S(1)} %copy-done.9, f32[3,128]{1,0:T(4,128)S(1)} %copy-done.10, s32[1,128]{1,0:T(1,128)S(1)} %bitcast.7, f32[4]{0:T(128)S(1)} %copy-done.12, f32[8,128]{1,0:T(8,128)S(1)} %get-tuple-element.79.own, ...), custom_call_target="tpu_custom_call" | custom-call | flops 100000000 | bytes 1048576 | tf_op jit(solution)/shard_map/final/pallas_call | solution.py:668
  (10 shorter events, 0.1 us)
Async XLA Ops:
  2.8 5.0 %collective-permute-start = (f32[32,128]{1,0:T(8,128)}, f32[32,128]{1,0:T(8,128)S(1)}, u32[]{:S(2)}, u32[]{:S(2)}) collective-permute-start(f32[32,128]{1,0:T(8,128)} %pack.1.block), channel_id=1, source_target_pairs={{0,8},{8,0},{16,24},{24,16},{1,9},{9,1},{17,25},{25,17},{2,10},{10... | collective-permute-start | bytes 49160 | tf_op jit(solution)/shard_map/ppermute | solution.py:654
  5.8 0.8 %copy-start.7 = (f32[32,128]{1,0:T(8,128)S(1)}, f32[32,128]{1,0:T(8,128)}, u32[]{:S(2)}) copy-start(f32[32,128]{1,0:T(8,128)} %pack.1.block) | copy-start | bytes 49156
  7.7 3.0 %copy-start.13 = (f32[2,32,128]{2,1,0:T(8,128)}, f32[2,32,128]{2,1,0:T(8,128)S(1)}, u32[]{:S(2)}) copy-start(f32[2,32,128]{2,1,0:T(8,128)S(1)} %pad_maximum_fusion.1.step) | copy-start | bytes 98308
  7.7 5.2 %collective-permute-start.1 = (f32[2,32,128]{2,1,0:T(8,128)S(1)}, f32[2,32,128]{2,1,0:T(8,128)S(1)}, u32[]{:S(2)}, u32[]{:S(2)}) collective-permute-start(f32[2,32,128]{2,1,0:T(8,128)S(1)} %pad_maximum_fusion.1.step), channel_id=1, source_target_pairs={{0,16},{8,24},{16,0},{24,8},{1,17},{9,25},{17,1},{25,9},{2,18},{10... | collective-permute-start | bytes 98312 | tf_op jit(solution)/shard_map/ppermute | solution.py:654
  12.9 5.2 %collective-permute-start.2 = (f32[4,32,128]{2,1,0:T(8,128)S(1)}, f32[4,32,128]{2,1,0:T(8,128)S(1)}, u32[]{:S(2)}, u32[]{:S(2)}) collective-permute-start(f32[4,32,128]{2,1,0:T(8,128)S(1)} %pad_maximum_fusion.data), channel_id=1, source_target_pairs={{0,6},{1,7},{2,4},{3,5},{4,2},{5,3},{6,0},{7,1},{8,14},{9,15},{10,... | collective-permute-start | bytes 196616 | tf_op jit(solution)/shard_map/ppermute | solution.py:654
  15.5 4.3 %collective-permute-start.3 = (f32[4,32,128]{2,1,0:T(8,128)S(1)}, f32[4,32,128]{2,1,0:T(8,128)S(1)}, u32[]{:S(2)}, u32[]{:S(2)}) collective-permute-start(f32[4,32,128]{2,1,0:T(8,128)S(1)} %pad_maximum_fusion.data), channel_id=1, source_target_pairs={{0,2},{1,3},{2,0},{3,1},{4,6},{5,7},{6,4},{7,5},{8,10},{9,11},{10,... | collective-permute-start | bytes 196616 | tf_op jit(solution)/shard_map/ppermute | solution.py:654
  16.0 4.4 %collective-permute-start.4 = (f32[4,32,128]{2,1,0:T(8,128)S(1)}, f32[4,32,128]{2,1,0:T(8,128)S(1)}, u32[]{:S(2)}, u32[]{:S(2)}) collective-permute-start(f32[4,32,128]{2,1,0:T(8,128)S(1)} %pad_maximum_fusion.data), channel_id=1, source_target_pairs={{0,4},{1,5},{2,6},{3,7},{4,0},{5,1},{6,2},{7,3},{8,12},{9,13},{10,... | collective-permute-start | bytes 196616 | tf_op jit(solution)/shard_map/ppermute | solution.py:654
  20.5 1.4 %copy-start.1 = (bf16[256,384]{1,0:T(8,128)(2,1)S(1)}, bf16[256,384]{1,0:T(8,128)(2,1)}, u32[]{:S(2)}) copy-start(bf16[256,384]{1,0:T(8,128)(2,1)} %get-tuple-element.56.wcu3) | copy-start | bytes 589828
  20.5 1.4 %copy-start.3 = (bf16[128,240]{1,0:T(8,128)(2,1)S(1)}, bf16[128,240]{1,0:T(8,128)(2,1)}, u32[]{:S(2)}) copy-start(bf16[128,240]{1,0:T(8,128)(2,1)} %get-tuple-element.55.rex3) | copy-start | bytes 184324
  20.5 1.4 %copy-start.4 = (f32[128,128]{1,0:T(8,128)S(1)}, f32[128,128]{1,0:T(8,128)}, u32[]{:S(2)}) copy-start(f32[128,128]{1,0:T(8,128)} %get-tuple-element.57.rv_ref) | copy-start | bytes 196612
  20.5 1.3 %copy-start.6 = (f32[16,128]{1,0:T(8,128)S(1)}, f32[16,128]{1,0:T(8,128)}, u32[]{:S(2)}) copy-start(f32[16,128]{1,0:T(8,128)} %radial.3) | copy-start | bytes 24580
  20.5 1.3 %collective-permute-start.5 = (f32[16,8,128]{2,1,0:T(8,128)S(1)}, f32[16,8,128]{2,1,0:T(8,128)S(1)}, u32[]{:S(2)}, u32[]{:S(2)}) collective-permute-start(f32[16,8,128]{2,1,0:T(8,128)S(1)} %fusion), channel_id=1, source_target_pairs={{0,1},{1,0},{2,3},{3,2},{4,5},{5,4},{6,7},{7,6},{8,9},{9,8},{10,11... | collective-permute-start | bytes 196616 | tf_op jit(solution)/shard_map/ppermute | solution.py:654
  27.6 3.0 %collective-permute-start.7 = (f32[512,128]{1,0:T(8,128)S(1)}, f32[512,128]{1,0:T(8,128)S(1)}, u32[]{:S(2)}, u32[]{:S(2)}) collective-permute-start(f32[512,128]{1,0:T(8,128)S(1)} %structure.3.sin_own), channel_id=1, source_target_pairs={{0,1},{1,0},{2,3},{3,2},{4,5},{5,4},{6,7},{7,6},{8,9},{9,8},{10,11... | collective-permute-start | bytes 786440 | tf_op jit(solution)/shard_map/ppermute | solution.py:654
  29.1 1.6 %collective-permute-start.6 = (f32[512,128]{1,0:T(8,128)S(1)}, f32[512,128]{1,0:T(8,128)S(1)}, u32[]{:S(2)}, u32[]{:S(2)}) collective-permute-start(f32[512,128]{1,0:T(8,128)S(1)} %structure.2.cos_own), channel_id=1, source_target_pairs={{0,1},{1,0},{2,3},{3,2},{4,5},{5,4},{6,7},{7,6},{8,9},{9,8},{10,11... | collective-permute-start | bytes 786440 | tf_op jit(solution)/shard_map/ppermute | solution.py:654
  29.5 1.2 %copy-start = (f32[512,128]{1,0:T(8,128)S(1)}, f32[512,128]{1,0:T(8,128)}, u32[]{:S(2)}) copy-start(f32[512,128]{1,0:T(8,128)} %kernel_filter.1) | copy-start | bytes 786436
  29.5 1.2 %copy-start.2 = (bf16[128,768]{1,0:T(8,128)(2,1)S(1)}, bf16[128,768]{1,0:T(8,128)(2,1)}, u32[]{:S(2)}) copy-start(bf16[128,768]{1,0:T(8,128)(2,1)} %get-tuple-element.75.wb3) | copy-start | bytes 589828
  29.6 1.2 %copy-start.5 = (bf16[64,384]{1,0:T(8,128)(2,1)S(1)}, bf16[64,384]{1,0:T(8,128)(2,1)}, u32[]{:S(2)}) copy-start(bf16[64,384]{1,0:T(8,128)(2,1)} %get-tuple-element.76.re3) | copy-start | bytes 147460
  34.6 1.2 %collective-permute-start.8 = (f32[8,128]{1,0:T(8,128)S(1)}, f32[8,128]{1,0:T(8,128)S(1)}, u32[]{:S(2)}, u32[]{:S(2)}) collective-permute-start(f32[8,128]{1,0:T(8,128)S(1)} %get-tuple-element.81), channel_id=1, source_target_pairs={{0,1},{1,0},{2,3},{3,2},{4,5},{5,4},{6,7},{7,6},{8,9},{9,8},{10,11... | collective-permute-start | bytes 12296 | tf_op jit(solution)/shard_map/ppermute | solution.py:654
  34.9 0.8 %copy-start.8 = (f32[3,128]{1,0:T(4,128)S(1)}, f32[3,128]{1,0:T(4,128)}, u32[]{:S(2)}) copy-start(f32[3,128]{1,0:T(4,128)} %pos.3) | copy-start | bytes 4612
  34.9 0.8 %copy-start.9 = (f32[3,128]{1,0:T(4,128)S(1)}, f32[3,128]{1,0:T(4,128)}, u32[]{:S(2)}) copy-start(f32[3,128]{1,0:T(4,128)} %vel.3) | copy-start | bytes 4612
  34.9 0.8 %copy-start.10 = (f32[3,128]{1,0:T(4,128)S(1)}, f32[3,128]{1,0:T(4,128)}, u32[]{:S(2)}) copy-start(f32[3,128]{1,0:T(4,128)} %frc.3) | copy-start | bytes 4612
  34.9 0.8 %copy-start.11 = (s32[128]{0:T(128)S(1)}, s32[128]{0:T(128)}, u32[]{:S(2)}) copy-start(s32[128]{0:T(128)} %param.20) | copy-start | bytes 1540
  34.9 0.8 %copy-start.12 = (f32[4]{0:T(128)S(1)}, f32[4]{0:T(128)}, u32[]{:S(2)}) copy-start(f32[4]{0:T(128)} %mass.3) | copy-start | bytes 52

commit v5 on v4

--- a/solution.py
+++ b/solution.py
@@ -68,7 +68,7 @@
 
 
 def sigmoid(x):
-    return 1.0 / (1.0 + jnp.exp(-x))
+    return 0.5 + 0.5 * jnp.tanh(0.5 * x)
 
 
 def cos_sin(turns):
@@ -166,8 +166,8 @@
 
 def mass_of(kind, mass):
     factor = jnp.zeros(kind.shape, f32)
-    for s in range(mass.shape[0]):
-        factor = factor + jnp.where(kind == s, mass[s], 0.0)
+    for s in range(mass.shape[1]):
+        factor = factor + jnp.where(kind == s, mass[0:1, s : s + 1], 0.0)
     return factor
 
 
@@ -179,7 +179,7 @@
     half_velocity = vel[...] + 0.5 * time_step * frc[...] * mass_of(kind, mass)
     moved = pos[...] + time_step * half_velocity
     lane = lanes((1, own))
-    code = jnp.where(lane < cnt[0], kind, -1).astype(f32)
+    code = jnp.where(lane < cnt[...], kind, -1).astype(f32)
     number = ((layer * strips + strip) * own + lane).astype(f32)
     out[0:3, :] = moved
     out[ROW_KIND : ROW_KIND + 1, :] = code
@@ -196,29 +196,46 @@
     out[ROW_LISTS:, :] = nbr[...].astype(f32)
 
 
+def mixed_table(embedding, radial, mix):
+    mixed = jnp.dot(embedding[...], mix[...], precision=highest, preferred_element_type=f32)
+    kinds = embedding.shape[0]
+    return jnp.concatenate([mixed[s : s + 1] * radial[...] for s in range(kinds)], axis=0)
+
+
 def weights_kernel(
-    embedding, radial, mix, self_w, charge_w, readout_w, readout_v, step, rex3, wcu3, wb3, re3, rv_out
+    embedding,
+    radial,
+    mix,
+    self_w,
+    charge_w,
+    readout_w,
+    readout_v,
+    ahead,
+    rex3,
+    wcu3,
+    wb3,
+    re3,
+    rv_out,
 ):
     kinds, channels = embedding.shape
-    basis = radial.shape[0]
-    emb = embedding[...]
-    mixed = jnp.dot(emb, mix[...], precision=highest, preferred_element_type=f32)
-    selfed = jnp.dot(emb, self_w[...], precision=highest, preferred_element_type=f32)
-    table = jnp.concatenate([mixed[s : s + 1] * radial[...] for s in range(kinds)], axis=0)
-    re3[...] = left3(table)
-    rest = jnp.zeros((channels - kinds * basis - kinds, channels), f32)
+    table = mixed_table(embedding, radial, mix)
+    selfed = jnp.dot(embedding[...], self_w[...], precision=highest, preferred_element_type=f32)
+    rest = jnp.zeros((channels - table.shape[0] - kinds, channels), f32)
     wide = jnp.concatenate([table, selfed, rest], axis=0).T
     rex3[...] = left3(wide[:, : rex3.shape[1] // 3])
     wcu3[...] = left3(jnp.concatenate([charge_w[...].T, readout_w[...].T], axis=0))
     wb3[...] = left3(jnp.concatenate([charge_w[...], readout_w[...]], axis=1))
+    re3[...] = left3(table)
     rv_out[...] = jnp.broadcast_to(readout_v[...], (channels, channels)).T
 
 
-def lift_kernel(block, out):
+def lift_kernel(all_atoms, block, kernel_filter, out, filter_out):
     out[0] = block[...]
-
-
-def tables_kernel(sizes, data, *refs):
+    keeper = jnp.where(rows(kernel_filter.shape) == zero_row, 0.0, 1.0 / all_atoms)
+    filter_out[...] = keeper * kernel_filter[...]
+
+
+def tables_kernel(sizes, data, ahead, *refs):
     own = data.shape[2]
     refs[4][...] = jnp.zeros_like(refs[4])
     refs = refs[:4]
@@ -238,6 +255,7 @@
     sizes,
     dims,
     group,
+    block,
     near_layers,
     early,
     mine,
@@ -288,7 +306,9 @@
             first_step(n * group + k)
         return carry
 
-    lax.fori_loop(0, total // group, first_steps, 0)
+    local_first = group % layers == 0
+    if not local_first:
+        lax.fori_loop(0, total // group, first_steps, 0)
 
     bound = jnp.where((row8 == ROW_KIND) | (row8 == ROW_ID), -1.0, 0.0)
     padding = jnp.where(row8 < 3, far_away, -1.0)
@@ -357,43 +377,49 @@
         one_hot = jnp.where(rows((tail, own)).astype(f32) == kind_row, 1.0, 0.0)
         x_ref[:, k * own : (k + 1) * own] = right3(jnp.concatenate(sums + [one_hot], axis=0))
 
-    def group_step(n, place):
-        start = n * group
-        found = [geometry(start + k, k) for k in range(group)]
-        for k in range(group):
-            basis_sums(k, found[k][0])
+    def block_step(start, place, offset):
+        found = [geometry(start + k, offset + k) for k in range(block)]
+        for k in range(block):
+            basis_sums(offset + k, found[k][0])
         live = jnp.concatenate([kind_row for kind_row, _ in found], axis=1) >= 0.0
-        pre = mm(rex3[...], x_ref[...])
+        pre = mm(rex3[...], x_ref[:, offset * own : (offset + block) * own])
         gate = sigmoid(pre)
         hidden = pre * gate
         both = mm(wcu3[...], right3(hidden))
         charges = jnp.where(live, both[:channels], 0.0)
         readout = both[channels:]
         readout_gate = sigmoid(readout)
-        rv = jnp.concatenate([rv_ref[...]] * group, axis=1)
+        rv = jnp.concatenate([rv_ref[...]] * block, axis=1)
         scaled = jnp.where(live, rv * readout_gate, 0.0)
         local = scaled * readout
         slope = gate * (1.0 + pre * (1.0 - gate))
         back = scaled * (1.0 + readout * (1.0 - readout_gate))
-        wide = jnp.sum(local.reshape(channels // 8, 8, group * own), axis=0)
-        for k in range(group):
+        wide = jnp.sum(local.reshape(channels // 8, 8, block * own), axis=0)
+        for k in range(block):
             energy_ref[...] += wide[:, k * own : (k + 1) * own]
         column = pl.multiple_of(place * own, own)
         high, low = split(charges)
-        q_out[0:channels, pl.ds(column, group * own)] = high
-        q_out[channels : 2 * channels, pl.ds(column, group * own)] = low
-        for k in range(group):
+        q_out[0:channels, pl.ds(column, block * own)] = high
+        q_out[channels : 2 * channels, pl.ds(column, block * own)] = low
+        for k in range(block):
             column = pl.multiple_of(found[k][1] * own, own)
             slope_out[:, pl.ds(column, own)] = slope[:, k * own : (k + 1) * own]
             readout_out[:, pl.ds(column, own)] = back[:, k * own : (k + 1) * own]
 
+    def group_step(n, place):
+        if local_first:
+            for k in range(group):
+                first_step(n * group + k)
+        for offset in range(0, group, block):
+            block_step(n * group + offset, place + offset, offset)
+
     if early:
 
         def steps(n, carry):
             group_step(n, n * group)
             return carry
 
-        lax.fori_loop(0, total // group, steps, 0)
+        lax.fori_loop(0, total // group, steps, 0, unroll=total == group)
     else:
         chunk = q_out.shape[1] // own
 
@@ -452,14 +478,12 @@
         out[zero_row : zero_row + 1, :] = energy[...]
 
 
-def near_kernel(sizes, near_layers, basis, kinds, starts, mine, pairs, *refs):
+def near_kernel(sizes, near_layers, side, starts, mine, *refs):
     layers, strips = sizes
-    *tables, cos_high, cos_low, sin_high, sin_low, live_out, fall_out = refs
+    tables, outs, live_out = refs[: 4 * len(starts)], refs[-5:-1], refs[-1]
     own = mine.shape[2]
     here = position_here()
-    spacing = basis_reach / (basis - 1)
-    outs = (cos_high, cos_low, sin_high, sin_low)
-    for j in range(2 * near_layers):
+    for j in range(side * near_layers, (side + 1) * near_layers):
         at = slice(j * own, (j + 1) * own)
         slot = slot_of(*near_domain(j, here, sizes, near_layers), here, sizes)
         record = mine[slot, 0:8, :]
@@ -469,18 +493,30 @@
             store_phases(record, layers, strips, outs, j * own)
         for n, start in enumerate(starts):
             parts = tables[4 * n : 4 * n + 4]
-            if j < near_layers and n > 0:
-                continue
-            if j >= near_layers and n == 0:
-                continue
             end = start + parts[0].shape[1] // own
 
-            @pl.when((slot >= start) & (slot < end))
-            def _():
+            def take():
                 column = pl.multiple_of((slot - start) * own, own)
                 for part, out in zip(parts, outs):
                     out[:, at] = part[:, pl.ds(column, own)]
 
+            if len(starts) == 1:
+                take()
+            else:
+                pl.when((slot >= start) & (slot < end))(take)
+
+
+def column_kernel(sizes, near_layers, data, *refs):
+    tables, outs = refs[:4], refs[4:]
+    for n in range(data.shape[0]):
+        store_phases(data[n, 0:8, :], *sizes, tables, n * data.shape[2])
+    near_kernel(sizes, near_layers, 0, [0], data, *tables, *outs)
+
+
+def fall_kernel(pairs, fall_out):
+    domains, basis = fall_out.shape[0:2]
+    spacing = basis_reach / (basis - 1)
+    for j in range(domains):
         d = pairs[j, 5]
         quarter = d * (1.0 / envelope_reach)
         square = quarter * quarter
@@ -494,6 +530,24 @@
             fall_out[j, b] = e * (lean * t + slope)
 
 
+def wave_weights(part, other, scale):
+    sums = part[...] + other[...]
+    return sums, scale[...] * sums
+
+
+def charge_gradient(weight, high, low):
+    channels = weight.shape[1]
+    top, bottom = split(weight.T)
+    wide = mm(jnp.concatenate([top, bottom], axis=0), high[...])
+    return wide[:channels] + wide[channels:] + mm(top, low[...])
+
+
+def pull_kernel(part, other, scale, high, low, grad_out, energy_out):
+    sums, weight = wave_weights(part, other, scale)
+    grad_out[...] = charge_gradient(weight, high, low)
+    energy_out[...] = jnp.sum(weight * sums, axis=0, keepdims=True)
+
+
 def backward_kernel(
     sizes,
     dims,
@@ -501,13 +555,11 @@
     near_layers,
     cos_own,
     cos_other,
-    sin_own,
-    sin_other,
-    kernel_filter,
+    grad_in,
+    sin_energy,
+    scale,
     cos_high,
     cos_low,
-    sin_high,
-    sin_low,
     live_in,
     fall_in,
     wb3,
@@ -518,7 +570,6 @@
     own_out,
     other_out,
     energy_out,
-    weight_ref,
     b_ref,
     f_ref,
     t_ref,
@@ -530,40 +581,29 @@
     layer, strip = position_here()
     basis = fall_in.shape[1]
     channels = slope_in.shape[0]
-    waves = KGRID**3
     domains = 2 * near_layers
     lanes_all = domains * own
-
-    cos_sum = cos_own[...] + cos_other[...]
-    sin_sum = sin_own[...] + sin_other[...]
-    local = cos_sum[zero_row : zero_row + 1]
-    keeper = jnp.where(rows((waves, channels)) == zero_row, 0.0, 1.0 / all_atoms)
-    scale = keeper * kernel_filter[...]
-    weight_cos = scale * cos_sum
-    weight_sin = scale * sin_sum
-    ewald = jnp.sum(weight_cos * cos_sum + weight_sin * sin_sum, axis=0, keepdims=True)
-    energy = jnp.sum(local + 0.5 * ewald, axis=1, keepdims=True)
-    energy_out[...] = jnp.broadcast_to(energy / all_atoms, energy_out.shape)
-
-    grad = None
-    for n, (weight, high, low) in enumerate(
-        ((weight_cos, cos_high, cos_low), (weight_sin, sin_high, sin_low))
-    ):
-        top, bottom = split(weight.T)
-        wide = mm(jnp.concatenate([top, bottom], axis=0), high[...])
-        part = wide[:channels] + wide[channels:] + mm(top, low[...])
-        grad = part if grad is None else grad + part
-        weight_ref[n * waves : (n + 1) * waves, :] = left3(weight)
-    grad = grad * live_in[0:1, :]
-    both = jnp.concatenate([grad, readout_in[:, 0:lanes_all]], axis=0)
-    grad = mm(wb3[...], right3(both)) * slope_in[:, 0:lanes_all]
-    b_ref[...] = mm(re3[...], right3(grad))
 
     base = ((layer * strips + (strip - (strip & 1))) * own).astype(f32)
     groups = 8
     size = 2 * own // groups
     group = rows((groups, own))
     member = rows((size, own))
+    for j in range(domains):
+        target = (pair_in[j, 4] - base).astype(i32)
+        t_ref[j, 0] = target // size
+        t_ref[j, 1] = target & (size - 1)
+        for m in range(slots):
+            one = jnp.where(t_ref[j, 1, m : m + 1, :] == member, 1.0, 0.0)
+            col_ref[j, :, m * own : (m + 1) * own] = one.astype(bf16)
+
+    sums, weight = wave_weights(cos_own, cos_other, scale)
+    grad = grad_in[...] + charge_gradient(weight, cos_high, cos_low)
+    grad = grad * live_in[0:1, :]
+    both = jnp.concatenate([grad, readout_in[:, 0:lanes_all]], axis=0)
+    grad = mm(wb3[...], right3(both)) * slope_in[:, 0:lanes_all]
+    b_ref[...] = mm(re3[...], right3(grad))
+
     found = None
     own_out[...] = jnp.zeros_like(own_out)
     for j in range(domains):
@@ -577,9 +617,6 @@
                 row = b_ref[k : k + 1, j * own : (j + 1) * own]
                 chosen = jnp.where(same[s], row, chosen)
             force = force + fall_in[j, b] * chosen
-        target = (pair_in[j, 4] - base).astype(i32)
-        t_ref[j, 0] = target // size
-        t_ref[j, 1] = target & (size - 1)
         for r in range(3):
             part = force * pair_in[j, r]
             high = part.astype(bf16).astype(f32)
@@ -596,8 +633,6 @@
                 ]
                 here = slice(2 * r * groups, 2 * (r + 1) * groups)
                 hot_ref[j, here, at] = jnp.concatenate(hot, axis=0).astype(bf16)
-            one = jnp.where(t_ref[j, 1, m : m + 1, :] == member, 1.0, 0.0)
-            col_ref[j, :, at] = one.astype(bf16)
         more = mm_nt(hot_ref[j], col_ref[j])
         found = more if found is None else found + more
 
@@ -617,8 +652,26 @@
         own_out[r : r + 1, :] += jnp.where(odd, sides[1], sides[0])
         other_out[r : r + 1, :] = jnp.where(odd, sides[0], sides[1])
 
-
-def ewald_kernel(sizes, weights, cos_high, cos_low, sin_high, sin_low, q_in, out):
+    local = sums[zero_row : zero_row + 1]
+    ewald = sin_energy[...] + jnp.sum(weight * sums, axis=0, keepdims=True)
+    energy = jnp.sum(local + 0.5 * ewald, axis=1, keepdims=True)
+    energy_out[...] = jnp.broadcast_to(energy / all_atoms, energy_out.shape)
+
+
+def ewald_kernel(
+    sizes,
+    cos_own,
+    cos_other,
+    sin_own,
+    sin_other,
+    scale,
+    cos_high,
+    cos_low,
+    sin_high,
+    sin_low,
+    q_in,
+    out,
+):
     layers, strips = sizes
     channels = q_in.shape[0] // 2
     waves = cos_high.shape[0]
@@ -626,10 +679,15 @@
     mine = slice(own, 2 * own)
     charge_high = q_in[0:channels, 0:own]
     charge_low = q_in[channels : 2 * channels, 0:own]
-    along = mm(weights[...], jnp.concatenate([charge_high, charge_low, charge_high], axis=0))
+    charges = jnp.concatenate([charge_high, charge_low, charge_high], axis=0)
+    halves = ((cos_own, cos_other), (sin_own, sin_other))
+    along_cos, along_sin = [
+        mm(left3(wave_weights(part, other, scale)[1]), charges)
+        for part, other in halves
+    ]
     cosine = cos_high[:, mine].astype(f32) + cos_low[:, mine].astype(f32)
     sine = sin_high[:, mine].astype(f32) + sin_low[:, mine].astype(f32)
-    turn = cosine * along[waves:] - sine * along[:waves]
+    turn = cosine * along_sin - sine * along_cos
     index = lanes((8, waves))
     axis = rows((8, waves))
     part_x = (index // (KGRID * KGRID)).astype(f32) / (strips * width_x)
@@ -656,23 +714,20 @@
 
 MIB = 1024 * 1024
 vmem = pl.BlockSpec(memory_space=pltpu.VMEM)
-smem = pl.BlockSpec(memory_space=pltpu.SMEM)
-
-
-def call(kernel, name, outs, ins, scratch=(), limit=8, scalars=(), unread=(), work=10**8):
-    def spec(n):
-        if n in unread:
-            return pl.BlockSpec(memory_space=pl.ANY)
-        return smem if n in scalars else vmem
+
+
+def call(kernel, name, outs, ins, scratch=(), unread=(), alias={}, limit=8, work=10**8):
+    anywhere = pl.BlockSpec(memory_space=pl.ANY)
 
     return pl.pallas_call(
         kernel,
         out_shape=[jax.ShapeDtypeStruct(shape, dtype) for shape, dtype in outs],
-        in_specs=[spec(n) for n in range(len(ins))],
+        in_specs=[anywhere if n in unread else vmem for n in range(len(ins))],
         out_specs=[vmem] * len(outs),
         scratch_shapes=[pltpu.VMEM(shape, dtype) for shape, dtype in scratch],
         compiler_params=pltpu.CompilerParams(vmem_limit_bytes=limit and limit * MIB),
         cost_estimate=pl.CostEstimate(flops=work, bytes_accessed=MIB, transcendentals=0),
+        input_output_aliases=alias,
         name=name,
     )(*ins)
 
@@ -709,7 +764,8 @@
     kind_row = species[None, :]
     total = layers * (strips // 2)
     early = total <= 16
-    group = min(8, total)
+    group = min(16, total)
+    block_size = min(4, group)
     near_layers = min(3, layers)
     near = 2 * near_layers
     depth = kinds * basis + -(-kinds // 16) * 16
@@ -719,8 +775,8 @@
         "pack",
         [((ROW_LISTS + slots, own), f32)],
         (
-            counts,
-            inverse_mass,
+            counts[None],
+            inverse_mass[None],
             positions,
             velocities,
             forces,
@@ -729,22 +785,40 @@
             send_inplane,
             send_normal,
         ),
-        scalars=(0, 1),
         limit=None,
     )
-    def phases(data):
+    def near_part(side, data, tables, starts, given=()):
+        parts = [t for table in tables for t in table]
+        return call(
+            functools.partial(near_kernel, sizes, near_layers, side, starts),
+            "near",
+            [((waves, near * own), bf16)] * 4 + [((8, near * own), f32)],
+            (data, *parts, *given),
+            unread=range(1 + len(parts), 1 + len(parts) + len(given)),
+            alias={1 + len(parts) + n: n for n in range(len(given))},
+            limit=8 if early else 32,
+            work=4 * 10**9,
+        )
+
+    def phases(data, ahead):
         wide = data.shape[0] * own
         return call(
             functools.partial(tables_kernel, sizes),
             "tables",
             [((waves, wide), bf16)] * 4 + [((8, own), f32)],
-            (data,),
+            (data, ahead),
+            unread=(1,),
             work=4 * 10**9,
         )
 
     arrived = exchange(block, "gz", 1)[None]
-    (data,) = call(
-        lift_kernel, "lift", [((1, *block.shape), f32)], (block,), limit=1, work=8 * 10**9
+    data, scale = call(
+        functools.partial(lift_kernel, all_atoms),
+        "lift",
+        [((1, *block.shape), f32), (kernel_filter.shape, f32)],
+        (block, kernel_filter),
+        limit=1,
+        work=8 * 10**9,
     )
     data = jnp.concatenate([data, arrived], axis=0)
     rex3, wcu3, wb3, re3, rv = call(
@@ -771,23 +845,33 @@
         unread=(7,),
         work=4 * 10**9,
     )
-
     bit = 2
     while bit < layers:
         data = jnp.concatenate([data, exchange(data, "gz", bit)], axis=0)
         bit *= 2
     tables, starts, zeros = [], [], []
     if early:
-        *table, zero = phases(data)
-        tables.append(table)
+        *both, zero = call(
+            functools.partial(column_kernel, sizes, near_layers),
+            "column",
+            [((waves, layers * own), bf16)] * 4
+            + [((waves, near * own), bf16)] * 4
+            + [((8, near * own), f32)],
+            (data,),
+            work=4 * 10**9,
+        )
+        tables.append(both[:4])
         starts.append(0)
+        near_tables = [*both[4:], zero]
+    else:
+        near_tables = near_part(0, data, tables, starts)
     bit = 2
     while bit < strips:
         bits = [3 * bit, bit, 2 * bit] if 2 * bit < strips else [bit]
         parts = [exchange(data, "xy", n) for n in bits]
         for n, part in enumerate(parts):
             if early:
-                *table, zero = phases(part)
+                *table, zero = phases(part, near_tables[4] if n == 0 else block)
                 zeros.append(zero)
                 tables.append(table)
                 starts.append((n + 1) * data.shape[0])
@@ -798,6 +882,7 @@
         records = records + zero
     theirs = exchange(records, "xy", 1)
 
+    *near_tables, live = near_part(1, data, tables[1:3], starts[1:3], near_tables)
     chunk = min(16, total)
     outs = [
         ((2 * channels, chunk * own), bf16),
@@ -817,7 +902,7 @@
         outs += [((waves, channels), f32)] * 2
         scratch += [((waves, chunk * own), bf16)] * 4
     q, energy_row, pairs, slope, readout, *sums = call(
-        functools.partial(forward_kernel, sizes, dims, group, near_layers, early),
+        functools.partial(forward_kernel, sizes, dims, group, block_size, near_layers, early),
         "forward",
         outs,
         (data, theirs, rex3, wcu3, rv, radial_weight),
@@ -835,31 +920,31 @@
             work=10**9,
         )
     others = [exchange(part, "xy", 1) for part in sums]
-    near_parts = call(
-        functools.partial(near_kernel, sizes, near_layers, basis, kinds, starts),
-        "near",
-        [((waves, near * own), bf16)] * 4
-        + [((8, near * own), f32), ((near, basis, slots, own), f32)],
-        (data, pairs, *[t for table in tables for t in table]),
-        limit=8 if early else 32,
+    (fall,) = call(
+        fall_kernel, "fall", [((near, basis, slots, own), f32)], (pairs,), work=10**9
+    )
+    grad, sin_energy = call(
+        pull_kernel,
+        "pull",
+        [((channels, near * own), f32), ((1, channels), f32)],
+        (sums[1], others[1], scale, *near_tables[2:]),
+        limit=16,
+        work=10**9,
     )
     groups = 8
-    own_grad, other_grad, energy, weights3 = call(
+    own_grad, other_grad, energy = call(
         functools.partial(backward_kernel, sizes, dims, all_atoms, near_layers),
         "backward",
-        [
-            ((8, own), f32),
-            ((8, own), f32),
-            ((1, channels), f32),
-            ((2 * waves, 3 * channels), bf16),
-        ],
+        [((8, own), f32), ((8, own), f32), ((1, channels), f32)],
         (
             sums[0],
             others[0],
-            sums[1],
-            others[1],
-            kernel_filter,
-            *near_parts,
+            grad,
+            sin_energy,
+            scale,
+            *near_tables[:2],
+            live,
+            fall,
             wb3,
             re3,
             pairs,
@@ -880,15 +965,14 @@
         functools.partial(ewald_kernel, sizes),
         "ewald",
         [((8, own), f32)],
-        (weights3, *near_parts[:4], q),
+        (sums[0], others[0], sums[1], others[1], scale, *near_tables, q),
         work=4 * 10**9,
     )
     moved, velocities_new, forces_new = call(
         final_kernel,
         "final",
         [((3, own), f32)] * 3,
-        (positions, velocities, forces, kind_row, inverse_mass, own_grad, ewald_grad, arrived),
-        scalars=(4,),
+        (positions, velocities, forces, kind_row, inverse_mass[None], own_grad, ewald_grad, arrived),
         limit=1,
     )
     return (moved, velocities_new, forces_new, energy[0, 0])

time: 37.2 us -> 36.2 us (0.973)
  local copies, waits for them, and re-layouts: 0.84 us -> 2.08 us
  Pallas kernels: 20 us -> 18.8 us
  waiting for transfers between devices: 3.85 us -> 2.88 us
    unnamed x33 -> x35, local copies, waits for them, and re-layouts: 0.83 us -> 2.08 us
    pallas_call x14 -> x16, Pallas kernels: 20 us -> 18.8 us  [call(): pl.pallas_call(kernel, out_shape=[jax.ShapeDtypeStruct(shape, dtype) for...]
    ppermute x9, waiting for transfers between devices: 3.85 us -> 2.88 us  [exchange(): return lax.ppermute(x, axis, [(i, i ^ bit) for i in range(count)])]
  transfers between devices with their start and end apart: 9 -> 9, of which waited for: 6 -> 5; matrix products, arithmetic and copies ran while one was open for 0% -> 0% of each run, Pallas kernels for 21% -> 23%
where the time goes in v5:
time: 36.2 us; the launch traced here: 35.9 us
  Pallas kernels  18.8 us (52%)
  starting transfers between devices  10.5 us (29%)
  waiting for transfers between devices  2.88 us (8%)
  local copies, waits for them, and re-layouts  2.08 us (6%)
  between operations  1.53 us (4%)
    pallas_call x16, Pallas kernels, call(): pl.pallas_call(kernel, out_shape=[jax.ShapeDtypeStruct(shape, dtype) for...  18.8 us
    ppermute x9, starting transfers between devices, exchange(): return lax.ppermute(x, axis, [(i, i ^ bit) for i in range(count)])  10.5 us
    ppermute x9, waiting for transfers between devices, exchange(): return lax.ppermute(x, axis, [(i, i ^ bit) for i in range(count)])  2.88 us
    unnamed x35, local copies, waits for them, and re-layouts  2.08 us
  transfers between devices with their start and end apart: 9, of which 5 were waited for; matrix products, arithmetic and copies ran while one was open for 0% of the time, Pallas kernels for 23%

profile of v5, /device:TPU:0, one launch (start us, length us, event | category | flops | bytes accessed | tf_op | source)
XLA Modules:
  0.0 35.9 jit_solution(5062944032706029181)
XLA Ops:
  1.3 1.5 %pack.1.block.ahead = f32[32,128]{1,0:T(8,128)} custom-call(s32[1,1]{1,0:T(1,128)} %bitcast.8.cnt, f32[1,4]{1,0:T(1,128)} %bitcast.11, f32[3,128]{1,0:T(4,128)} %pos.3, f32[3,128]{1,0:T(4,128)} %vel.3, f32[3,128]{1,0:T(4,128)} %frc.3, s32[1,128]{1,0:T(1,128)} %bitcast.9, s32[24,128]{1,0:T(8,128)} %nbr.1, s32[2,32]{1,0:T(2,128)} %inplane.1, s32[2,64]{1,0:T(2,128)} %normal.1), custom_call_target="tpu_custom_call" | custom-call | flops 100000000 | bytes 1048576 | tf_op jit(solution)/shard_map/pack/pallas_call | solution.py:722
  2.8 3.0 %collective-permute-start = (f32[32,128]{1,0:T(8,128)}, f32[32,128]{1,0:T(8,128)S(1)}, u32[]{:S(2)}, u32[]{:S(2)}) collective-permute-start(f32[32,128]{1,0:T(8,128)} %pack.1.block.ahead), channel_id=1, source_target_pairs={{0,8},{8,0},{16,24},{24,16},{1,9},{9,1},{17,25},{25,17},{2,10},{10... | collective-permute-start | bytes 49160 | tf_op jit(solution)/shard_map/ppermute | solution.py:712
  5.8 0.0 copy-start.6
  5.8 0.9 %copy-done.6 = f32[512,128]{1,0:T(8,128)S(1)} copy-done((f32[512,128]{1,0:T(8,128)S(1)}, f32[512,128]{1,0:T(8,128)}, u32[]{:S(2)}) %copy-start.6) | copy-done | bytes 262168
  6.7 0.0 copy-start.7
  6.7 0.7 %copy-done.7 = f32[32,128]{1,0:T(8,128)S(1)} copy-done((f32[32,128]{1,0:T(8,128)S(1)}, f32[32,128]{1,0:T(8,128)}, u32[]{:S(2)}) %copy-start.7) | copy-done | bytes 16408
  7.5 0.2 collective-permute-done
  7.7 0.0 copy-start.14
  7.7 3.0 %collective-permute-start.1 = (f32[2,32,128]{2,1,0:T(8,128)S(1)}, f32[2,32,128]{2,1,0:T(8,128)S(1)}, u32[]{:S(2)}, u32[]{:S(2)}) collective-permute-start(f32[2,32,128]{2,1,0:T(8,128)S(1)} %pad_maximum_fusion.1.ahead), channel_id=1, source_target_pairs={{0,16},{8,24},{16,0},{24,8},{1,17},{9,25},{17,1},{25,9},{2,18},{10... | collective-permute-start | bytes 98312 | tf_op jit(solution)/shard_map/ppermute | solution.py:712
  10.7 0.0 copy-done.14
  10.8 2.2 %weights.1 = (bf16[128,240]{1,0:T(8,128)(2,1)}, bf16[256,384]{1,0:T(8,128)(2,1)}, bf16[128,768]{1,0:T(8,128)(2,1)}, bf16[64,384]{1,0:T(8,128)(2,1)}, f32[128,128]{1,0:T(8,128)}) custom-call(f32[4,128]{1,0:T(4,128)} %embedding.1, f32[16,128]{1,0:T(8,128)} %radial.3, f32[128,128]{1,0:T(8,128)} %mix.1, f32[128,128]{1,0:T(8,128)} %self_w.1, ...), custom_call_target="tpu_custom_call" | custom-call | flops 4000000000 | bytes 1048576 | tf_op jit(solution)/shard_map/weights/pallas_call | solution.py:722
  12.9 0.0 collective-permute-done.1
  12.9 2.5 %collective-permute-start.2 = (f32[4,32,128]{2,1,0:T(8,128)S(1)}, f32[4,32,128]{2,1,0:T(8,128)S(1)}, u32[]{:S(2)}, u32[]{:S(2)}) collective-permute-start(f32[4,32,128]{2,1,0:T(8,128)S(1)} %pad_maximum_fusion.data), channel_id=1, source_target_pairs={{0,6},{1,7},{2,4},{3,5},{4,2},{5,3},{6,0},{7,1},{8,14},{9,15},{10,... | collective-permute-start | bytes 196616 | tf_op jit(solution)/shard_map/ppermute | solution.py:712
  15.5 0.5 %collective-permute-start.3 = (f32[4,32,128]{2,1,0:T(8,128)S(1)}, f32[4,32,128]{2,1,0:T(8,128)S(1)}, u32[]{:S(2)}, u32[]{:S(2)}) collective-permute-start(f32[4,32,128]{2,1,0:T(8,128)S(1)} %pad_maximum_fusion.data), channel_id=1, source_target_pairs={{0,2},{1,3},{2,0},{3,1},{4,6},{5,7},{6,4},{7,5},{8,10},{9,11},{10,... | collective-permute-start | bytes 196616 | tf_op jit(solution)/shard_map/ppermute | solution.py:712
  16.0 0.5 %collective-permute-start.4 = (f32[4,32,128]{2,1,0:T(8,128)S(1)}, f32[4,32,128]{2,1,0:T(8,128)S(1)}, u32[]{:S(2)}, u32[]{:S(2)}) collective-permute-start(f32[4,32,128]{2,1,0:T(8,128)S(1)} %pad_maximum_fusion.data), channel_id=1, source_target_pairs={{0,4},{1,5},{2,6},{3,7},{4,0},{5,1},{6,2},{7,3},{8,12},{9,13},{10,... | collective-permute-start | bytes 196616 | tf_op jit(solution)/shard_map/ppermute | solution.py:712
  16.5 0.9 %column.1 = (bf16[512,512]{1,0:T(8,128)(2,1)S(1)}, bf16[512,512]{1,0:T(8,128)(2,1)S(1)}, bf16[512,512]{1,0:T(8,128)(2,1)S(1)}, bf16[512,512]{1,0:T(8,128)(2,1)S(...) custom-call(f32[4,32,128]{2,1,0:T(8,128)S(1)} %pad_maximum_fusion.data), custom_call_target="tpu_custom_call" | custom-call | flops 4000000000 | bytes 1048576 | tf_op jit(solution)/shard_map/column/pallas_call | solution.py:722
  17.5 0.7 %collective-permute-done.2.data = f32[4,32,128]{2,1,0:T(8,128)S(1)} collective-permute-done((f32[4,32,128]{2,1,0:T(8,128)S(1)}, f32[4,32,128]{2,1,0:T(8,128)S(1)}, u32[]{:S(2)}, u32[]{:S(2)}) %collective-permute-start.2) | collective-permute-done | bytes 65568 | tf_op jit(solution)/shard_map/ppermute | solution.py:712
  18.2 0.0 copy-start.8
  18.2 0.7 %tables.3 = (bf16[512,512]{1,0:T(8,128)(2,1)S(1)}, bf16[512,512]{1,0:T(8,128)(2,1)S(1)}, bf16[512,512]{1,0:T(8,128)(2,1)S(1)}, bf16[512,512]{1,0:T(8,128)(2,1)S(1)}, f32[8,128]{1,0:T(8,128)S(1)}) custom-call(f32[4,32,128]{2,1,0:T(8,128)S(1)} %collective-permute-done.2.data, f32[8,768]{1,0:T(8,128)S(1)} %get-tuple-element.55.ahead.refs_12_), custom_call_target="tpu_custom_call" | custom-call | flops 4000000000 | bytes 1048576 | tf_op jit(solution)/shard_map/tables/pallas_call | solution.py:722
  18.9 0.9 %collective-permute-done.3.data = f32[4,32,128]{2,1,0:T(8,128)S(1)} collective-permute-done((f32[4,32,128]{2,1,0:T(8,128)S(1)}, f32[4,32,128]{2,1,0:T(8,128)S(1)}, u32[]{:S(2)}, u32[]{:S(2)}) %collective-permute-start.3) | collective-permute-done | bytes 65568 | tf_op jit(solution)/shard_map/ppermute | solution.py:712
  19.7 0.0 copy-done.8
  19.7 0.7 %tables.4 = (bf16[512,512]{1,0:T(8,128)(2,1)S(1)}, bf16[512,512]{1,0:T(8,128)(2,1)S(1)}, bf16[512,512]{1,0:T(8,128)(2,1)S(1)}, bf16[512,512]{1,0:T(8,128)(2,1)S(1)}, f32[8,128]{1,0:T(8,128)S(1)}) custom-call(f32[4,32,128]{2,1,0:T(8,128)S(1)} %collective-permute-done.3.data, f32[32,128]{1,0:T(8,128)S(1)} %copy-done.8), custom_call_target="tpu_custom_call" | custom-call | flops 4000000000 | bytes 1048576 | tf_op jit(solution)/shard_map/tables/pallas_call | solution.py:722
  20.4 0.0 collective-permute-done.4.data
  20.5 0.0 copy-start.1
  20.5 0.0 copy-start.2
  20.5 0.0 copy-start.3
  20.5 0.0 copy-start.5
  20.5 0.1 collective-permute-start.5
  20.6 0.7 %tables.5 = (bf16[512,512]{1,0:T(8,128)(2,1)S(1)}, bf16[512,512]{1,0:T(8,128)(2,1)S(1)}, bf16[512,512]{1,0:T(8,128)(2,1)S(1)}, bf16[512,512]{1,0:T(8,128)(2,1)S(1)}, f32[8,128]{1,0:T(8,128)}) custom-call(f32[4,32,128]{2,1,0:T(8,128)S(1)} %collective-permute-done.4.data, f32[32,128]{1,0:T(8,128)S(1)} %copy-done.8), custom_call_target="tpu_custom_call" | custom-call | flops 4000000000 | bytes 1048576 | tf_op jit(solution)/shard_map/tables/pallas_call | solution.py:722
  21.3 0.6 %collective-permute-done.5.theirs = f32[16,8,128]{2,1,0:T(8,128)S(1)} collective-permute-done((f32[16,8,128]{2,1,0:T(8,128)S(1)}, f32[16,8,128]{2,1,0:T(8,128)S(1)}, u32[]{:S(2)}, u32[]{:S(2)}) %collective-permute-start.5) | collective-permute-done | bytes 65568 | tf_op jit(solution)/shard_map/ppermute | solution.py:712
  21.8 0.0 copy-done.1
  21.8 0.0 copy-done.2
  21.8 0.0 copy-done.3
  21.8 0.0 copy-done.5
  21.9 4.1 %forward.1 = (bf16[256,2048]{1,0:T(8,128)(2,1)S(1)}, f32[1,128]{1,0:T(1,128)S(1)}, f32[7,6,24,128]{3,2,1,0:T(8,128)S(1)}, f32[128,896]{1,0:T(8,128)S(1)}, f32[128,896]{1,0:T(8,128)S(1)}) custom-call(f32[16,32,128]{2,1,0:T(8,128)S(1)} %constant_dynamic-update-slice_fusion.mine, f32[16,8,128]{2,1,0:T(8,128)S(1)} %collective-permute-done.5.theirs, ...), custom_call_target="tpu_custom_call" | custom-call | flops 100000000 | bytes 1048576 | tf_op jit(solution)/shard_map/forward/pallas_call | solution.py:722
  25.9 1.3 %structure.3.part.sin_own = f32[512,128]{1,0:T(8,128)S(1)} custom-call(bf16[512,512]{1,0:T(8,128)(2,1)S(1)} %get-tuple-element.69.refs_0_, bf16[512,512]{1,0:T(8,128)(2,1)S(1)} %get-tuple-element.70.refs_1_, bf16[512,512]{1,0:T(8,128)(2,1)S(1)} %get-tuple-element.71.refs_2_, bf16[512,512]{1,0:T(8,128)(2,1)S(1)} %get-tuple-element.72.refs_3_, ...), custom_call_target="tpu_custom_call" | custom-call | flops 1000000000 | bytes 1048576 | tf_op jit(solution)/shard_map/structure/pallas_call | solution.py:722
  27.2 0.2 collective-permute-start.7
  27.4 1.3 %structure.2.cos_own = f32[512,128]{1,0:T(8,128)S(1)} custom-call(bf16[512,512]{1,0:T(8,128)(2,1)S(1)} %get-tuple-element.53.refs_0_, bf16[512,512]{1,0:T(8,128)(2,1)S(1)} %get-tuple-element.54.refs_1_, bf16[512,512]{1,0:T(8,128)(2,1)S(1)} %get-tuple-element.56.refs_2_.refs_0_, bf16[512,512]{1,0:T(8,128)(2,1)S(1)} %get-tuple-element.57.refs_3_.refs_1_, ...), custom_call_target="tpu_custom_call" | custom-call | flops 1000000000 | bytes 1048576 | tf_op jit(solution)/shard_map/structure/pallas_call | solution.py:722
  28.7 0.4 %collective-permute-start.6 = (f32[512,128]{1,0:T(8,128)S(1)}, f32[512,128]{1,0:T(8,128)S(1)}, u32[]{:S(2)}, u32[]{:S(2)}) collective-permute-start(f32[512,128]{1,0:T(8,128)S(1)} %structure.2.cos_own), channel_id=1, source_target_pairs={{0,1},{1,0},{2,3},{3,2},{4,5},{5,4},{6,7},{7,6},{8,9},{9,8},{10,11... | collective-permute-start | bytes 786440 | tf_op jit(solution)/shard_map/ppermute | solution.py:712
  29.1 0.5 %near.1 = (bf16[512,768]{1,0:T(8,128)(2,1)S(1)}, bf16[512,768]{1,0:T(8,128)(2,1)S(1)}, bf16[512,768]{1,0:T(8,128)(2,1)S(1)}, bf16[512,768]{1,0:T(8,128)(2,1)S(1)}, f32[8,768]{1,0:T(8,128)S(1)}) custom-call(f32[16,32,128]{2,1,0:T(8,128)S(1)} %constant_dynamic-update-slice_fusion.mine, ...), custom_call_target="tpu_custom_call", output_to_operand_aliasing={{0}: (9, {}), {1}: (10, {}), {2}: (11, {}), {3}: (12, {}), ... | custom-call | flops 4000000000 | bytes 1048576 | tf_op jit(solution)/shard_map/near/pallas_call | solution.py:722
  29.6 0.3 fall.1.fall_in
  29.9 0.0 collective-permute-done.7.other.sin_other
  29.9 0.0 copy-start
  29.9 0.0 copy-start.4
  29.9 0.6 %pull.1 = (f32[128,768]{1,0:T(8,128)S(1)}, f32[1,128]{1,0:T(1,128)S(1)}) custom-call(f32[512,128]{1,0:T(8,128)S(1)} %structure.3.part.sin_own, f32[512,128]{1,0:T(8,128)S(1)} %collective-permute-done.7.other.sin_other, f32[512,128]{1,0:T(8,128)S(1)} %get-tuple-element.77.scale, bf16[512,768]{1,0:T(8,128)(2,1)S(1)} %get-tuple-element.82.high.sin_high, ...), custom_call_target="tpu_custom_call" | custom-call | flops 1000000000 | bytes 1048576 | tf_op jit(solution)/shard_map/pull/pallas_call | solution.py:722
  30.5 0.0 collective-permute-done.6.cos_other
  30.5 0.3 copy-done
  30.8 0.0 copy-done.4
  30.8 3.1 %backward.1 = (f32[8,128]{1,0:T(8,128)S(1)}, f32[8,128]{1,0:T(8,128)S(1)}, f32[1,128]{1,0:T(1,128)}) custom-call(f32[512,128]{1,0:T(8,128)S(1)} %structure.2.cos_own, f32[512,128]{1,0:T(8,128)S(1)} %collective-permute-done.6.cos_other, f32[128,768]{1,0:T(8,128)S(1)} %get-tuple-element.84.grad_in, f32[1,128]{1,0:T(1,128)S(1)} %get-tuple-element.85.sin_energy, ...), custom_call_target="tpu_custom_call" | custom-call | flops 100000000 | bytes 1048576 | tf_op jit(solution)/shard_map/backward/pallas_call | solution.py:722
  33.9 0.0 copy-start.9
  33.9 0.0 copy-start.10
  33.9 0.0 copy-start.11
  33.9 0.0 copy-start.12
  33.9 0.0 copy-start.13
  34.0 0.2 collective-permute-start.8
  34.2 0.5 %ewald.1 = f32[8,128]{1,0:T(8,128)S(1)} custom-call(f32[512,128]{1,0:T(8,128)S(1)} %structure.2.cos_own, f32[512,128]{1,0:T(8,128)S(1)} %collective-permute-done.6.cos_other, f32[512,128]{1,0:T(8,128)S(1)} %structure.3.part.sin_own, f32[512,128]{1,0:T(8,128)S(1)} %collective-permute-done.7.other.sin_other, f32[512,128]{1,0:T(8,128)S(1)} %get-tuple-element.77.scale, ...), custom_call_target="tpu_custom_call" | custom-call | flops 4000000000 | bytes 1048576 | tf_op jit(solution)/shard_map/ewald/pallas_call | solution.py:722
  34.7 0.5 %collective-permute-done.8.other = f32[8,128]{1,0:T(8,128)S(1)} collective-permute-done((f32[8,128]{1,0:T(8,128)S(1)}, f32[8,128]{1,0:T(8,128)S(1)}, u32[]{:S(2)}, u32[]{:S(2)}) %collective-permute-start.8) | collective-permute-done | bytes 4128 | tf_op jit(solution)/shard_map/ppermute | solution.py:712
  35.2 0.0 copy-done.9
  35.2 0.0 copy-done.10
  35.2 0.0 copy-done.11
  35.2 0.0 copy-done.12
  35.2 0.0 copy-done.13
  35.2 0.7 %final.1 = (f32[3,128]{1,0:T(4,128)}, f32[3,128]{1,0:T(4,128)}, f32[3,128]{1,0:T(4,128)}) custom-call(f32[3,128]{1,0:T(4,128)S(1)} %copy-done.9, f32[3,128]{1,0:T(4,128)S(1)} %copy-done.10, f32[3,128]{1,0:T(4,128)S(1)} %copy-done.11, s32[1,128]{1,0:T(1,128)S(1)} %bitcast.10, f32[1,4]{1,0:T(1,128)S(1)} %bitcast.12, f32[8,128]{1,0:T(8,128)S(1)} %get-tuple-element.94.own, ...), custom_call_target="tpu_custom_call" | custom-call | flops 100000000 | bytes 1048576 | tf_op jit(solution)/shard_map/final/pallas_call | solution.py:722
  (10 shorter events, 0.1 us)
Async XLA Ops:
  2.8 5.0 %collective-permute-start = (f32[32,128]{1,0:T(8,128)}, f32[32,128]{1,0:T(8,128)S(1)}, u32[]{:S(2)}, u32[]{:S(2)}) collective-permute-start(f32[32,128]{1,0:T(8,128)} %pack.1.block.ahead), channel_id=1, source_target_pairs={{0,8},{8,0},{16,24},{24,16},{1,9},{9,1},{17,25},{25,17},{2,10},{10... | collective-permute-start | bytes 49160 | tf_op jit(solution)/shard_map/ppermute | solution.py:712
  5.8 0.9 %copy-start.6 = (f32[512,128]{1,0:T(8,128)S(1)}, f32[512,128]{1,0:T(8,128)}, u32[]{:S(2)}) copy-start(f32[512,128]{1,0:T(8,128)} %kernel_filter.1) | copy-start | bytes 786436
  6.7 0.7 %copy-start.7 = (f32[32,128]{1,0:T(8,128)S(1)}, f32[32,128]{1,0:T(8,128)}, u32[]{:S(2)}) copy-start(f32[32,128]{1,0:T(8,128)} %pack.1.block.ahead) | copy-start | bytes 49156
  7.7 3.0 %copy-start.14 = (f32[2,32,128]{2,1,0:T(8,128)}, f32[2,32,128]{2,1,0:T(8,128)S(1)}, u32[]{:S(2)}) copy-start(f32[2,32,128]{2,1,0:T(8,128)S(1)} %pad_maximum_fusion.1.ahead) | copy-start | bytes 98308
  7.7 5.2 %collective-permute-start.1 = (f32[2,32,128]{2,1,0:T(8,128)S(1)}, f32[2,32,128]{2,1,0:T(8,128)S(1)}, u32[]{:S(2)}, u32[]{:S(2)}) collective-permute-start(f32[2,32,128]{2,1,0:T(8,128)S(1)} %pad_maximum_fusion.1.ahead), channel_id=1, source_target_pairs={{0,16},{8,24},{16,0},{24,8},{1,17},{9,25},{17,1},{25,9},{2,18},{10... | collective-permute-start | bytes 98312 | tf_op jit(solution)/shard_map/ppermute | solution.py:712
  12.9 5.2 %collective-permute-start.2 = (f32[4,32,128]{2,1,0:T(8,128)S(1)}, f32[4,32,128]{2,1,0:T(8,128)S(1)}, u32[]{:S(2)}, u32[]{:S(2)}) collective-permute-start(f32[4,32,128]{2,1,0:T(8,128)S(1)} %pad_maximum_fusion.data), channel_id=1, source_target_pairs={{0,6},{1,7},{2,4},{3,5},{4,2},{5,3},{6,0},{7,1},{8,14},{9,15},{10,... | collective-permute-start | bytes 196616 | tf_op jit(solution)/shard_map/ppermute | solution.py:712
  15.5 4.3 %collective-permute-start.3 = (f32[4,32,128]{2,1,0:T(8,128)S(1)}, f32[4,32,128]{2,1,0:T(8,128)S(1)}, u32[]{:S(2)}, u32[]{:S(2)}) collective-permute-start(f32[4,32,128]{2,1,0:T(8,128)S(1)} %pad_maximum_fusion.data), channel_id=1, source_target_pairs={{0,2},{1,3},{2,0},{3,1},{4,6},{5,7},{6,4},{7,5},{8,10},{9,11},{10,... | collective-permute-start | bytes 196616 | tf_op jit(solution)/shard_map/ppermute | solution.py:712
  16.0 4.4 %collective-permute-start.4 = (f32[4,32,128]{2,1,0:T(8,128)S(1)}, f32[4,32,128]{2,1,0:T(8,128)S(1)}, u32[]{:S(2)}, u32[]{:S(2)}) collective-permute-start(f32[4,32,128]{2,1,0:T(8,128)S(1)} %pad_maximum_fusion.data), channel_id=1, source_target_pairs={{0,4},{1,5},{2,6},{3,7},{4,0},{5,1},{6,2},{7,3},{8,12},{9,13},{10,... | collective-permute-start | bytes 196616 | tf_op jit(solution)/shard_map/ppermute | solution.py:712
  18.2 1.6 %copy-start.8 = (f32[32,128]{1,0:T(8,128)S(1)}, f32[32,128]{1,0:T(8,128)}, u32[]{:S(2)}) copy-start(f32[32,128]{1,0:T(8,128)} %pack.1.block.ahead) | copy-start | bytes 49156
  20.5 1.4 %copy-start.1 = (bf16[256,384]{1,0:T(8,128)(2,1)S(1)}, bf16[256,384]{1,0:T(8,128)(2,1)}, u32[]{:S(2)}) copy-start(bf16[256,384]{1,0:T(8,128)(2,1)} %get-tuple-element.65.wcu3) | copy-start | bytes 589828
  20.5 1.4 %copy-start.2 = (bf16[128,240]{1,0:T(8,128)(2,1)S(1)}, bf16[128,240]{1,0:T(8,128)(2,1)}, u32[]{:S(2)}) copy-start(bf16[128,240]{1,0:T(8,128)(2,1)} %get-tuple-element.64.rex3) | copy-start | bytes 184324
  20.5 1.4 %copy-start.3 = (f32[128,128]{1,0:T(8,128)S(1)}, f32[128,128]{1,0:T(8,128)}, u32[]{:S(2)}) copy-start(f32[128,128]{1,0:T(8,128)} %get-tuple-element.66.rv_ref) | copy-start | bytes 196612
  20.5 1.3 %copy-start.5 = (f32[16,128]{1,0:T(8,128)S(1)}, f32[16,128]{1,0:T(8,128)}, u32[]{:S(2)}) copy-start(f32[16,128]{1,0:T(8,128)} %radial.3) | copy-start | bytes 24580
  20.5 1.3 %collective-permute-start.5 = (f32[16,8,128]{2,1,0:T(8,128)S(1)}, f32[16,8,128]{2,1,0:T(8,128)S(1)}, u32[]{:S(2)}, u32[]{:S(2)}) collective-permute-start(f32[16,8,128]{2,1,0:T(8,128)S(1)} %fusion), channel_id=1, source_target_pairs={{0,1},{1,0},{2,3},{3,2},{4,5},{5,4},{6,7},{7,6},{8,9},{9,8},{10,11... | collective-permute-start | bytes 196616 | tf_op jit(solution)/shard_map/ppermute | solution.py:712
  27.2 2.7 %collective-permute-start.7 = (f32[512,128]{1,0:T(8,128)S(1)}, f32[512,128]{1,0:T(8,128)S(1)}, u32[]{:S(2)}, u32[]{:S(2)}) collective-permute-start(f32[512,128]{1,0:T(8,128)S(1)} %structure.3.part.sin_own), channel_id=1, source_target_pairs={{0,1},{1,0},{2,3},{3,2},{4,5},{5,4},{6,7},{7,6},{8,9},{9,8},{10,11... | collective-permute-start | bytes 786440 | tf_op jit(solution)/shard_map/ppermute | solution.py:712
  28.7 1.8 %collective-permute-start.6 = (f32[512,128]{1,0:T(8,128)S(1)}, f32[512,128]{1,0:T(8,128)S(1)}, u32[]{:S(2)}, u32[]{:S(2)}) collective-permute-start(f32[512,128]{1,0:T(8,128)S(1)} %structure.2.cos_own), channel_id=1, source_target_pairs={{0,1},{1,0},{2,3},{3,2},{4,5},{5,4},{6,7},{7,6},{8,9},{9,8},{10,11... | collective-permute-start | bytes 786440 | tf_op jit(solution)/shard_map/ppermute | solution.py:712
  29.9 0.9 %copy-start = (bf16[128,768]{1,0:T(8,128)(2,1)S(1)}, bf16[128,768]{1,0:T(8,128)(2,1)}, u32[]{:S(2)}) copy-start(bf16[128,768]{1,0:T(8,128)(2,1)} %get-tuple-element.90.wb3) | copy-start | bytes 589828
  29.9 0.9 %copy-start.4 = (bf16[64,384]{1,0:T(8,128)(2,1)S(1)}, bf16[64,384]{1,0:T(8,128)(2,1)}, u32[]{:S(2)}) copy-start(bf16[64,384]{1,0:T(8,128)(2,1)} %get-tuple-element.91.re3) | copy-start | bytes 147460
  33.9 1.3 %copy-start.9 = (f32[3,128]{1,0:T(4,128)S(1)}, f32[3,128]{1,0:T(4,128)}, u32[]{:S(2)}) copy-start(f32[3,128]{1,0:T(4,128)} %pos.3) | copy-start | bytes 4612
  33.9 1.3 %copy-start.10 = (f32[3,128]{1,0:T(4,128)S(1)}, f32[3,128]{1,0:T(4,128)}, u32[]{:S(2)}) copy-start(f32[3,128]{1,0:T(4,128)} %vel.3) | copy-start | bytes 4612
  33.9 1.3 %copy-start.11 = (f32[3,128]{1,0:T(4,128)S(1)}, f32[3,128]{1,0:T(4,128)}, u32[]{:S(2)}) copy-start(f32[3,128]{1,0:T(4,128)} %frc.3) | copy-start | bytes 4612
  33.9 1.3 %copy-start.12 = (s32[128]{0:T(128)S(1)}, s32[128]{0:T(128)}, u32[]{:S(2)}) copy-start(s32[128]{0:T(128)} %param.20) | copy-start | bytes 1540
  33.9 1.3 %copy-start.13 = (f32[4]{0:T(128)S(1)}, f32[4]{0:T(128)}, u32[]{:S(2)}) copy-start(f32[4]{0:T(128)} %param.26) | copy-start | bytes 52
  34.0 1.2 %collective-permute-start.8 = (f32[8,128]{1,0:T(8,128)S(1)}, f32[8,128]{1,0:T(8,128)S(1)}, u32[]{:S(2)}, u32[]{:S(2)}) collective-permute-start(f32[8,128]{1,0:T(8,128)S(1)} %get-tuple-element.95), channel_id=1, source_target_pairs={{0,1},{1,0},{2,3},{3,2},{4,5},{5,4},{6,7},{7,6},{8,9},{9,8},{10,11... | collective-permute-start | bytes 12296 | tf_op jit(solution)/shard_map/ppermute | solution.py:712

commit v6 on v5

--- a/solution.py
+++ b/solution.py
@@ -123,33 +123,38 @@
         sin_high[here, at], sin_low[here, at] = split(sine)
 
 
-def by_digits(x, strips, change):
+ORDER_GZ = (0, 2, 3, 1)
+ORDER_XY = (0, 3, 1, 2)
+
+
+def by_digits(x, count, table):
     result, shift = 0, 0
-    while 1 << (shift + 2) < strips:
-        result = result | (change((x >> shift) & 3) << shift)
+    while 1 << (shift + 1) < count:
+        d = (x >> shift) & 3
+        mapped = jnp.where(d == 1, table[1], jnp.where(d == 2, table[2], table[3]))
+        result = result | (jnp.where(d == 0, 0, mapped) << shift)
         shift += 2
     return result | ((x >> shift) << shift)
 
 
-def to_place(d):
-    return jnp.where(d == 0, 0, jnp.where(d == 3, 1, d + 1))
-
-
-def from_place(d):
-    return jnp.where(d == 0, 0, jnp.where(d == 1, 3, d - 1))
+def inverse(order):
+    return tuple(order.index(n) for n in range(4))
 
 
 def domain_at(slot, here, sizes):
     layer, strip = here
     layers, strips = sizes
-    x = by_digits(slot // layers, strips, from_place)
-    return layer ^ (slot & (layers - 1)), strip ^ (2 * x)
+    z = by_digits(slot & (layers - 1), layers, ORDER_GZ)
+    x = by_digits(slot // layers, strips // 2, ORDER_XY)
+    return layer ^ z, strip ^ (2 * x)
 
 
 def slot_of(g, p, here, sizes):
     layer, strip = here
     layers, strips = sizes
-    return (g ^ layer) + layers * by_digits((p ^ strip) >> 1, strips, to_place)
+    z = by_digits(g ^ layer, layers, inverse(ORDER_GZ))
+    x = by_digits((p ^ strip) >> 1, strips // 2, inverse(ORDER_XY))
+    return z + layers * x
 
 
 def near_domain(j, here, sizes, near_layers):
@@ -196,12 +201,6 @@
     out[ROW_LISTS:, :] = nbr[...].astype(f32)
 
 
-def mixed_table(embedding, radial, mix):
-    mixed = jnp.dot(embedding[...], mix[...], precision=highest, preferred_element_type=f32)
-    kinds = embedding.shape[0]
-    return jnp.concatenate([mixed[s : s + 1] * radial[...] for s in range(kinds)], axis=0)
-
-
 def weights_kernel(
     embedding,
     radial,
@@ -218,8 +217,10 @@
     rv_out,
 ):
     kinds, channels = embedding.shape
-    table = mixed_table(embedding, radial, mix)
-    selfed = jnp.dot(embedding[...], self_w[...], precision=highest, preferred_element_type=f32)
+    both = jnp.concatenate([mix[...], self_w[...]], axis=1)
+    both = jnp.dot(embedding[...], both, precision=highest, preferred_element_type=f32)
+    mixed, selfed = both[:, :channels], both[:, channels:]
+    table = jnp.concatenate([mixed[s : s + 1] * radial[...] for s in range(kinds)], axis=0)
     rest = jnp.zeros((channels - table.shape[0] - kinds, channels), f32)
     wide = jnp.concatenate([table, selfed, rest], axis=0).T
     rex3[...] = left3(wide[:, : rex3.shape[1] // 3])
@@ -264,6 +265,8 @@
     wcu3,
     rv_ref,
     radial,
+    later_wb3,
+    later_re3,
     q_out,
     energy_out,
     pair_out,
@@ -811,7 +814,6 @@
             work=4 * 10**9,
         )
 
-    arrived = exchange(block, "gz", 1)[None]
     data, scale = call(
         functools.partial(lift_kernel, all_atoms),
         "lift",
@@ -820,7 +822,6 @@
         limit=1,
         work=8 * 10**9,
     )
-    data = jnp.concatenate([data, arrived], axis=0)
     rex3, wcu3, wb3, re3, rv = call(
         weights_kernel,
         "weights",
@@ -839,16 +840,19 @@
             charge_weight,
             readout_weight,
             readout_vector[None, :],
-            data,
+            block,
         ),
         limit=None,
         unread=(7,),
         work=4 * 10**9,
     )
-    bit = 2
+    bit = 1
     while bit < layers:
-        data = jnp.concatenate([data, exchange(data, "gz", bit)], axis=0)
-        bit *= 2
+        bits = [bit * n for n in ORDER_GZ[1:]] if 2 * bit < layers else [bit]
+        source = block[None] if bit == 1 else data
+        data = jnp.concatenate([data] + [exchange(source, "gz", n) for n in bits], axis=0)
+        bit *= 4
+
     tables, starts, zeros = [], [], []
     if early:
         *both, zero = call(
@@ -858,7 +862,7 @@
             + [((waves, near * own), bf16)] * 4
             + [((8, near * own), f32)],
             (data,),
-            work=4 * 10**9,
+            work=10**9,
         )
         tables.append(both[:4])
         starts.append(0)
@@ -867,7 +871,7 @@
         near_tables = near_part(0, data, tables, starts)
     bit = 2
     while bit < strips:
-        bits = [3 * bit, bit, 2 * bit] if 2 * bit < strips else [bit]
+        bits = [bit * n for n in ORDER_XY[1:]] if 2 * bit < strips else [bit]
         parts = [exchange(data, "xy", n) for n in bits]
         for n, part in enumerate(parts):
             if early:
@@ -905,7 +909,7 @@
         functools.partial(forward_kernel, sizes, dims, group, block_size, near_layers, early),
         "forward",
         outs,
-        (data, theirs, rex3, wcu3, rv, radial_weight),
+        (data, theirs, rex3, wcu3, rv, radial_weight, wb3, re3),
         scratch,
         limit=16 if early else 48,
     )

time: 36.2 us -> 35.6 us (0.983)
  starting transfers between devices: 10.5 us -> 10.1 us
    ppermute x9 -> x10, starting transfers between devices: 10.5 us -> 10.1 us  [exchange(): return lax.ppermute(x, axis, [(i, i ^ bit) for i in range(count)])]
    unnamed x35 -> x34, local copies, waits for them, and re-layouts: 2.08 us -> 1.75 us
    ppermute x9 -> x10, waiting for transfers between devices: 2.88 us -> 2.95 us  [exchange(): return lax.ppermute(x, axis, [(i, i ^ bit) for i in range(count)])]
  transfers between devices with their start and end apart: 9 -> 10, of which waited for: 5 -> 5; matrix products, arithmetic and copies ran while one was open for 0% -> 0% of each run, Pallas kernels for 23% -> 23%
where the time goes in v6:
time: 35.6 us; the launch traced here: 35.3 us
  Pallas kernels  18.9 us (53%)
  starting transfers between devices  10.1 us (28%)
  waiting for transfers between devices  2.95 us (8%)
  local copies, waits for them, and re-layouts  1.76 us (5%)
  between operations  1.54 us (4%)
    pallas_call x16, Pallas kernels, call(): pl.pallas_call(kernel, out_shape=[jax.ShapeDtypeStruct(shape, dtype) for...  18.9 us
    ppermute x10, starting transfers between devices, exchange(): return lax.ppermute(x, axis, [(i, i ^ bit) for i in range(count)])  10.1 us
    ppermute x10, waiting for transfers between devices, exchange(): return lax.ppermute(x, axis, [(i, i ^ bit) for i in range(count)])  2.95 us
    unnamed x34, local copies, waits for them, and re-layouts  1.75 us
  transfers between devices with their start and end apart: 10, of which 5 were waited for; matrix products, arithmetic and copies ran while one was open for 0% of the time, Pallas kernels for 23%

profile of v6, /device:TPU:0, one launch (start us, length us, event | category | flops | bytes accessed | tf_op | source)
XLA Modules:
  0.0 35.3 jit_solution(2102787071898599333)
XLA Ops:
  1.3 1.5 %pack.1.block.ahead = f32[32,128]{1,0:T(8,128)} custom-call(s32[1,1]{1,0:T(1,128)} %bitcast.7.cnt, f32[1,4]{1,0:T(1,128)} %bitcast.13, f32[3,128]{1,0:T(4,128)} %pos.3, f32[3,128]{1,0:T(4,128)} %vel.3, f32[3,128]{1,0:T(4,128)} %frc.3, s32[1,128]{1,0:T(1,128)} %bitcast.11, s32[24,128]{1,0:T(8,128)} %nbr.1, s32[2,32]{1,0:T(2,128)} %inplane.1, s32[2,64]{1,0:T(2,128)} %normal.1), custom_call_target="tpu_custom_call" | custom-call | flops 100000000 | bytes 1048576 | tf_op jit(solution)/shard_map/pack/pallas_call | solution.py:725
  2.8 4.0 %collective-permute-start = (f32[1,32,128]{2,1,0:T(8,128)}, f32[1,32,128]{2,1,0:T(8,128)S(1)}, u32[]{:S(2)}, u32[]{:S(2)}) collective-permute-start(f32[1,32,128]{2,1,0:T(8,128)} %bitcast.8), channel_id=1, source_target_pairs={{0,16},{8,24},{16,0},{24,8},{1,17},{9,25},{17,1},{25,9},{2,18},{10... | collective-permute-start | bytes 49160 | tf_op jit(solution)/shard_map/ppermute | solution.py:715
  6.8 1.3 %collective-permute-start.1 = (f32[1,32,128]{2,1,0:T(8,128)}, f32[1,32,128]{2,1,0:T(8,128)S(1)}, u32[]{:S(2)}, u32[]{:S(2)}) collective-permute-start(f32[1,32,128]{2,1,0:T(8,128)} %bitcast.9), channel_id=1, source_target_pairs={{0,24},{8,16},{16,8},{24,0},{1,25},{9,17},{17,9},{25,1},{2,26},{10... | collective-permute-start | bytes 49160 | tf_op jit(solution)/shard_map/ppermute | solution.py:715
  8.1 0.2 collective-permute-start.2
  8.4 0.0 copy-start.6
  8.4 0.9 %copy-done.6 = f32[512,128]{1,0:T(8,128)S(1)} copy-done((f32[512,128]{1,0:T(8,128)S(1)}, f32[512,128]{1,0:T(8,128)}, u32[]{:S(2)}) %copy-start.6) | copy-done | bytes 262168
  9.3 0.0 copy-start.7
  9.3 0.7 %copy-done.7 = f32[32,128]{1,0:T(8,128)S(1)} copy-done((f32[32,128]{1,0:T(8,128)S(1)}, f32[32,128]{1,0:T(8,128)}, u32[]{:S(2)}) %copy-start.7) | copy-done | bytes 16408
  10.1 2.1 %weights.1 = (bf16[128,240]{1,0:T(8,128)(2,1)}, bf16[256,384]{1,0:T(8,128)(2,1)}, bf16[128,768]{1,0:T(8,128)(2,1)}, bf16[64,384]{1,0:T(8,128)(2,1)}, f32[128,128]{1,0:T(8,128)}) custom-call(f32[4,128]{1,0:T(4,128)} %embedding.1, f32[16,128]{1,0:T(8,128)} %radial.3, f32[128,128]{1,0:T(8,128)} %mix.1, f32[128,128]{1,0:T(8,128)} %self_w.1, ...), custom_call_target="tpu_custom_call" | custom-call | flops 4000000000 | bytes 1048576 | tf_op jit(solution)/shard_map/weights/pallas_call | solution.py:725
  12.2 0.0 collective-permute-done
  12.2 0.3 collective-permute-done.1
  12.5 0.0 collective-permute-done.2
  12.6 2.5 %collective-permute-start.3 = (f32[4,32,128]{2,1,0:T(8,128)S(1)}, f32[4,32,128]{2,1,0:T(8,128)S(1)}, u32[]{:S(2)}, u32[]{:S(2)}) collective-permute-start(f32[4,32,128]{2,1,0:T(8,128)S(1)} %get-tuple-element.101.data), channel_id=1, source_target_pairs={{0,6},{1,7},{2,4},{3,5},{4,2},{5,3},{6,0},{7,1},{8,14},{9,15},{10,... | collective-permute-start | bytes 196616 | tf_op jit(solution)/shard_map/ppermute | solution.py:715
  15.1 0.5 %collective-permute-start.4 = (f32[4,32,128]{2,1,0:T(8,128)S(1)}, f32[4,32,128]{2,1,0:T(8,128)S(1)}, u32[]{:S(2)}, u32[]{:S(2)}) collective-permute-start(f32[4,32,128]{2,1,0:T(8,128)S(1)} %get-tuple-element.101.data), channel_id=1, source_target_pairs={{0,2},{1,3},{2,0},{3,1},{4,6},{5,7},{6,4},{7,5},{8,10},{9,11},{10,... | collective-permute-start | bytes 196616 | tf_op jit(solution)/shard_map/ppermute | solution.py:715
  15.6 0.5 %collective-permute-start.5 = (f32[4,32,128]{2,1,0:T(8,128)S(1)}, f32[4,32,128]{2,1,0:T(8,128)S(1)}, u32[]{:S(2)}, u32[]{:S(2)}) collective-permute-start(f32[4,32,128]{2,1,0:T(8,128)S(1)} %get-tuple-element.101.data), channel_id=1, source_target_pairs={{0,4},{1,5},{2,6},{3,7},{4,0},{5,1},{6,2},{7,3},{8,12},{9,13},{10,... | collective-permute-start | bytes 196616 | tf_op jit(solution)/shard_map/ppermute | solution.py:715
  16.1 0.9 %column.1 = (bf16[512,512]{1,0:T(8,128)(2,1)S(1)}, bf16[512,512]{1,0:T(8,128)(2,1)S(1)}, bf16[512,512]{1,0:T(8,128)(2,1)S(1)}, bf16[512,512]{1,0:T(8,128)(2,1)S(...) custom-call(f32[4,32,128]{2,1,0:T(8,128)S(1)} %get-tuple-element.101, ...), custom_call_target="tpu_custom_call" | custom-call | flops 1000000000 | bytes 1048576 | tf_op jit(solution)/shard_map/column/pallas_call | solution.py:725
  17.1 0.8 %collective-permute-done.3.data = f32[4,32,128]{2,1,0:T(8,128)S(1)} collective-permute-done((f32[4,32,128]{2,1,0:T(8,128)S(1)}, f32[4,32,128]{2,1,0:T(8,128)S(1)}, u32[]{:S(2)}, u32[]{:S(2)}) %collective-permute-start.3) | collective-permute-done | bytes 65568 | tf_op jit(solution)/shard_map/ppermute | solution.py:715
  17.9 0.0 copy-start.8
  17.9 0.7 %tables.3 = (bf16[512,512]{1,0:T(8,128)(2,1)S(1)}, bf16[512,512]{1,0:T(8,128)(2,1)S(1)}, bf16[512,512]{1,0:T(8,128)(2,1)S(1)}, bf16[512,512]{1,0:T(8,128)(2,1)S(1)}, f32[8,128]{1,0:T(8,128)S(1)}) custom-call(f32[4,32,128]{2,1,0:T(8,128)S(1)} %collective-permute-done.3.data, f32[8,768]{1,0:T(8,128)S(1)} %get-tuple-element.55.ahead.refs_12_), custom_call_target="tpu_custom_call" | custom-call | flops 4000000000 | bytes 1048576 | tf_op jit(solution)/shard_map/tables/pallas_call | solution.py:725
  18.6 0.8 %collective-permute-done.4.data = f32[4,32,128]{2,1,0:T(8,128)S(1)} collective-permute-done((f32[4,32,128]{2,1,0:T(8,128)S(1)}, f32[4,32,128]{2,1,0:T(8,128)S(1)}, u32[]{:S(2)}, u32[]{:S(2)}) %collective-permute-start.4) | collective-permute-done | bytes 65568 | tf_op jit(solution)/shard_map/ppermute | solution.py:715
  19.3 0.0 copy-done.8
  19.3 0.7 %tables.4 = (bf16[512,512]{1,0:T(8,128)(2,1)S(1)}, bf16[512,512]{1,0:T(8,128)(2,1)S(1)}, bf16[512,512]{1,0:T(8,128)(2,1)S(1)}, bf16[512,512]{1,0:T(8,128)(2,1)S(1)}, f32[8,128]{1,0:T(8,128)S(1)}) custom-call(f32[4,32,128]{2,1,0:T(8,128)S(1)} %collective-permute-done.4.data, f32[32,128]{1,0:T(8,128)S(1)} %copy-done.8), custom_call_target="tpu_custom_call" | custom-call | flops 4000000000 | bytes 1048576 | tf_op jit(solution)/shard_map/tables/pallas_call | solution.py:725
  20.0 0.0 collective-permute-done.5.data
  20.1 0.0 copy-start
  20.1 0.0 copy-start.1
  20.1 0.0 copy-start.2
  20.1 0.0 copy-start.3
  20.1 0.0 copy-start.4
  20.1 0.0 copy-start.5
  20.1 0.1 collective-permute-start.6
  20.2 0.7 %tables.5 = (bf16[512,512]{1,0:T(8,128)(2,1)S(1)}, bf16[512,512]{1,0:T(8,128)(2,1)S(1)}, bf16[512,512]{1,0:T(8,128)(2,1)S(1)}, bf16[512,512]{1,0:T(8,128)(2,1)S(1)}, f32[8,128]{1,0:T(8,128)}) custom-call(f32[4,32,128]{2,1,0:T(8,128)S(1)} %collective-permute-done.5.data, f32[32,128]{1,0:T(8,128)S(1)} %copy-done.8), custom_call_target="tpu_custom_call" | custom-call | flops 4000000000 | bytes 1048576 | tf_op jit(solution)/shard_map/tables/pallas_call | solution.py:725
  20.9 0.6 %collective-permute-done.6.theirs = f32[16,8,128]{2,1,0:T(8,128)S(1)} collective-permute-done((f32[16,8,128]{2,1,0:T(8,128)S(1)}, f32[16,8,128]{2,1,0:T(8,128)S(1)}, u32[]{:S(2)}, u32[]{:S(2)}) %collective-permute-start.6) | collective-permute-done | bytes 65568 | tf_op jit(solution)/shard_map/ppermute | solution.py:715
  21.5 0.0 copy-done
  21.5 0.0 copy-done.1
  21.5 0.0 copy-done.2
  21.5 0.0 copy-done.3
  21.5 0.0 copy-done.4
  21.5 0.0 copy-done.5
  21.5 4.1 %forward.1 = (bf16[256,2048]{1,0:T(8,128)(2,1)S(1)}, f32[1,128]{1,0:T(1,128)S(1)}, f32[7,6,24,128]{3,2,1,0:T(8,128)S(1)}, f32[128,896]{1,0:T(8,128)S(1)}, f32[128,896]{1,0:T(8,128)S(1)}) custom-call(f32[16,32,128]{2,1,0:T(8,128)S(1)} %constant_dynamic-update-slice_fusion.4.mine, f32[16,8,128]{2,1,0:T(8,128)S(1)} %collective-permute-done.6.theirs, ...), custom_call_target="tpu_custom_call" | custom-call | flops 100000000 | bytes 1048576 | tf_op jit(solution)/shard_map/forward/pallas_call | solution.py:725
  25.6 1.3 %structure.3.part.sin_own = f32[512,128]{1,0:T(8,128)S(1)} custom-call(bf16[512,512]{1,0:T(8,128)(2,1)S(1)} %get-tuple-element.71.refs_0_, bf16[512,512]{1,0:T(8,128)(2,1)S(1)} %get-tuple-element.72.refs_1_, bf16[512,512]{1,0:T(8,128)(2,1)S(1)} %get-tuple-element.73.refs_2_, bf16[512,512]{1,0:T(8,128)(2,1)S(1)} %get-tuple-element.74.refs_3_, ...), custom_call_target="tpu_custom_call" | custom-call | flops 1000000000 | bytes 1048576 | tf_op jit(solution)/shard_map/structure/pallas_call | solution.py:725
  26.9 0.2 collective-permute-start.8
  27.1 1.3 %structure.2.cos_own = f32[512,128]{1,0:T(8,128)S(1)} custom-call(bf16[512,512]{1,0:T(8,128)(2,1)S(1)} %get-tuple-element.53.refs_0_, bf16[512,512]{1,0:T(8,128)(2,1)S(1)} %get-tuple-element.54.refs_1_, bf16[512,512]{1,0:T(8,128)(2,1)S(1)} %get-tuple-element.56.refs_2_.refs_0_, bf16[512,512]{1,0:T(8,128)(2,1)S(1)} %get-tuple-element.57.refs_3_.refs_1_, ...), custom_call_target="tpu_custom_call" | custom-call | flops 1000000000 | bytes 1048576 | tf_op jit(solution)/shard_map/structure/pallas_call | solution.py:725
  28.4 0.4 %collective-permute-start.7 = (f32[512,128]{1,0:T(8,128)S(1)}, f32[512,128]{1,0:T(8,128)S(1)}, u32[]{:S(2)}, u32[]{:S(2)}) collective-permute-start(f32[512,128]{1,0:T(8,128)S(1)} %structure.2.cos_own), channel_id=1, source_target_pairs={{0,1},{1,0},{2,3},{3,2},{4,5},{5,4},{6,7},{7,6},{8,9},{9,8},{10,11... | collective-permute-start | bytes 786440 | tf_op jit(solution)/shard_map/ppermute | solution.py:715
  28.8 0.5 %near.1 = (bf16[512,768]{1,0:T(8,128)(2,1)S(1)}, bf16[512,768]{1,0:T(8,128)(2,1)S(1)}, bf16[512,768]{1,0:T(8,128)(2,1)S(1)}, bf16[512,768]{1,0:T(8,128)(2,1)S(1)}, f32[8,768]{1,0:T(8,128)S(1)}) custom-call(f32[16,32,128]{2,1,0:T(8,128)S(1)} %constant_dynamic-update-slice_fusion.4.mine,, ...), custom_call_target="tpu_custom_call", output_to_operand_aliasing={{0}: (9, {}), {1}: (10, {}), {2}: (11, {}), {3}: (12, {}), ... | custom-call | flops 4000000000 | bytes 1048576 | tf_op jit(solution)/shard_map/near/pallas_call | solution.py:725
  29.3 0.3 fall.1.fall_in
  29.6 0.0 collective-permute-done.8.other.sin_other
  29.6 0.6 %pull.1 = (f32[128,768]{1,0:T(8,128)S(1)}, f32[1,128]{1,0:T(1,128)S(1)}) custom-call(f32[512,128]{1,0:T(8,128)S(1)} %structure.3.part.sin_own, f32[512,128]{1,0:T(8,128)S(1)} %collective-permute-done.8.other.sin_other, f32[512,128]{1,0:T(8,128)S(1)} %get-tuple-element.79.scale, bf16[512,768]{1,0:T(8,128)(2,1)S(1)} %get-tuple-element.84.high.sin_high, ...), custom_call_target="tpu_custom_call" | custom-call | flops 1000000000 | bytes 1048576 | tf_op jit(solution)/shard_map/pull/pallas_call | solution.py:725
  30.2 0.0 collective-permute-done.7.cos_other
  30.2 3.2 %backward.1 = (f32[8,128]{1,0:T(8,128)S(1)}, f32[8,128]{1,0:T(8,128)S(1)}, f32[1,128]{1,0:T(1,128)}) custom-call(f32[512,128]{1,0:T(8,128)S(1)} %structure.2.cos_own, f32[512,128]{1,0:T(8,128)S(1)} %collective-permute-done.7.cos_other, f32[128,768]{1,0:T(8,128)S(1)} %get-tuple-element.86.grad_in, f32[1,128]{1,0:T(1,128)S(1)} %get-tuple-element.87.sin_energy, ...), custom_call_target="tpu_custom_call" | custom-call | flops 100000000 | bytes 1048576 | tf_op jit(solution)/shard_map/backward/pallas_call | solution.py:725
  33.3 0.0 copy-start.9
  33.3 0.0 copy-start.10
  33.3 0.0 copy-start.11
  33.3 0.0 copy-start.12
  33.3 0.0 copy-start.13
  33.4 0.2 collective-permute-start.9
  33.6 0.5 %ewald.1 = f32[8,128]{1,0:T(8,128)S(1)} custom-call(f32[512,128]{1,0:T(8,128)S(1)} %structure.2.cos_own, f32[512,128]{1,0:T(8,128)S(1)} %collective-permute-done.7.cos_other, f32[512,128]{1,0:T(8,128)S(1)} %structure.3.part.sin_own, f32[512,128]{1,0:T(8,128)S(1)} %collective-permute-done.8.other.sin_other, f32[512,128]{1,0:T(8,128)S(1)} %get-tuple-element.79.scale, ...), custom_call_target="tpu_custom_call" | custom-call | flops 4000000000 | bytes 1048576 | tf_op jit(solution)/shard_map/ewald/pallas_call | solution.py:725
  34.1 0.5 %collective-permute-done.9.other = f32[8,128]{1,0:T(8,128)S(1)} collective-permute-done((f32[8,128]{1,0:T(8,128)S(1)}, f32[8,128]{1,0:T(8,128)S(1)}, u32[]{:S(2)}, u32[]{:S(2)}) %collective-permute-start.9) | collective-permute-done | bytes 4128 | tf_op jit(solution)/shard_map/ppermute | solution.py:715
  34.6 0.0 copy-done.9
  34.6 0.0 copy-done.10
  34.6 0.0 copy-done.11
  34.6 0.0 copy-done.12
  34.6 0.0 copy-done.13
  34.6 0.7 %final.1 = (f32[3,128]{1,0:T(4,128)}, f32[3,128]{1,0:T(4,128)}, f32[3,128]{1,0:T(4,128)}) custom-call(f32[3,128]{1,0:T(4,128)S(1)} %copy-done.9, f32[3,128]{1,0:T(4,128)S(1)} %copy-done.10, f32[3,128]{1,0:T(4,128)S(1)} %copy-done.11, s32[1,128]{1,0:T(1,128)S(1)} %bitcast.12, f32[1,4]{1,0:T(1,128)S(1)} %bitcast.14, f32[8,128]{1,0:T(8,128)S(1)} %get-tuple-element.94.own, ...), custom_call_target="tpu_custom_call" | custom-call | flops 100000000 | bytes 1048576 | tf_op jit(solution)/shard_map/final/pallas_call | solution.py:725
  (9 shorter events, 0.1 us)
Async XLA Ops:
  2.8 9.4 %collective-permute-start = (f32[1,32,128]{2,1,0:T(8,128)}, f32[1,32,128]{2,1,0:T(8,128)S(1)}, u32[]{:S(2)}, u32[]{:S(2)}) collective-permute-start(f32[1,32,128]{2,1,0:T(8,128)} %bitcast.8), channel_id=1, source_target_pairs={{0,16},{8,24},{16,0},{24,8},{1,17},{9,25},{17,1},{25,9},{2,18},{10... | collective-permute-start | bytes 49160 | tf_op jit(solution)/shard_map/ppermute | solution.py:715
  6.8 5.7 %collective-permute-start.1 = (f32[1,32,128]{2,1,0:T(8,128)}, f32[1,32,128]{2,1,0:T(8,128)S(1)}, u32[]{:S(2)}, u32[]{:S(2)}) collective-permute-start(f32[1,32,128]{2,1,0:T(8,128)} %bitcast.9), channel_id=1, source_target_pairs={{0,24},{8,16},{16,8},{24,0},{1,25},{9,17},{17,9},{25,1},{2,26},{10... | collective-permute-start | bytes 49160 | tf_op jit(solution)/shard_map/ppermute | solution.py:715
  8.1 4.4 %collective-permute-start.2 = (f32[1,32,128]{2,1,0:T(8,128)}, f32[1,32,128]{2,1,0:T(8,128)S(1)}, u32[]{:S(2)}, u32[]{:S(2)}) collective-permute-start(f32[1,32,128]{2,1,0:T(8,128)} %bitcast.10), channel_id=1, source_target_pairs={{0,8},{8,0},{16,24},{24,16},{1,9},{9,1},{17,25},{25,17},{2,10},{10... | collective-permute-start | bytes 49160 | tf_op jit(solution)/shard_map/ppermute | solution.py:715
  8.4 0.9 %copy-start.6 = (f32[512,128]{1,0:T(8,128)S(1)}, f32[512,128]{1,0:T(8,128)}, u32[]{:S(2)}) copy-start(f32[512,128]{1,0:T(8,128)} %kernel_filter.1) | copy-start | bytes 786436
  9.3 0.7 %copy-start.7 = (f32[32,128]{1,0:T(8,128)S(1)}, f32[32,128]{1,0:T(8,128)}, u32[]{:S(2)}) copy-start(f32[32,128]{1,0:T(8,128)} %pack.1.block.ahead) | copy-start | bytes 49156
  12.6 5.3 %collective-permute-start.3 = (f32[4,32,128]{2,1,0:T(8,128)S(1)}, f32[4,32,128]{2,1,0:T(8,128)S(1)}, u32[]{:S(2)}, u32[]{:S(2)}) collective-permute-start(f32[4,32,128]{2,1,0:T(8,128)S(1)} %get-tuple-element.101.data), channel_id=1, source_target_pairs={{0,6},{1,7},{2,4},{3,5},{4,2},{5,3},{6,0},{7,1},{8,14},{9,15},{10,... | collective-permute-start | bytes 196616 | tf_op jit(solution)/shard_map/ppermute | solution.py:715
  15.1 4.3 %collective-permute-start.4 = (f32[4,32,128]{2,1,0:T(8,128)S(1)}, f32[4,32,128]{2,1,0:T(8,128)S(1)}, u32[]{:S(2)}, u32[]{:S(2)}) collective-permute-start(f32[4,32,128]{2,1,0:T(8,128)S(1)} %get-tuple-element.101.data), channel_id=1, source_target_pairs={{0,2},{1,3},{2,0},{3,1},{4,6},{5,7},{6,4},{7,5},{8,10},{9,11},{10,... | collective-permute-start | bytes 196616 | tf_op jit(solution)/shard_map/ppermute | solution.py:715
  15.6 4.4 %collective-permute-start.5 = (f32[4,32,128]{2,1,0:T(8,128)S(1)}, f32[4,32,128]{2,1,0:T(8,128)S(1)}, u32[]{:S(2)}, u32[]{:S(2)}) collective-permute-start(f32[4,32,128]{2,1,0:T(8,128)S(1)} %get-tuple-element.101.data), channel_id=1, source_target_pairs={{0,4},{1,5},{2,6},{3,7},{4,0},{5,1},{6,2},{7,3},{8,12},{9,13},{10,... | collective-permute-start | bytes 196616 | tf_op jit(solution)/shard_map/ppermute | solution.py:715
  17.9 1.4 %copy-start.8 = (f32[32,128]{1,0:T(8,128)S(1)}, f32[32,128]{1,0:T(8,128)}, u32[]{:S(2)}) copy-start(f32[32,128]{1,0:T(8,128)} %pack.1.block.ahead) | copy-start | bytes 49156
  20.1 1.4 %copy-start = (bf16[128,768]{1,0:T(8,128)(2,1)S(1)}, bf16[128,768]{1,0:T(8,128)(2,1)}, u32[]{:S(2)}) copy-start(bf16[128,768]{1,0:T(8,128)(2,1)} %get-tuple-element.67.later_wb3.wb3) | copy-start | bytes 589828
  20.1 1.4 %copy-start.1 = (bf16[64,384]{1,0:T(8,128)(2,1)S(1)}, bf16[64,384]{1,0:T(8,128)(2,1)}, u32[]{:S(2)}) copy-start(bf16[64,384]{1,0:T(8,128)(2,1)} %get-tuple-element.68.later_re3.re3) | copy-start | bytes 147460
  20.1 1.4 %copy-start.2 = (bf16[256,384]{1,0:T(8,128)(2,1)S(1)}, bf16[256,384]{1,0:T(8,128)(2,1)}, u32[]{:S(2)}) copy-start(bf16[256,384]{1,0:T(8,128)(2,1)} %get-tuple-element.65.wcu3) | copy-start | bytes 589828
  20.1 1.4 %copy-start.3 = (bf16[128,240]{1,0:T(8,128)(2,1)S(1)}, bf16[128,240]{1,0:T(8,128)(2,1)}, u32[]{:S(2)}) copy-start(bf16[128,240]{1,0:T(8,128)(2,1)} %get-tuple-element.64.rex3) | copy-start | bytes 184324
  20.1 1.4 %copy-start.4 = (f32[128,128]{1,0:T(8,128)S(1)}, f32[128,128]{1,0:T(8,128)}, u32[]{:S(2)}) copy-start(f32[128,128]{1,0:T(8,128)} %get-tuple-element.66.rv_ref) | copy-start | bytes 196612
  20.1 1.4 %copy-start.5 = (f32[16,128]{1,0:T(8,128)S(1)}, f32[16,128]{1,0:T(8,128)}, u32[]{:S(2)}) copy-start(f32[16,128]{1,0:T(8,128)} %radial.3) | copy-start | bytes 24580
  20.1 1.3 %collective-permute-start.6 = (f32[16,8,128]{2,1,0:T(8,128)S(1)}, f32[16,8,128]{2,1,0:T(8,128)S(1)}, u32[]{:S(2)}, u32[]{:S(2)}) collective-permute-start(f32[16,8,128]{2,1,0:T(8,128)S(1)} %fusion), channel_id=1, source_target_pairs={{0,1},{1,0},{2,3},{3,2},{4,5},{5,4},{6,7},{7,6},{8,9},{9,8},{10,11... | collective-permute-start | bytes 196616 | tf_op jit(solution)/shard_map/ppermute | solution.py:715
  26.9 2.7 %collective-permute-start.8 = (f32[512,128]{1,0:T(8,128)S(1)}, f32[512,128]{1,0:T(8,128)S(1)}, u32[]{:S(2)}, u32[]{:S(2)}) collective-permute-start(f32[512,128]{1,0:T(8,128)S(1)} %structure.3.part.sin_own), channel_id=1, source_target_pairs={{0,1},{1,0},{2,3},{3,2},{4,5},{5,4},{6,7},{7,6},{8,9},{9,8},{10,11... | collective-permute-start | bytes 786440 | tf_op jit(solution)/shard_map/ppermute | solution.py:715
  28.4 1.8 %collective-permute-start.7 = (f32[512,128]{1,0:T(8,128)S(1)}, f32[512,128]{1,0:T(8,128)S(1)}, u32[]{:S(2)}, u32[]{:S(2)}) collective-permute-start(f32[512,128]{1,0:T(8,128)S(1)} %structure.2.cos_own), channel_id=1, source_target_pairs={{0,1},{1,0},{2,3},{3,2},{4,5},{5,4},{6,7},{7,6},{8,9},{9,8},{10,11... | collective-permute-start | bytes 786440 | tf_op jit(solution)/shard_map/ppermute | solution.py:715
  33.3 1.3 %copy-start.9 = (f32[3,128]{1,0:T(4,128)S(1)}, f32[3,128]{1,0:T(4,128)}, u32[]{:S(2)}) copy-start(f32[3,128]{1,0:T(4,128)} %pos.3) | copy-start | bytes 4612
  33.3 1.3 %copy-start.10 = (f32[3,128]{1,0:T(4,128)S(1)}, f32[3,128]{1,0:T(4,128)}, u32[]{:S(2)}) copy-start(f32[3,128]{1,0:T(4,128)} %vel.3) | copy-start | bytes 4612
  33.3 1.3 %copy-start.11 = (f32[3,128]{1,0:T(4,128)S(1)}, f32[3,128]{1,0:T(4,128)}, u32[]{:S(2)}) copy-start(f32[3,128]{1,0:T(4,128)} %frc.3) | copy-start | bytes 4612
  33.3 1.3 %copy-start.12 = (s32[128]{0:T(128)S(1)}, s32[128]{0:T(128)}, u32[]{:S(2)}) copy-start(s32[128]{0:T(128)} %param.20) | copy-start | bytes 1540
  33.3 1.3 %copy-start.13 = (f32[4]{0:T(128)S(1)}, f32[4]{0:T(128)}, u32[]{:S(2)}) copy-start(f32[4]{0:T(128)} %param.26) | copy-start | bytes 52
  33.4 1.2 %collective-permute-start.9 = (f32[8,128]{1,0:T(8,128)S(1)}, f32[8,128]{1,0:T(8,128)S(1)}, u32[]{:S(2)}, u32[]{:S(2)}) collective-permute-start(f32[8,128]{1,0:T(8,128)S(1)} %get-tuple-element.95), channel_id=1, source_target_pairs={{0,1},{1,0},{2,3},{3,2},{4,5},{5,4},{6,7},{7,6},{8,9},{9,8},{10,11... | collective-permute-start | bytes 12296 | tf_op jit(solution)/shard_map/ppermute | solution.py:715

commit v7 on v6

--- a/solution.py
+++ b/solution.py
@@ -427,12 +427,14 @@
         chunk = q_out.shape[1] // own
 
         def chunk_step(c, carry):
+            place = total // chunk - 1 - c
+
             def steps(n, inner):
-                group_step(c * (chunk // group) + n, n * group)
+                group_step(place * (chunk // group) + n, n * group)
                 return inner
 
             def phases(n, inner):
-                record = mine[c * chunk + n, 0:8, :]
+                record = mine[place * chunk + n, 0:8, :]
                 store_phases(record, layers, strips, tables, pl.multiple_of(n * own, own))
                 return inner
 
@@ -766,7 +768,7 @@
     waves = KGRID**3
     kind_row = species[None, :]
     total = layers * (strips // 2)
-    early = total <= 16
+    early = total <= 16 and strips <= 8
     group = min(16, total)
     block_size = min(4, group)
     near_layers = min(3, layers)

time: 35.6 us -> 35.6 us (level)
  no operation moved by 1% of the time
where the time goes in v7:
time: 35.6 us; the launch traced here: 35.3 us
  Pallas kernels  18.9 us (53%)
  starting transfers between devices  10.1 us (28%)
  waiting for transfers between devices  2.95 us (8%)
  local copies, waits for them, and re-layouts  1.76 us (5%)
  between operations  1.54 us (4%)
    pallas_call x16, Pallas kernels, call(): pl.pallas_call(kernel, out_shape=[jax.ShapeDtypeStruct(shape, dtype) for...  18.9 us
    ppermute x10, starting transfers between devices, exchange(): return lax.ppermute(x, axis, [(i, i ^ bit) for i in range(count)])  10.1 us
    ppermute x10, waiting for transfers between devices, exchange(): return lax.ppermute(x, axis, [(i, i ^ bit) for i in range(count)])  2.95 us
    unnamed x34, local copies, waits for them, and re-layouts  1.75 us
  transfers between devices with their start and end apart: 10, of which 5 were waited for; matrix products, arithmetic and copies ran while one was open for 0% of the time, Pallas kernels for 23%

profile of v7, /device:TPU:0, one launch (start us, length us, event | category | flops | bytes accessed | tf_op | source)
XLA Modules:
  0.0 35.3 jit_solution(2102787071898599333)
XLA Ops:
  1.3 1.5 %pack.1.block.ahead = f32[32,128]{1,0:T(8,128)} custom-call(s32[1,1]{1,0:T(1,128)} %bitcast.7.cnt, f32[1,4]{1,0:T(1,128)} %bitcast.13, f32[3,128]{1,0:T(4,128)} %pos.3, f32[3,128]{1,0:T(4,128)} %vel.3, f32[3,128]{1,0:T(4,128)} %frc.3, s32[1,128]{1,0:T(1,128)} %bitcast.11, s32[24,128]{1,0:T(8,128)} %nbr.1, s32[2,32]{1,0:T(2,128)} %inplane.1, s32[2,64]{1,0:T(2,128)} %normal.1), custom_call_target="tpu_custom_call" | custom-call | flops 100000000 | bytes 1048576 | tf_op jit(solution)/shard_map/pack/pallas_call | solution.py:727
  2.8 4.0 %collective-permute-start = (f32[1,32,128]{2,1,0:T(8,128)}, f32[1,32,128]{2,1,0:T(8,128)S(1)}, u32[]{:S(2)}, u32[]{:S(2)}) collective-permute-start(f32[1,32,128]{2,1,0:T(8,128)} %bitcast.8), channel_id=1, source_target_pairs={{0,16},{8,24},{16,0},{24,8},{1,17},{9,25},{17,1},{25,9},{2,18},{10... | collective-permute-start | bytes 49160 | tf_op jit(solution)/shard_map/ppermute | solution.py:717
  6.8 1.3 %collective-permute-start.1 = (f32[1,32,128]{2,1,0:T(8,128)}, f32[1,32,128]{2,1,0:T(8,128)S(1)}, u32[]{:S(2)}, u32[]{:S(2)}) collective-permute-start(f32[1,32,128]{2,1,0:T(8,128)} %bitcast.9), channel_id=1, source_target_pairs={{0,24},{8,16},{16,8},{24,0},{1,25},{9,17},{17,9},{25,1},{2,26},{10... | collective-permute-start | bytes 49160 | tf_op jit(solution)/shard_map/ppermute | solution.py:717
  8.1 0.2 collective-permute-start.2
  8.4 0.0 copy-start.6
  8.4 0.9 %copy-done.6 = f32[512,128]{1,0:T(8,128)S(1)} copy-done((f32[512,128]{1,0:T(8,128)S(1)}, f32[512,128]{1,0:T(8,128)}, u32[]{:S(2)}) %copy-start.6) | copy-done | bytes 262168
  9.3 0.0 copy-start.7
  9.3 0.7 %copy-done.7 = f32[32,128]{1,0:T(8,128)S(1)} copy-done((f32[32,128]{1,0:T(8,128)S(1)}, f32[32,128]{1,0:T(8,128)}, u32[]{:S(2)}) %copy-start.7) | copy-done | bytes 16408
  10.1 2.1 %weights.1 = (bf16[128,240]{1,0:T(8,128)(2,1)}, bf16[256,384]{1,0:T(8,128)(2,1)}, bf16[128,768]{1,0:T(8,128)(2,1)}, bf16[64,384]{1,0:T(8,128)(2,1)}, f32[128,128]{1,0:T(8,128)}) custom-call(f32[4,128]{1,0:T(4,128)} %embedding.1, f32[16,128]{1,0:T(8,128)} %radial.3, f32[128,128]{1,0:T(8,128)} %mix.1, f32[128,128]{1,0:T(8,128)} %self_w.1, ...), custom_call_target="tpu_custom_call" | custom-call | flops 4000000000 | bytes 1048576 | tf_op jit(solution)/shard_map/weights/pallas_call | solution.py:727
  12.2 0.0 collective-permute-done
  12.2 0.3 collective-permute-done.1
  12.5 0.0 collective-permute-done.2
  12.6 2.5 %collective-permute-start.3 = (f32[4,32,128]{2,1,0:T(8,128)S(1)}, f32[4,32,128]{2,1,0:T(8,128)S(1)}, u32[]{:S(2)}, u32[]{:S(2)}) collective-permute-start(f32[4,32,128]{2,1,0:T(8,128)S(1)} %get-tuple-element.101.data), channel_id=1, source_target_pairs={{0,6},{1,7},{2,4},{3,5},{4,2},{5,3},{6,0},{7,1},{8,14},{9,15},{10,... | collective-permute-start | bytes 196616 | tf_op jit(solution)/shard_map/ppermute | solution.py:717
  15.1 0.5 %collective-permute-start.4 = (f32[4,32,128]{2,1,0:T(8,128)S(1)}, f32[4,32,128]{2,1,0:T(8,128)S(1)}, u32[]{:S(2)}, u32[]{:S(2)}) collective-permute-start(f32[4,32,128]{2,1,0:T(8,128)S(1)} %get-tuple-element.101.data), channel_id=1, source_target_pairs={{0,2},{1,3},{2,0},{3,1},{4,6},{5,7},{6,4},{7,5},{8,10},{9,11},{10,... | collective-permute-start | bytes 196616 | tf_op jit(solution)/shard_map/ppermute | solution.py:717
  15.6 0.5 %collective-permute-start.5 = (f32[4,32,128]{2,1,0:T(8,128)S(1)}, f32[4,32,128]{2,1,0:T(8,128)S(1)}, u32[]{:S(2)}, u32[]{:S(2)}) collective-permute-start(f32[4,32,128]{2,1,0:T(8,128)S(1)} %get-tuple-element.101.data), channel_id=1, source_target_pairs={{0,4},{1,5},{2,6},{3,7},{4,0},{5,1},{6,2},{7,3},{8,12},{9,13},{10,... | collective-permute-start | bytes 196616 | tf_op jit(solution)/shard_map/ppermute | solution.py:717
  16.1 0.9 %column.1 = (bf16[512,512]{1,0:T(8,128)(2,1)S(1)}, bf16[512,512]{1,0:T(8,128)(2,1)S(1)}, bf16[512,512]{1,0:T(8,128)(2,1)S(1)}, bf16[512,512]{1,0:T(8,128)(2,1)S(...) custom-call(f32[4,32,128]{2,1,0:T(8,128)S(1)} %get-tuple-element.101, ...), custom_call_target="tpu_custom_call" | custom-call | flops 1000000000 | bytes 1048576 | tf_op jit(solution)/shard_map/column/pallas_call | solution.py:727
  17.1 0.8 %collective-permute-done.3.data = f32[4,32,128]{2,1,0:T(8,128)S(1)} collective-permute-done((f32[4,32,128]{2,1,0:T(8,128)S(1)}, f32[4,32,128]{2,1,0:T(8,128)S(1)}, u32[]{:S(2)}, u32[]{:S(2)}) %collective-permute-start.3) | collective-permute-done | bytes 65568 | tf_op jit(solution)/shard_map/ppermute | solution.py:717
  17.9 0.0 copy-start.8
  17.9 0.7 %tables.3 = (bf16[512,512]{1,0:T(8,128)(2,1)S(1)}, bf16[512,512]{1,0:T(8,128)(2,1)S(1)}, bf16[512,512]{1,0:T(8,128)(2,1)S(1)}, bf16[512,512]{1,0:T(8,128)(2,1)S(1)}, f32[8,128]{1,0:T(8,128)S(1)}) custom-call(f32[4,32,128]{2,1,0:T(8,128)S(1)} %collective-permute-done.3.data, f32[8,768]{1,0:T(8,128)S(1)} %get-tuple-element.55.ahead.refs_12_), custom_call_target="tpu_custom_call" | custom-call | flops 4000000000 | bytes 1048576 | tf_op jit(solution)/shard_map/tables/pallas_call | solution.py:727
  18.6 0.8 %collective-permute-done.4.data = f32[4,32,128]{2,1,0:T(8,128)S(1)} collective-permute-done((f32[4,32,128]{2,1,0:T(8,128)S(1)}, f32[4,32,128]{2,1,0:T(8,128)S(1)}, u32[]{:S(2)}, u32[]{:S(2)}) %collective-permute-start.4) | collective-permute-done | bytes 65568 | tf_op jit(solution)/shard_map/ppermute | solution.py:717
  19.3 0.0 copy-done.8
  19.3 0.7 %tables.4 = (bf16[512,512]{1,0:T(8,128)(2,1)S(1)}, bf16[512,512]{1,0:T(8,128)(2,1)S(1)}, bf16[512,512]{1,0:T(8,128)(2,1)S(1)}, bf16[512,512]{1,0:T(8,128)(2,1)S(1)}, f32[8,128]{1,0:T(8,128)S(1)}) custom-call(f32[4,32,128]{2,1,0:T(8,128)S(1)} %collective-permute-done.4.data, f32[32,128]{1,0:T(8,128)S(1)} %copy-done.8), custom_call_target="tpu_custom_call" | custom-call | flops 4000000000 | bytes 1048576 | tf_op jit(solution)/shard_map/tables/pallas_call | solution.py:727
  20.0 0.0 collective-permute-done.5.data
  20.1 0.0 copy-start
  20.1 0.0 copy-start.1
  20.1 0.0 copy-start.2
  20.1 0.0 copy-start.3
  20.1 0.0 copy-start.4
  20.1 0.0 copy-start.5
  20.1 0.1 collective-permute-start.6
  20.2 0.7 %tables.5 = (bf16[512,512]{1,0:T(8,128)(2,1)S(1)}, bf16[512,512]{1,0:T(8,128)(2,1)S(1)}, bf16[512,512]{1,0:T(8,128)(2,1)S(1)}, bf16[512,512]{1,0:T(8,128)(2,1)S(1)}, f32[8,128]{1,0:T(8,128)}) custom-call(f32[4,32,128]{2,1,0:T(8,128)S(1)} %collective-permute-done.5.data, f32[32,128]{1,0:T(8,128)S(1)} %copy-done.8), custom_call_target="tpu_custom_call" | custom-call | flops 4000000000 | bytes 1048576 | tf_op jit(solution)/shard_map/tables/pallas_call | solution.py:727
  20.9 0.6 %collective-permute-done.6.theirs = f32[16,8,128]{2,1,0:T(8,128)S(1)} collective-permute-done((f32[16,8,128]{2,1,0:T(8,128)S(1)}, f32[16,8,128]{2,1,0:T(8,128)S(1)}, u32[]{:S(2)}, u32[]{:S(2)}) %collective-permute-start.6) | collective-permute-done | bytes 65568 | tf_op jit(solution)/shard_map/ppermute | solution.py:717
  21.5 0.0 copy-done
  21.5 0.0 copy-done.1
  21.5 0.0 copy-done.2
  21.5 0.0 copy-done.3
  21.5 0.0 copy-done.4
  21.5 0.0 copy-done.5
  21.5 4.1 %forward.1 = (bf16[256,2048]{1,0:T(8,128)(2,1)S(1)}, f32[1,128]{1,0:T(1,128)S(1)}, f32[7,6,24,128]{3,2,1,0:T(8,128)S(1)}, f32[128,896]{1,0:T(8,128)S(1)}, f32[128,896]{1,0:T(8,128)S(1)}) custom-call(f32[16,32,128]{2,1,0:T(8,128)S(1)} %constant_dynamic-update-slice_fusion.4.mine, f32[16,8,128]{2,1,0:T(8,128)S(1)} %collective-permute-done.6.theirs, ...), custom_call_target="tpu_custom_call" | custom-call | flops 100000000 | bytes 1048576 | tf_op jit(solution)/shard_map/forward/pallas_call | solution.py:727
  25.6 1.3 %structure.3.part.sin_own = f32[512,128]{1,0:T(8,128)S(1)} custom-call(bf16[512,512]{1,0:T(8,128)(2,1)S(1)} %get-tuple-element.71.refs_0_, bf16[512,512]{1,0:T(8,128)(2,1)S(1)} %get-tuple-element.72.refs_1_, bf16[512,512]{1,0:T(8,128)(2,1)S(1)} %get-tuple-element.73.refs_2_, bf16[512,512]{1,0:T(8,128)(2,1)S(1)} %get-tuple-element.74.refs_3_, ...), custom_call_target="tpu_custom_call" | custom-call | flops 1000000000 | bytes 1048576 | tf_op jit(solution)/shard_map/structure/pallas_call | solution.py:727
  26.9 0.2 collective-permute-start.8
  27.1 1.3 %structure.2.cos_own = f32[512,128]{1,0:T(8,128)S(1)} custom-call(bf16[512,512]{1,0:T(8,128)(2,1)S(1)} %get-tuple-element.53.refs_0_, bf16[512,512]{1,0:T(8,128)(2,1)S(1)} %get-tuple-element.54.refs_1_, bf16[512,512]{1,0:T(8,128)(2,1)S(1)} %get-tuple-element.56.refs_2_.refs_0_, bf16[512,512]{1,0:T(8,128)(2,1)S(1)} %get-tuple-element.57.refs_3_.refs_1_, ...), custom_call_target="tpu_custom_call" | custom-call | flops 1000000000 | bytes 1048576 | tf_op jit(solution)/shard_map/structure/pallas_call | solution.py:727
  28.4 0.4 %collective-permute-start.7 = (f32[512,128]{1,0:T(8,128)S(1)}, f32[512,128]{1,0:T(8,128)S(1)}, u32[]{:S(2)}, u32[]{:S(2)}) collective-permute-start(f32[512,128]{1,0:T(8,128)S(1)} %structure.2.cos_own), channel_id=1, source_target_pairs={{0,1},{1,0},{2,3},{3,2},{4,5},{5,4},{6,7},{7,6},{8,9},{9,8},{10,11... | collective-permute-start | bytes 786440 | tf_op jit(solution)/shard_map/ppermute | solution.py:717
  28.8 0.5 %near.1 = (bf16[512,768]{1,0:T(8,128)(2,1)S(1)}, bf16[512,768]{1,0:T(8,128)(2,1)S(1)}, bf16[512,768]{1,0:T(8,128)(2,1)S(1)}, bf16[512,768]{1,0:T(8,128)(2,1)S(1)}, f32[8,768]{1,0:T(8,128)S(1)}) custom-call(f32[16,32,128]{2,1,0:T(8,128)S(1)} %constant_dynamic-update-slice_fusion.4.mine,, ...), custom_call_target="tpu_custom_call", output_to_operand_aliasing={{0}: (9, {}), {1}: (10, {}), {2}: (11, {}), {3}: (12, {}), ... | custom-call | flops 4000000000 | bytes 1048576 | tf_op jit(solution)/shard_map/near/pallas_call | solution.py:727
  29.3 0.3 fall.1.fall_in
  29.6 0.0 collective-permute-done.8.other.sin_other
  29.6 0.6 %pull.1 = (f32[128,768]{1,0:T(8,128)S(1)}, f32[1,128]{1,0:T(1,128)S(1)}) custom-call(f32[512,128]{1,0:T(8,128)S(1)} %structure.3.part.sin_own, f32[512,128]{1,0:T(8,128)S(1)} %collective-permute-done.8.other.sin_other, f32[512,128]{1,0:T(8,128)S(1)} %get-tuple-element.79.scale, bf16[512,768]{1,0:T(8,128)(2,1)S(1)} %get-tuple-element.84.high.sin_high, ...), custom_call_target="tpu_custom_call" | custom-call | flops 1000000000 | bytes 1048576 | tf_op jit(solution)/shard_map/pull/pallas_call | solution.py:727
  30.2 0.0 collective-permute-done.7.cos_other
  30.2 3.2 %backward.1 = (f32[8,128]{1,0:T(8,128)S(1)}, f32[8,128]{1,0:T(8,128)S(1)}, f32[1,128]{1,0:T(1,128)}) custom-call(f32[512,128]{1,0:T(8,128)S(1)} %structure.2.cos_own, f32[512,128]{1,0:T(8,128)S(1)} %collective-permute-done.7.cos_other, f32[128,768]{1,0:T(8,128)S(1)} %get-tuple-element.86.grad_in, f32[1,128]{1,0:T(1,128)S(1)} %get-tuple-element.87.sin_energy, ...), custom_call_target="tpu_custom_call" | custom-call | flops 100000000 | bytes 1048576 | tf_op jit(solution)/shard_map/backward/pallas_call | solution.py:727
  33.3 0.0 copy-start.9
  33.3 0.0 copy-start.10
  33.3 0.0 copy-start.11
  33.3 0.0 copy-start.12
  33.3 0.0 copy-start.13
  33.4 0.2 collective-permute-start.9
  33.6 0.5 %ewald.1 = f32[8,128]{1,0:T(8,128)S(1)} custom-call(f32[512,128]{1,0:T(8,128)S(1)} %structure.2.cos_own, f32[512,128]{1,0:T(8,128)S(1)} %collective-permute-done.7.cos_other, f32[512,128]{1,0:T(8,128)S(1)} %structure.3.part.sin_own, f32[512,128]{1,0:T(8,128)S(1)} %collective-permute-done.8.other.sin_other, f32[512,128]{1,0:T(8,128)S(1)} %get-tuple-element.79.scale, ...), custom_call_target="tpu_custom_call" | custom-call | flops 4000000000 | bytes 1048576 | tf_op jit(solution)/shard_map/ewald/pallas_call | solution.py:727
  34.1 0.5 %collective-permute-done.9.other = f32[8,128]{1,0:T(8,128)S(1)} collective-permute-done((f32[8,128]{1,0:T(8,128)S(1)}, f32[8,128]{1,0:T(8,128)S(1)}, u32[]{:S(2)}, u32[]{:S(2)}) %collective-permute-start.9) | collective-permute-done | bytes 4128 | tf_op jit(solution)/shard_map/ppermute | solution.py:717
  34.6 0.0 copy-done.9
  34.6 0.0 copy-done.10
  34.6 0.0 copy-done.11
  34.6 0.0 copy-done.12
  34.6 0.0 copy-done.13
  34.6 0.7 %final.1 = (f32[3,128]{1,0:T(4,128)}, f32[3,128]{1,0:T(4,128)}, f32[3,128]{1,0:T(4,128)}) custom-call(f32[3,128]{1,0:T(4,128)S(1)} %copy-done.9, f32[3,128]{1,0:T(4,128)S(1)} %copy-done.10, f32[3,128]{1,0:T(4,128)S(1)} %copy-done.11, s32[1,128]{1,0:T(1,128)S(1)} %bitcast.12, f32[1,4]{1,0:T(1,128)S(1)} %bitcast.14, f32[8,128]{1,0:T(8,128)S(1)} %get-tuple-element.94.own, ...), custom_call_target="tpu_custom_call" | custom-call | flops 100000000 | bytes 1048576 | tf_op jit(solution)/shard_map/final/pallas_call | solution.py:727
  (9 shorter events, 0.1 us)
Async XLA Ops:
  2.8 9.4 %collective-permute-start = (f32[1,32,128]{2,1,0:T(8,128)}, f32[1,32,128]{2,1,0:T(8,128)S(1)}, u32[]{:S(2)}, u32[]{:S(2)}) collective-permute-start(f32[1,32,128]{2,1,0:T(8,128)} %bitcast.8), channel_id=1, source_target_pairs={{0,16},{8,24},{16,0},{24,8},{1,17},{9,25},{17,1},{25,9},{2,18},{10... | collective-permute-start | bytes 49160 | tf_op jit(solution)/shard_map/ppermute | solution.py:717
  6.8 5.7 %collective-permute-start.1 = (f32[1,32,128]{2,1,0:T(8,128)}, f32[1,32,128]{2,1,0:T(8,128)S(1)}, u32[]{:S(2)}, u32[]{:S(2)}) collective-permute-start(f32[1,32,128]{2,1,0:T(8,128)} %bitcast.9), channel_id=1, source_target_pairs={{0,24},{8,16},{16,8},{24,0},{1,25},{9,17},{17,9},{25,1},{2,26},{10... | collective-permute-start | bytes 49160 | tf_op jit(solution)/shard_map/ppermute | solution.py:717
  8.1 4.4 %collective-permute-start.2 = (f32[1,32,128]{2,1,0:T(8,128)}, f32[1,32,128]{2,1,0:T(8,128)S(1)}, u32[]{:S(2)}, u32[]{:S(2)}) collective-permute-start(f32[1,32,128]{2,1,0:T(8,128)} %bitcast.10), channel_id=1, source_target_pairs={{0,8},{8,0},{16,24},{24,16},{1,9},{9,1},{17,25},{25,17},{2,10},{10... | collective-permute-start | bytes 49160 | tf_op jit(solution)/shard_map/ppermute | solution.py:717
  8.4 0.9 %copy-start.6 = (f32[512,128]{1,0:T(8,128)S(1)}, f32[512,128]{1,0:T(8,128)}, u32[]{:S(2)}) copy-start(f32[512,128]{1,0:T(8,128)} %kernel_filter.1) | copy-start | bytes 786436
  9.3 0.7 %copy-start.7 = (f32[32,128]{1,0:T(8,128)S(1)}, f32[32,128]{1,0:T(8,128)}, u32[]{:S(2)}) copy-start(f32[32,128]{1,0:T(8,128)} %pack.1.block.ahead) | copy-start | bytes 49156
  12.6 5.3 %collective-permute-start.3 = (f32[4,32,128]{2,1,0:T(8,128)S(1)}, f32[4,32,128]{2,1,0:T(8,128)S(1)}, u32[]{:S(2)}, u32[]{:S(2)}) collective-permute-start(f32[4,32,128]{2,1,0:T(8,128)S(1)} %get-tuple-element.101.data), channel_id=1, source_target_pairs={{0,6},{1,7},{2,4},{3,5},{4,2},{5,3},{6,0},{7,1},{8,14},{9,15},{10,... | collective-permute-start | bytes 196616 | tf_op jit(solution)/shard_map/ppermute | solution.py:717
  15.1 4.3 %collective-permute-start.4 = (f32[4,32,128]{2,1,0:T(8,128)S(1)}, f32[4,32,128]{2,1,0:T(8,128)S(1)}, u32[]{:S(2)}, u32[]{:S(2)}) collective-permute-start(f32[4,32,128]{2,1,0:T(8,128)S(1)} %get-tuple-element.101.data), channel_id=1, source_target_pairs={{0,2},{1,3},{2,0},{3,1},{4,6},{5,7},{6,4},{7,5},{8,10},{9,11},{10,... | collective-permute-start | bytes 196616 | tf_op jit(solution)/shard_map/ppermute | solution.py:717
  15.6 4.4 %collective-permute-start.5 = (f32[4,32,128]{2,1,0:T(8,128)S(1)}, f32[4,32,128]{2,1,0:T(8,128)S(1)}, u32[]{:S(2)}, u32[]{:S(2)}) collective-permute-start(f32[4,32,128]{2,1,0:T(8,128)S(1)} %get-tuple-element.101.data), channel_id=1, source_target_pairs={{0,4},{1,5},{2,6},{3,7},{4,0},{5,1},{6,2},{7,3},{8,12},{9,13},{10,... | collective-permute-start | bytes 196616 | tf_op jit(solution)/shard_map/ppermute | solution.py:717
  17.9 1.4 %copy-start.8 = (f32[32,128]{1,0:T(8,128)S(1)}, f32[32,128]{1,0:T(8,128)}, u32[]{:S(2)}) copy-start(f32[32,128]{1,0:T(8,128)} %pack.1.block.ahead) | copy-start | bytes 49156
  20.1 1.4 %copy-start = (bf16[128,768]{1,0:T(8,128)(2,1)S(1)}, bf16[128,768]{1,0:T(8,128)(2,1)}, u32[]{:S(2)}) copy-start(bf16[128,768]{1,0:T(8,128)(2,1)} %get-tuple-element.67.later_wb3.wb3) | copy-start | bytes 589828
  20.1 1.4 %copy-start.1 = (bf16[64,384]{1,0:T(8,128)(2,1)S(1)}, bf16[64,384]{1,0:T(8,128)(2,1)}, u32[]{:S(2)}) copy-start(bf16[64,384]{1,0:T(8,128)(2,1)} %get-tuple-element.68.later_re3.re3) | copy-start | bytes 147460
  20.1 1.4 %copy-start.2 = (bf16[256,384]{1,0:T(8,128)(2,1)S(1)}, bf16[256,384]{1,0:T(8,128)(2,1)}, u32[]{:S(2)}) copy-start(bf16[256,384]{1,0:T(8,128)(2,1)} %get-tuple-element.65.wcu3) | copy-start | bytes 589828
  20.1 1.4 %copy-start.3 = (bf16[128,240]{1,0:T(8,128)(2,1)S(1)}, bf16[128,240]{1,0:T(8,128)(2,1)}, u32[]{:S(2)}) copy-start(bf16[128,240]{1,0:T(8,128)(2,1)} %get-tuple-element.64.rex3) | copy-start | bytes 184324
  20.1 1.4 %copy-start.4 = (f32[128,128]{1,0:T(8,128)S(1)}, f32[128,128]{1,0:T(8,128)}, u32[]{:S(2)}) copy-start(f32[128,128]{1,0:T(8,128)} %get-tuple-element.66.rv_ref) | copy-start | bytes 196612
  20.1 1.4 %copy-start.5 = (f32[16,128]{1,0:T(8,128)S(1)}, f32[16,128]{1,0:T(8,128)}, u32[]{:S(2)}) copy-start(f32[16,128]{1,0:T(8,128)} %radial.3) | copy-start | bytes 24580
  20.1 1.3 %collective-permute-start.6 = (f32[16,8,128]{2,1,0:T(8,128)S(1)}, f32[16,8,128]{2,1,0:T(8,128)S(1)}, u32[]{:S(2)}, u32[]{:S(2)}) collective-permute-start(f32[16,8,128]{2,1,0:T(8,128)S(1)} %fusion), channel_id=1, source_target_pairs={{0,1},{1,0},{2,3},{3,2},{4,5},{5,4},{6,7},{7,6},{8,9},{9,8},{10,11... | collective-permute-start | bytes 196616 | tf_op jit(solution)/shard_map/ppermute | solution.py:717
  26.9 2.7 %collective-permute-start.8 = (f32[512,128]{1,0:T(8,128)S(1)}, f32[512,128]{1,0:T(8,128)S(1)}, u32[]{:S(2)}, u32[]{:S(2)}) collective-permute-start(f32[512,128]{1,0:T(8,128)S(1)} %structure.3.part.sin_own), channel_id=1, source_target_pairs={{0,1},{1,0},{2,3},{3,2},{4,5},{5,4},{6,7},{7,6},{8,9},{9,8},{10,11... | collective-permute-start | bytes 786440 | tf_op jit(solution)/shard_map/ppermute | solution.py:717
  28.4 1.8 %collective-permute-start.7 = (f32[512,128]{1,0:T(8,128)S(1)}, f32[512,128]{1,0:T(8,128)S(1)}, u32[]{:S(2)}, u32[]{:S(2)}) collective-permute-start(f32[512,128]{1,0:T(8,128)S(1)} %structure.2.cos_own), channel_id=1, source_target_pairs={{0,1},{1,0},{2,3},{3,2},{4,5},{5,4},{6,7},{7,6},{8,9},{9,8},{10,11... | collective-permute-start | bytes 786440 | tf_op jit(solution)/shard_map/ppermute | solution.py:717
  33.3 1.3 %copy-start.9 = (f32[3,128]{1,0:T(4,128)S(1)}, f32[3,128]{1,0:T(4,128)}, u32[]{:S(2)}) copy-start(f32[3,128]{1,0:T(4,128)} %pos.3) | copy-start | bytes 4612
  33.3 1.3 %copy-start.10 = (f32[3,128]{1,0:T(4,128)S(1)}, f32[3,128]{1,0:T(4,128)}, u32[]{:S(2)}) copy-start(f32[3,128]{1,0:T(4,128)} %vel.3) | copy-start | bytes 4612
  33.3 1.3 %copy-start.11 = (f32[3,128]{1,0:T(4,128)S(1)}, f32[3,128]{1,0:T(4,128)}, u32[]{:S(2)}) copy-start(f32[3,128]{1,0:T(4,128)} %frc.3) | copy-start | bytes 4612
  33.3 1.3 %copy-start.12 = (s32[128]{0:T(128)S(1)}, s32[128]{0:T(128)}, u32[]{:S(2)}) copy-start(s32[128]{0:T(128)} %param.20) | copy-start | bytes 1540
  33.3 1.3 %copy-start.13 = (f32[4]{0:T(128)S(1)}, f32[4]{0:T(128)}, u32[]{:S(2)}) copy-start(f32[4]{0:T(128)} %param.26) | copy-start | bytes 52
  33.4 1.2 %collective-permute-start.9 = (f32[8,128]{1,0:T(8,128)S(1)}, f32[8,128]{1,0:T(8,128)S(1)}, u32[]{:S(2)}, u32[]{:S(2)}) collective-permute-start(f32[8,128]{1,0:T(8,128)S(1)} %get-tuple-element.95), channel_id=1, source_target_pairs={{0,1},{1,0},{2,3},{3,2},{4,5},{5,4},{6,7},{7,6},{8,9},{9,8},{10,11... | collective-permute-start | bytes 12296 | tf_op jit(solution)/shard_map/ppermute | solution.py:717
